TPU v7x, 128 devices: a whole 4x4x4 slice. The times are simulated.
128 devices in a mesh: ctx: 16 (over y, x), ch: 8 (over z, core).
Axes of the slice: x: 4, y: 4, z: 4, core: 2. Of those that a mesh axis runs over, the one named last changes fastest.
Arguments:
- tokens: bfloat16 [8192, 8192], P('ctx', 'ch'), may hold values from -6 to 6
- in_weight: bfloat16 [8192, 3, 4096], P('ch', None, 'ctx'), may hold values from -0.09375 to 0.09375
- short_taps: float32 [7, 3, 4096], P(None, None, 'ch'), may hold values from -2 to 2
- residues: float32 [16, 4096], P(None, 'ch'), may hold values from -1.5 to 1.5
- decay_scale: float32 [16, 4096], P(None, 'ch'), may hold values from 0.2 to 512, as said below
- skip_gain: float32 [4096], P('ch'), may hold values from -4 to 4
Outputs:
- filtered: bfloat16 [8192, 4096], P('ctx', 'ch')
Inputs may be any that keep to these rules, and one draw needn't show every extreme that they name: decay_scale[r, c] / 8192 is the fraction by which mode r of channel c fades per position.
All inputs are finite; a program needn't handle non-finite values.
Results may differ from a plain program's by a relative error of at most 0.035.
Values may be sent and summed in bfloat16 or wider, within the bound.
No kernel may reach another device: no remote copies, remote signals or barrier semaphores. Data moves between devices by JAX's collectives and lax.ppermute only.
A program may use at most 128 MiB of HBM per device.

v0:
```python
import math

import jax
import jax.numpy as jnp
from jax import lax
from jax.sharding import PartitionSpec as P

SHORT = 7


def passed_along(value, axis, steps):
    count = lax.axis_size(axis)
    initial, last = (max(0, -steps), min(count, count - steps))
    return lax.ppermute(value, axis, [(source, source + steps) for source in range(initial, last)])


def on_device(tokens, in_weight, short_taps, residues, decay_scale, skip_gain):
    length = tokens.shape[0]
    partial_value = jnp.einsum(
        "td,dmg->tmg",
        tokens,
        lax.all_gather(in_weight, "ctx", axis=2, tiled=True),
        preferred_element_type=jnp.float32,
    )
    projected = lax.psum_scatter(
        partial_value.astype(jnp.bfloat16), "ch", scatter_dimension=2, tiled=True
    )
    previous = passed_along(projected[length - (SHORT - 1) :], "ctx", 1)
    extended = jnp.concatenate([previous, projected], axis=0).astype(jnp.float32)
    smoothed = short_taps[0] * extended[SHORT - 1 : SHORT - 1 + length]
    for offset in range(1, SHORT):
        smoothed = (
            smoothed
            + short_taps[offset] * extended[SHORT - 1 - offset : SHORT - 1 - offset + length]
        )
    gate_part = smoothed[:, 0, :]
    source = smoothed[:, 1, :] * smoothed[:, 2, :]
    channels = source.shape[1]
    seq_total = length * lax.axis_size("ctx")
    decay_rate = decay_scale / seq_total
    mode_weight = residues * jnp.sqrt(-jnp.expm1(-2.0 * decay_rate))
    offsets = jnp.arange(length, dtype=jnp.float32)
    fading = jnp.exp(-decay_rate[:, None, :] * offsets[None, :, None])
    kernel = jnp.sum(fading * mode_weight[:, None, :], axis=0)
    highest = lax.Precision.HIGHEST
    block_len = math.gcd(length, 64)
    block_count = length // block_len
    pieces = source.reshape(block_count, block_len, channels)
    lag_steps = (
        jnp.arange(block_len, dtype=jnp.int32)[:, None]
        - jnp.arange(block_len, dtype=jnp.int32)[None, :]
    )
    toeplitz = jnp.where((lag_steps >= 0)[:, :, None], kernel[jnp.maximum(lag_steps, 0)], 0.0)
    within = jnp.einsum("tsc,jsc->jtc", toeplitz, pieces, precision=highest)
    block_steps = jnp.arange(block_len, dtype=jnp.float32)
    closing = jnp.exp(-decay_rate[:, None, :] * (block_len - 1.0 - block_steps)[None, :, None])
    block_ends = jnp.einsum("rsc,jsc->jrc", closing, pieces, precision=highest)
    block_ids = jnp.arange(block_count, dtype=jnp.int32)
    block_gap = block_ids[:, None] - 1 - block_ids[None, :]
    gap_float = jnp.maximum(block_gap, 0).astype(jnp.float32)
    passing = jnp.exp(-(decay_rate * block_len)[None, None, :, :] * gap_float[:, :, None, None])
    passing = jnp.where((block_gap >= 0)[:, :, None, None], passing, 0.0)
    block_starts = jnp.einsum("jirc,irc->jrc", passing, block_ends, precision=highest)
    opening = jnp.exp(-decay_rate[:, None, :] * (block_steps + 1.0)[None, :, None])
    within = within + jnp.einsum(
        "rtc,jrc->jtc", opening, mode_weight[None, :, :] * block_starts, precision=highest
    )
    local_conv = within.reshape(length, channels)
    tail_decay = jnp.exp(-decay_rate[:, None, :] * (length - 1.0 - offsets)[None, :, None])
    end_state = jnp.sum(tail_decay * source[None, :, :], axis=1)
    states = lax.all_gather(end_state[None].astype(jnp.bfloat16), "ctx", axis=0, tiled=True).astype(
        jnp.float32
    )
    position = lax.axis_index("ctx")
    earlier_ids = jnp.arange(states.shape[0], dtype=jnp.int32)
    distance = jnp.maximum(position - 1 - earlier_ids, 0).astype(jnp.float32)
    weights = jnp.exp(-(decay_rate * length)[None, :, :] * distance[:, None, None])
    weights = jnp.where((earlier_ids < position)[:, None, None], weights, 0.0)
    incoming = jnp.sum(weights * states, axis=0)
    lead_decay = jnp.exp(-decay_rate[:, None, :] * (offsets + 1.0)[None, :, None])
    carried = jnp.sum(lead_decay * (mode_weight * incoming)[:, None, :], axis=0)
    convolved = local_conv + carried
    return (gate_part * (convolved + skip_gain[None, :] * source)).astype(jnp.bfloat16)


def solution(mesh):
    return jax.shard_map(
        on_device,
        mesh=mesh,
        in_specs=(
            P("ctx", "ch"),
            P("ch", None, "ctx"),
            P(None, None, "ch"),
            P(None, "ch"),
            P(None, "ch"),
            P("ch"),
        ),
        out_specs=P("ctx", "ch"),
        check_vma=False,
    )
```

profile of v0, /device:TPU:1, one launch (start us, length us, event | category | flops | bytes accessed | tf_op | source)
XLA Modules:
  0.0 411.9 jit_solution(9464340326151091559)
XLA Ops:
  6.5 0.0 copy-start
  6.5 0.0 all-gather.3.cloned.1.call-start
  6.5 0.7 all-gather.3.cloned.1.call-update
  7.3 0.0 reduce-scatter.2.cloned.1.call-start
  7.3 168.2 %all-gather.3.cloned.1.call-done = bf16[1024,3,4096]{2,0,1:T(8,128)(2,1)} async-done(((bf16[1024,3,256]{2,0,1:T(8,128)(2,1)}), bf16[1024,3,4096]{2,0,1:T(8,128)(2,1)}) %all-gather.3.cloned.1.call-update) | async-done | bytes 25165840 | tf_op jit(solution)/shard_map/all_gather | solution.py:22
  175.5 0.0 copy-done
  175.5 23.7 %convolution_convert_fusion = bf16[512,3,4096]{2,0,1:T(8,128)(2,1)} fusion(bf16[1024,3,4096]{2,0,1:T(8,128)(2,1)} %all-gather.3.cloned.1.call-done, bf16[512,1024]{1,0:T(8,128)(2,1)S(1)} %copy-done), kind=kOutput, calls=%fused_computation.6 | convolution fusion | flops 12891193344 | bytes 38797312 | tf_op jit(solution)/shard_map/td,dmg->tmg/dot_general | solution.py:19
  199.2 0.0 copy-start.6
  199.2 0.0 copy-start.5
  199.2 0.0 reduce-scatter.2.cloned.1.call-update
  199.2 0.1 reshape.140
  199.4 0.6 fusion.35
  200.0 0.1 maximum_convert_fusion.1
  200.1 0.0 copy-done.6
  200.2 0.0 copy-done.5
  200.2 71.4 %reduce-scatter.2.cloned.1.call-done = bf16[512,3,512]{2,0,1:T(8,128)(2,1)} async-done(((bf16[512,3,4096]{2,0,1:T(8,128)(2,1)}), bf16[512,3,512]{2,0,1:T(8,128)(2,1)}) %reduce-scatter.2.cloned.1.call-update) | async-done | bytes 1572880 | tf_op jit(solution)/shard_map/reduce_scatter | solution.py:25
  271.6 0.7 slice.74
  272.3 3.1 collective-permute-start
  275.4 0.1 copy.20
  275.6 0.8 collective-permute-done
  276.3 1.9 maximum_convert_fusion
  278.2 2.6 fusion.10
  280.8 0.0 copy-start.2
  280.8 0.2 fusion.42
  281.1 0.2 slice_multiply_fusion.7
  281.3 1.3 copy-done.2
  282.6 2.9 multiply_reduce_fusion.1
  285.4 22.6 %all-gather = bf16[256,512]{1,0:T(8,128)(2,1)} all-gather(bf16[16,512]{1,0:T(8,128)(2,1)S(1)} %multiply_reduce_fusion.1), channel_id=2, replica_groups=mesh['ctx'=16,'ch'=8] {'ctx'}, dimensions={0}, use_global_device_ids=true | all-gather | bytes 278528 | tf_op jit(solution)/shard_map/all_gather | solution.py:71
  308.1 0.8 copy.18
  308.9 1.1 fusion.34
  310.0 1.4 fusion.37
  311.4 0.8 copy.19
  312.3 7.8 %multiply_reduce_fusion.2 = (f32[512,512]{1,0:T(8,128)S(1)}, f32[512,512]{1,0:T(8,128)}) fusion(f32[16,512]{1,0:T(8,128)S(1)} %get-tuple-element.8, f32[16,512]{1,0:T(8,128)S(1)} %get-tuple-element.18, f32[16,512]{1,0:T(8,128)} %get-tuple-element.7, f32[512]{0:T(512)S(1)} %iota_add_fusion), kind=kLoop, calls=%fused_computation.5 | loop fusion | flops 24641536 | bytes 2197504 | tf_op jit(solution)/shard_map/reduce_sum | solution.py:44
  320.1 16.8 %gather_fusion = f32[4096,512]{1,0:T(8,128)} fusion(f32[512,512]{1,0:T(8,128)S(1)} %get-tuple-element.5, s32[4096]{0:T(1024)S(1)} %broadcast_clamp_fusion), kind=kCustom, calls=%fused_computation | custom fusion | bytes 16793600 | tf_op jit(solution)/shard_map/gather | solution.py:53
  336.8 16.3 %copy.17 = f32[64,64,512]{1,0,2:T(8,128)} copy(f32[64,64,512]{2,1,0:T(8,128)} %bitcast.55) | data formatting | bytes 16777216 | tf_op jit(solution)/shard_map/gather | solution.py:53
  353.1 0.0 copy-start.7
  353.1 0.0 copy-start.9
  353.1 8.3 %fusion.22 = f32[16,512,8]{0,2,1:T(8,128)} fusion(f32[8,64,512]{1,0,2:T(8,128)S(1)} %copy.18, f32[64]{0:T(128)S(1)} %iota_subtract_fusion.2, f32[16,512]{0,1:T(8,128)S(1)} %copy.20), kind=kOutput, calls=%fused_computation.36 | convolution fusion | flops 50855936 | bytes 1343744 | tf_op jit(solution)/shard_map/rsc,jsc->jrc/dot_general | solution.py:57
  361.4 2.2 copy.38
  363.6 0.0 copy-done.7
  363.6 0.0 copy-done.9
  363.6 0.5 multiply_reduce_fusion.3
  364.2 2.0 copy.30
  366.1 0.0 copy-start.3
  366.1 0.0 copy-start.4
  366.1 29.1 %fusion = f32[512,8,64]{2,1,0:T(8,128)S(1)} fusion(f32[8,64,512]{1,0,2:T(8,128)S(1)} %copy.18, f32[64,64,512]{1,0,2:T(8,128)} %copy.17, pred[64,64]{1,0:T(8,128)(4,1)S(1)} %subtract_compare_fusion), kind=kOutput, calls=%fused_computation.3 | convolution fusion | flops 203423744 | bytes 10489856 | tf_op jit(solution)/shard_map/tsc,jsc->jtc/dot_general | solution.py:54
  395.3 0.0 copy-done.3
  395.3 0.0 copy-done.4
  395.3 4.2 %add_bitcast_fusion = f32[8,64,512]{1,0,2:T(8,128)S(1)} fusion(f32[512,8,64]{2,1,0:T(8,128)S(1)} %fusion, f32[64]{0:T(128)S(1)} %iota_add_fusion.1, f32[16,512]{0,1:T(8,128)S(1)} %copy.20, f32[16,512,8]{0,2,1:T(8,128)S(1)} %copy-done.3, f32[16,512]{0,1:T(8,128)S(1)} %copy-done.4), kind=kOutput, calls=%fused_computation.30 | convolution fusion | flops 51183616 | bytes 2425088 | tf_op jit(solution)/shard_map/rtc,jrc->jtc/dot_general | solution.py:65
  399.5 0.0 copy-start.8
  399.5 0.0 copy-start.1
  399.5 1.7 copy.22
  401.2 0.0 copy-done.8
  401.2 3.9 fusion.30
  405.1 0.0 copy-done.1
  (16 shorter events, 0.1 us)
Async XLA Ops:
  6.5 168.9 %copy-start = (bf16[512,1024]{1,0:T(8,128)(2,1)S(1)}, bf16[512,1024]{1,0:T(8,128)(2,1)}, u32[]{:S(2)}) copy-start(bf16[512,1024]{1,0:T(8,128)(2,1)} %param.6) | copy-start | bytes 3145732
  6.5 168.9 %all-gather.3.cloned.1.call-start = ((), (), s32[]{:S(2)}) async-start(), calls=%async_computation.1 | async-start | bytes 26738688 | tf_op jit(solution)/shard_map/all_gather | solution.py:22
  7.3 264.3 %reduce-scatter.2.cloned.1.call-start = ((), (), s32[]{:S(2)}) async-start(), calls=%async_computation.2 | async-start | bytes 14155776 | tf_op jit(solution)/shard_map/reduce_scatter | solution.py:25
  199.2 0.9 copy-start.6
  199.2 1.0 copy-start.5
  272.3 4.0 collective-permute-start
  280.8 1.7 copy-start.2
  353.1 10.5 %copy-start.7 = (f32[16,512]{1,0:T(8,128)S(1)}, f32[16,512]{1,0:T(8,128)}, u32[]{:S(2)}) copy-start(f32[16,512]{1,0:T(8,128)} %get-tuple-element.16) | copy-start | bytes 98308
  353.1 10.5 %copy-start.9 = (pred[8,8]{1,0:T(8,128)(4,1)S(1)}, pred[8,8]{1,0:T(8,128)(4,1)}, u32[]{:S(2)}) copy-start(pred[8,8]{1,0:T(8,128)(4,1)} %fusion.35) | copy-start | bytes 196
  366.1 29.1 %copy-start.3 = (f32[16,512,8]{0,2,1:T(8,128)S(1)}, f32[16,512,8]{0,2,1:T(8,128)}, u32[]{:S(2)}) copy-start(f32[16,512,8]{0,2,1:T(8,128)} %copy.30) | copy-start | bytes 786436
  366.1 29.1 %copy-start.4 = (f32[16,512]{0,1:T(8,128)S(1)}, f32[16,512]{0,1:T(8,128)}, u32[]{:S(2)}) copy-start(f32[16,512]{0,1:T(8,128)} %copy.19) | copy-start | bytes 98308
  399.5 1.7 copy-start.8
  399.5 5.6 %copy-start.1 = (bf16[512,1024]{1,0:T(8,128)(2,1)S(1)}, bf16[512,1024]{1,0:T(8,128)(2,1)}, u32[]{:S(2)}) copy-start(bf16[512,1024]{1,0:T(8,128)(2,1)} %param.6) | copy-start | bytes 3145732
Sparse Core Ops, SparseCore 0:
  9.5 165.9 all-gather.2
  199.3 72.2 reduce-scatter.1
where the time goes:
time: 419 us; the launch traced here: 412 us
  waiting for transfers between devices  241 us (58%)
  matrix products  65.3 us (16%)
  local copies, waits for them, and re-layouts  42.8 us (10%)
  other arithmetic  23.4 us (6%)
  blocking collectives  22.6 us (5%)
  between operations  13.6 us (3%)
    all_gather x1, waiting for transfers between devices, on_device(): lax.all_gather(in_weight, 'ctx', axis=2, tiled=True)  168 us
    reduce_scatter x1, waiting for transfers between devices, on_device(): lax.psum_scatter(partial_value.astype(jnp.bfloat16), 'ch', scatter_dimens...  71.4 us
    gather x2, local copies, waits for them, and re-layouts, on_device(): kernel[jnp.maximum(lag_steps, 0)]  33.1 us
    dot_general x1, matrix products, on_device(): within = jnp.einsum('tsc,jsc->jtc', toeplitz, pieces, precision=highest)  29.1 us
    dot_general x1, matrix products, on_device(): jnp.einsum('td,dmg->tmg', tokens, lax.all_gather(in_weight, 'ctx', axis=2...  23.7 us
    all_gather x1, blocking collectives, on_device(): lax.all_gather(end_state[None].astype(jnp.bfloat16), 'ctx', axis=0, tiled...  22.6 us
  transfers between devices with their start and end apart: 3, of which 3 were waited for; matrix products, arithmetic and copies ran while one was open for 0% of the time, Pallas kernels for 0%

commit v1 on v0

v1 whole, which is shorter than its diff:
```python
import functools

import jax
import jax.numpy as jnp
from jax import lax
from jax.experimental import pallas as pl
from jax.experimental.pallas import tpu as pltpu
from jax.sharding import Mesh
from jax.sharding import PartitionSpec as P

SHORT = 7
HALO = 8
SEGMENTS = 8
LANES = 128
N = 4
F32 = jnp.float32
BF16 = jnp.bfloat16
VMEM_LIMIT = 48 * 1024 * 1024


def split_ring(value, axis):
    up = [(2 * i, 2 * ((i + 1) % N)) for i in range(N)]
    down = [(2 * i + 1, 2 * ((i - 1) % N) + 1) for i in range(N)]
    return lax.ppermute(value, (axis, "c"), up + down)


def core_swap(value):
    return lax.ppermute(value, "c", [(0, 1), (1, 0)])


def later(value, steps):
    return lax.ppermute(value, "y", [(i, i + steps) for i in range(N - steps)])


def project_kernel(
    where_ref, t_own, t_a, t_b, t_c, t_d, w_own, w_a, w_b, w_c, w_d,
    far_ref, near_ref, own_ref, t_buf, w_buf, t_sem, w_sem,
):
    core = where_ref[4]
    rows = t_own.shape[0]
    half = rows // 2
    depth = w_own.shape[0] // 2

    def tile_copies(i):
        if i < 3:
            return [pltpu.make_async_copy((t_own, t_a, t_b)[i], t_buf.at[i], t_sem.at[i])]
        return [
            pltpu.make_async_copy(t_c, t_buf.at[3, pl.ds(pl.multiple_of(half * core, half), half)], t_sem.at[3]),
            pltpu.make_async_copy(t_d, t_buf.at[3, pl.ds(pl.multiple_of(half * (1 - core), half), half)], t_sem.at[4]),
        ]

    def fetch(k):
        for index, source in enumerate((w_own, w_a, w_b)):
            @pl.when(where_ref[5 + k] == index)
            def _():
                pltpu.make_async_copy(source.at[pl.ds(0, depth)], w_buf.at[k, pl.ds(0, depth)], w_sem.at[k, 0]).start()
                pltpu.make_async_copy(source.at[pl.ds(depth, depth)], w_buf.at[k, pl.ds(depth, depth)], w_sem.at[k, 1]).start()

        @pl.when(where_ref[5 + k] == 3)
        def _():
            low = pl.multiple_of(depth * core, depth)
            high = pl.multiple_of(depth * (1 - core), depth)
            pltpu.make_async_copy(w_c, w_buf.at[k, pl.ds(low, depth)], w_sem.at[k, 0]).start()
            pltpu.make_async_copy(w_d, w_buf.at[k, pl.ds(high, depth)], w_sem.at[k, 1]).start()

    def arrive(k):
        for part in range(2):
            pltpu.make_async_copy(w_c, w_buf.at[k, pl.ds(part * depth, depth)], w_sem.at[k, part]).wait()

    for copy in tile_copies(0):
        copy.start()
    fetch(1)
    fetch(0)
    fetch(2)
    for i in range(1, 4):
        for copy in tile_copies(i):
            copy.start()
    for k in (1, 0, 2):
        arrive(k)
    for i in range(4):
        for copy in tile_copies(i):
            copy.wait()
        tile = where_ref[i]
        mine = tile // 2 == core
        at = pl.multiple_of(rows * (tile % 2), rows)
        off = pl.multiple_of(at + 2 * rows * jnp.where(mine, 0, 1), rows)
        near_ref[pl.ds(off, rows), :] = jnp.dot(t_buf[i], w_buf[1], preferred_element_type=F32).astype(BF16)

        @pl.when(mine)
        def _():
            far_ref[pl.ds(at, rows), :] = jnp.dot(t_buf[i], w_buf[0], preferred_element_type=F32).astype(BF16)
            own_ref[pl.ds(at, rows), :] = jnp.dot(t_buf[i], w_buf[2], preferred_element_type=F32).astype(BF16)


def project(where, tokens, weights):
    rows, depth = tokens[0].shape
    width = weights[0].shape[1]
    hbm = pl.BlockSpec(memory_space=pl.ANY)
    vmem = pl.BlockSpec(memory_space=pltpu.VMEM)
    return pl.pallas_call(
        project_kernel,
        out_shape=(
            jax.ShapeDtypeStruct((2 * rows, width), BF16),
            jax.ShapeDtypeStruct((4 * rows, width), BF16),
            jax.ShapeDtypeStruct((2 * rows, width), BF16),
        ),
        in_specs=[pl.BlockSpec(memory_space=pltpu.SMEM)] + [hbm] * 10,
        out_specs=(vmem, vmem, vmem),
        scratch_shapes=[
            pltpu.VMEM((4, rows, depth), BF16),
            pltpu.VMEM((3, depth, width), BF16),
            pltpu.SemaphoreType.DMA((5,)),
            pltpu.SemaphoreType.DMA((3, 2)),
        ],
        compiler_params=pltpu.CompilerParams(vmem_limit_bytes=VMEM_LIMIT),
        cost_estimate=pl.CostEstimate(
            flops=2 * 8 * rows * depth * width,
            bytes_accessed=2 * (4 * rows * depth + 3 * depth * width + 8 * rows * width),
            transcendentals=0,
        ),
        name="project",
    )(where, *tokens, *weights)


def smooth(ext, taps, start, count):
    total = taps[0][None, :] * ext[pl.ds(HALO + start, count), :]
    for k in range(1, SHORT):
        total = total + taps[k][None, :] * ext[pl.ds(HALO + start - k, count), :]
    return total


def states_kernel(first_ref, second_ref, halo_ref, taps_ref, rate_ref, source_ref, init_ref, end_ref, ext1, ext2, ends):
    length, width = first_ref.shape
    modes = rate_ref.shape[0]
    seg = length // SEGMENTS
    ext1[pl.ds(0, HALO), :] = halo_ref[0]
    ext2[pl.ds(0, HALO), :] = halo_ref[1]
    ext1[pl.ds(HALO, length), :] = first_ref[...].astype(F32)
    ext2[pl.ds(HALO, length), :] = second_ref[...].astype(F32)
    taps1 = [taps_ref[k, 1] for k in range(SHORT)]
    taps2 = [taps_ref[k, 2] for k in range(SHORT)]
    step = 64
    for start in range(0, length, step):
        product = smooth(ext1, taps1, start, step) * smooth(ext2, taps2, start, step)
        for lane in range(0, width, LANES):
            source_ref[lane // LANES, pl.ds(start, step), :] = product[:, lane : lane + LANES]
    for lane in range(0, width, LANES):
        column = source_ref.at[lane // LANES]
        lanes = pl.ds(lane, LANES)
        fade = [jnp.broadcast_to(jnp.exp(-rate_ref[r, lanes])[None, :], (SEGMENTS, LANES)) for r in range(modes)]

        def body(i, states):
            for j in range(4):
                x = column[pl.ds(4 * i + j, SEGMENTS, stride=seg), :]
                states = tuple(f * s + x for f, s in zip(fade, states))
            return states

        zero = jnp.zeros((SEGMENTS, LANES), F32)
        states = lax.fori_loop(0, seg // 4, body, (zero,) * modes)
        for r in range(modes):
            ends[r, :, lanes] = states[r]
    passing = jnp.exp(-rate_ref[...] * float(seg))
    state = jnp.zeros((modes, width), F32)
    for s in range(SEGMENTS):
        init_ref[:, s, :] = state
        state = passing * state + ends[:, s, :]
    end_ref[...] = state


def convolve_kernel(core_ref, source_ref, init_ref, rate_ref, weight_ref, skip_ref, other_ref, one_ref, two_ref, out_ref):
    modes = rate_ref.shape[0]
    width, length = rate_ref.shape[1], source_ref.shape[1]
    seg = length // SEGMENTS
    rate = rate_ref[...]
    before = one_ref[...] + jnp.exp(-rate * (2.0 * length)) * two_ref[...]
    incoming = jnp.where(core_ref[0] == 0, before, jnp.exp(-rate * float(length)) * before + other_ref[...])
    index = lax.broadcasted_iota(jnp.int32, (SEGMENTS, LANES), 0).astype(F32) * float(seg)
    for lane in range(0, width, LANES):
        lanes = pl.ds(lane, LANES)
        column, result = source_ref.at[lane // LANES], out_ref.at[lane // LANES]

        def spread(row):
            return jnp.broadcast_to(row[None, :], (SEGMENTS, LANES))

        rates = [spread(rate_ref[r, lanes]) for r in range(modes)]
        fade = [jnp.exp(-v) for v in rates]
        weight = [spread(weight_ref[r, lanes]) for r in range(modes)]
        skip = spread(skip_ref[0, lanes])
        states = tuple(
            init_ref[r, :, lanes] + jnp.exp(-rates[r] * index) * spread(incoming[r, lane : lane + LANES])
            for r in range(modes)
        )

        def body(i, states):
            for j in range(4):
                at = pl.ds(4 * i + j, SEGMENTS, stride=seg)
                x = column[at, :]
                states = tuple(f * s + x for f, s in zip(fade, states))
                terms = [w * s for w, s in zip(weight, states)] + [skip * x]
                while len(terms) > 1:
                    terms = [a + b for a, b in zip(terms[::2], terms[1::2])] + ([terms[-1]] if len(terms) % 2 else [])
                result[at, :] = terms[0]
            return states

        lax.fori_loop(0, seg // 4, body, states)


def gate_kernel(parity_ref, part_ref, halo_ref, taps_ref, conv_ref, even_ref, odd_ref, ext):
    length, width = part_ref.shape
    half = length // 2
    ext[pl.ds(0, HALO), :] = halo_ref[...]
    ext[pl.ds(HALO, length), :] = part_ref[...].astype(F32)
    taps = [taps_ref[k, 0] for k in range(SHORT)]
    step = 64

    def block(out_ref, base):
        for start in range(0, half, step):
            gate = smooth(ext, taps, base + start, step)
            for lane in range(0, width, LANES):
                lanes = slice(lane, lane + LANES)
                filtered = gate[:, lanes] * conv_ref[lane // LANES, pl.ds(base + start, step), :]
                out_ref[pl.ds(start, step), lanes] = filtered.astype(BF16)

    @pl.when(parity_ref[0] == 0)
    def _():
        block(even_ref, 0)
        block(odd_ref, half)

    @pl.when(parity_ref[0] == 1)
    def _():
        block(even_ref, half)
        block(odd_ref, 0)


def local_call(kernel, shapes, scalars, arrays, scratch, cycles, name):
    vmem = pl.BlockSpec(memory_space=pltpu.VMEM)
    return pl.pallas_call(
        kernel,
        out_shape=shapes,
        in_specs=[pl.BlockSpec(memory_space=pltpu.SMEM)] * len(scalars) + [vmem] * len(arrays),
        out_specs=tuple(vmem for _ in shapes),
        scratch_shapes=scratch,
        compiler_params=pltpu.CompilerParams(vmem_limit_bytes=VMEM_LIMIT),
        cost_estimate=pl.CostEstimate(flops=cycles, bytes_accessed=cycles, transcendentals=0),
        name=name,
    )(*scalars, *arrays)


def on_device(tokens, in_weight, short_taps, residues, decay_scale, skip_gain):
    y, x, z, c = (lax.axis_index(a) for a in ("y", "x", "z", "c"))
    rows, depth = tokens.shape
    width = in_weight.shape[2]
    seq_total = rows * N * N
    first_core = c == 0

    def both(value):
        other = core_swap(value)
        return jnp.where(first_core, value, other), jnp.where(first_core, other, value)

    weights = jnp.transpose(in_weight, (1, 0, 2))
    low, high = both(weights)
    own_weights = [jnp.concatenate([low[m], high[m]], axis=0) for m in range(3)]
    t_own = jnp.concatenate(both(tokens), axis=1)

    t_a = split_ring(t_own, "x")
    t_b = core_swap(t_a)
    t_c = split_ring(
        lax.dynamic_slice_in_dim(t_a, c * (rows // 2), rows // 2, axis=0), "x"
    )
    t_d = core_swap(t_c)
    held_tokens = (t_own, t_a, t_b, t_c, t_d)

    channels = short_taps.shape[2]
    packed = jnp.concatenate(
        [short_taps.reshape(SHORT * 3, channels), residues, decay_scale, skip_gain[None]], axis=0
    )
    packed = lax.dynamic_slice_in_dim(packed, (x % 2) * width, width, axis=1)
    packed = jnp.where(c == x // 2, packed, core_swap(packed))
    modes = residues.shape[0]
    taps = packed[: SHORT * 3].reshape(SHORT, 3, width)
    rate = packed[SHORT * 3 + modes : SHORT * 3 + 2 * modes] / seq_total
    mode_weight = packed[SHORT * 3 : SHORT * 3 + modes] * jnp.sqrt(-jnp.expm1(-2.0 * rate))
    skip = packed[SHORT * 3 + 2 * modes :]

    side = 1 - 2 * c

    def held_at(row):
        delta = (row - y) % N
        return jnp.where(delta == 0, 0, jnp.where(delta == 2, 3, jnp.where(delta == (side * -1) % N, 1, 2)))

    where = jnp.stack(
        [x, (x - side) % N, (x + side) % N, (x + 2) % N, c, held_at(z + 2), held_at(z + side), held_at(z)]
    ).astype(jnp.int32)

    def stream(m):
        w_own = own_weights[m]
        w_a = split_ring(w_own, "y")
        w_b = core_swap(w_a)
        half = w_own.shape[0] // 2
        w_c = split_ring(lax.dynamic_slice_in_dim(w_a, c * half, half, axis=0), "y")
        w_d = core_swap(w_c)
        far, near, own = project(where, held_tokens, (w_own, w_a, w_b, w_c, w_d))
        count = far.shape[0]
        arrived = split_ring(far, "z")
        near = lax.dynamic_update_slice(
            near, (near[:count].astype(F32) + arrived.astype(F32)).astype(BF16), (0, 0)
        )
        reached = split_ring(near, "z")
        crossed = core_swap(reached[count:])
        return (own.astype(F32) + reached[:count].astype(F32) + crossed.astype(F32)).astype(BF16)

    def last_rows(value):
        ring = [(2 * i, 2 * i + 1) for i in range(N)] + [(2 * i + 1, 2 * i + 2) for i in range(N - 1)]
        return lax.ppermute(value, ("y", "c"), ring).astype(F32)

    first = stream(1)
    second = stream(2)
    length = first.shape[0]
    halo = last_rows(jnp.stack([first[length - HALO :], second[length - HALO :]]))
    state = jax.ShapeDtypeStruct((modes, width), F32)
    full = jax.ShapeDtypeStruct((width // LANES, length, LANES), F32)
    extended = pltpu.VMEM((HALO + length, width), F32)
    source, init, end = local_call(
        states_kernel,
        (full, jax.ShapeDtypeStruct((modes, SEGMENTS, width), F32), state),
        (),
        (first, second, halo, taps, rate),
        [extended, extended, pltpu.VMEM((modes, SEGMENTS, width), F32)],
        4_000_000,
        "states",
    )
    other = core_swap(end)
    fade = jnp.exp(-rate * float(length))
    chip = jnp.where(first_core, fade * end + other, fade * other + end)
    one = later(chip, 1)
    two = later(chip + jnp.exp(-rate * (2.0 * length)) * one, 2)
    (convolved,) = local_call(
        convolve_kernel,
        (full,),
        (c.astype(jnp.int32)[None],),
        (source, init, rate, mode_weight, skip, other, one, two),
        [],
        8_000_000,
        "convolve",
    )
    gate = stream(0)
    gate_halo = last_rows(gate[length - HALO :])
    block = jax.ShapeDtypeStruct((length // 2, width), BF16)
    blocks = local_call(
        gate_kernel,
        (block, block),
        ((x % 2).astype(jnp.int32)[None],),
        (gate, gate_halo, taps, convolved),
        [extended],
        2_000_000,
        "gate",
    )
    placed = []
    for r in range(2):
        moves = [
            (2 * xs + cs, 2 * (2 * cs + (xs % 2 + r) % 2) + xs // 2) for xs in range(N) for cs in range(2)
        ]
        placed.append(lax.ppermute(blocks[r], ("x", "c"), moves))
    even = x % 2 == 0
    return jnp.concatenate(
        [jnp.where(even, placed[0], placed[1]), jnp.where(even, placed[1], placed[0])], axis=1
    )


def solution(mesh):
    grid = Mesh(mesh.devices.reshape(N, N, N, 2), ("y", "x", "z", "c"))
    ctx, ch = ("y", "x"), ("z", "c")
    return jax.shard_map(
        on_device,
        mesh=grid,
        in_specs=(
            P(ctx, ch),
            P(ch, None, ctx),
            P(None, None, ch),
            P(None, ch),
            P(None, ch),
            P(ch),
        ),
        out_specs=P(ctx, ch),
        check_vma=False,
    )
```

time: 419 us -> 198 us (0.47); the launches traced: 412 us -> 197 us
  waiting for transfers between devices: 241 us -> 70.9 us
  matrix products: 65.3 us -> 0 us
  starting transfers between devices: 3.12 us -> 60.2 us
  Pallas kernels: 0 us -> 34.8 us
  local copies, waits for them, and re-layouts: 42.8 us -> 16.3 us
  blocking collectives: 22.6 us -> 0 us
  between operations: 13.6 us -> 0.41 us
  other arithmetic: 23.4 us -> 14.9 us
    all_gather x1 -> x0, waiting for transfers between devices: 168 us -> none  [on_device(): lax.all_gather(in_weight, 'ctx', axis=2, tiled=True)]
    reduce_scatter x1 -> x0, waiting for transfers between devices: 71.4 us -> none  [on_device(): lax.psum_scatter(partial_value.astype(jnp.bfloat16), 'ch', scatter_dimens...]
    ppermute x1 -> x35, waiting for transfers between devices: 0.77 us -> 70.9 us  [the longest x14 56.5 us: split_ring(): return lax.ppermute(value, (axis, 'c'), up + down)]
    dot_general x4 -> x0, matrix products: 65.3 us -> none  [the longest x1 29.1 us: on_device(): within = jnp.einsum('tsc,jsc->jtc', toeplitz, pieces, precision=highest)]
    ppermute x1 -> x35, starting transfers between devices: 3.08 us -> 60.2 us  [the longest x14 26.2 us: split_ring(): return lax.ppermute(value, (axis, 'c'), up + down)]
    pallas_call x0 -> x6, Pallas kernels: none -> 34.8 us  [the longest x3 26.3 us: project(): pl.pallas_call(project_kernel, out_shape=(jax.ShapeDtypeStruct((2 * rows,...]
    gather x2 -> x0, local copies, waits for them, and re-layouts: 33.1 us -> none  [on_device(): kernel[jnp.maximum(lag_steps, 0)]]
    all_gather x1 -> x0, blocking collectives: 22.6 us -> none  [on_device(): lax.all_gather(end_state[None].astype(jnp.bfloat16), 'ctx', axis=0, tiled...]
  transfers between devices with their start and end apart: 3 -> 35, of which waited for: 3 -> 16; matrix products, arithmetic and copies ran while one was open for 0% -> 12% of each run, Pallas kernels for 0% -> 15%
where the time goes in v1:
time: 198 us; the launch traced here: 197 us
  waiting for transfers between devices  70.9 us (36%)
  starting transfers between devices  60.2 us (30%)
  Pallas kernels  34.8 us (18%)
  local copies, waits for them, and re-layouts  16.3 us (8%)
  other arithmetic  14.9 us (8%)
    ppermute x14, waiting for transfers between devices, split_ring(): return lax.ppermute(value, (axis, 'c'), up + down)  56.5 us
    pallas_call x3, Pallas kernels, project(): pl.pallas_call(project_kernel, out_shape=(jax.ShapeDtypeStruct((2 * rows,...  26.3 us
    ppermute x14, starting transfers between devices, split_ring(): return lax.ppermute(value, (axis, 'c'), up + down)  26.2 us
    ppermute x15, starting transfers between devices, core_swap(): return lax.ppermute(value, 'c', [(0, 1), (1, 0)])  12.3 us
    ppermute x2, starting transfers between devices, later(): return lax.ppermute(value, 'y', [(i, i + steps) for i in range(N - steps)])  9.69 us
    pallas_call x3, Pallas kernels, local_call(): pl.pallas_call(kernel, out_shape=shapes, in_specs=[pl.BlockSpec(memory_sp...  8.43 us
    unnamed x35, local copies, waits for them, and re-layouts  7.46 us
    ppermute x2, waiting for transfers between devices, on_device(): placed.append(lax.ppermute(blocks[r], ('x', 'c'), moves))  6.92 us
  transfers between devices with their start and end apart: 35, of which 16 were waited for; matrix products, arithmetic and copies ran while one was open for 12% of the time, Pallas kernels for 15%

profile of v1, /device:TPU:1, one launch (start us, length us, event | category | flops | bytes accessed | tf_op | source)
XLA Modules:
  0.0 197.5 jit_solution(2178659892107778565)
XLA Ops:
  0.0 1.4 collective-permute-start
  1.4 4.0 %collective-permute-done = bf16[512,1024]{1,0:T(8,128)(2,1)S(1)} collective-permute-done((bf16[512,1024]{1,0:T(8,128)(2,1)}, bf16[512,1024]{1,0:T(8,128)(2,1)S(1)}, u32[]{:S(2)}, u32[]{:S(2)}) %collective-permute-start) | collective-permute-done | bytes 1048608 | tf_op jit(solution)/shard_map/ppermute | solution.py:28
  5.4 1.4 broadcast_select_fusion.3
  7.0 2.6 %collective-permute-start.1 = (bf16[512,2048]{1,0:T(8,128)(2,1)S(1)}, bf16[512,2048]{1,0:T(8,128)(2,1)}, u32[]{:S(2)}, u32[]{:S(2)}) collective-permute-start(bf16[512,2048]{1,0:T(8,128)(2,1)S(1)} %pad_maximum_fusion.t_own), channel_id=1, source_target_pairs={{0,8},{8,16},{16,24},{24,0},{1,25},{9,1},{17,9},{25,17},{2,10},{10... | collective-permute-start | bytes 6291464 | tf_op jit(solution)/shard_map/ppermute | solution.py:24
  9.6 1.6 broadcast_select_fusion.1
  11.2 1.2 slice_bitcast_fusion
  12.4 1.1 pad_maximum_fusion.3.w_own
  13.5 2.7 %collective-permute-start.22 = (bf16[2048,256]{1,0:T(8,128)(2,1)}, bf16[2048,256]{1,0:T(8,128)(2,1)}, u32[]{:S(2)}, u32[]{:S(2)}) collective-permute-start(bf16[2048,256]{1,0:T(8,128)(2,1)} %pad_maximum_fusion.3.w_own), channel_id=1, source_target_pairs={{0,32},{32,64},{64,96},{96,0},{1,97},{33,1},{65,33},{97,65},{2,34}... | collective-permute-start | bytes 3145736 | tf_op jit(solution)/shard_map/ppermute | solution.py:24
  16.2 2.2 %pad_maximum_fusion.2.w_own = bf16[2048,256]{1,0:T(8,128)(2,1)} fusion(bf16[1024,256]{1,0:T(8,128)(2,1)} %get-tuple-element.41, bf16[1024,256]{1,0:T(8,128)(2,1)} %get-tuple-element.48), kind=kLoop, calls=%fused_computation.4 | loop fusion | flops 2097152 | bytes 2097152 | tf_op jit(solution)/shard_map/concatenate | solution.py:262
  18.9 1.0 pad_maximum_fusion.1.w_own
  20.2 12.4 %collective-permute-done.1.t_a = bf16[512,2048]{1,0:T(8,128)(2,1)} collective-permute-done((bf16[512,2048]{1,0:T(8,128)(2,1)S(1)}, bf16[512,2048]{1,0:T(8,128)(2,1)}, u32[]{:S(2)}, u32[]{:S(2)}) %collective-permute-start.1) | collective-permute-done | bytes 2097184 | tf_op jit(solution)/shard_map/ppermute | solution.py:24
  32.6 1.3 constant_dynamic-slice_fusion.3
  33.9 3.6 %collective-permute-start.3 = (bf16[256,2048]{1,0:T(8,128)(2,1)S(1)}, bf16[256,2048]{1,0:T(8,128)(2,1)S(1)}, u32[]{:S(2)}, u32[]{:S(2)}) collective-permute-start(bf16[256,2048]{1,0:T(8,128)(2,1)S(1)} %constant_dynamic-slice_fusion.3), channel_id=1, source_target_pairs={{0,8},{8,16},{16,24},{24,0},{1,25},{9,1},{17,9},{25,17},{2,10},{10... | collective-permute-start | bytes 3145736 | tf_op jit(solution)/shard_map/ppermute | solution.py:24
  37.5 1.1 constant_dynamic-slice_fusion
  38.5 2.5 %collective-permute-start.24 = (bf16[1024,256]{1,0:T(8,128)(2,1)S(1)}, bf16[1024,256]{1,0:T(8,128)(2,1)S(1)}, u32[]{:S(2)}, u32[]{:S(2)}) collective-permute-start(bf16[1024,256]{1,0:T(8,128)(2,1)S(1)} %constant_dynamic-slice_fusion), channel_id=1, source_target_pairs={{0,32},{32,64},{64,96},{96,0},{1,97},{33,1},{65,33},{97,65},{2,34}... | collective-permute-start | bytes 1572872 | tf_op jit(solution)/shard_map/ppermute | solution.py:24
  41.1 1.1 constant_dynamic-slice_fusion.1
  42.1 1.7 collective-permute-start.17
  43.8 7.0 %collective-permute-done.6.w_a = bf16[2048,256]{1,0:T(8,128)(2,1)} collective-permute-done((bf16[2048,256]{1,0:T(8,128)(2,1)}, bf16[2048,256]{1,0:T(8,128)(2,1)}, u32[]{:S(2)}, u32[]{:S(2)}) %collective-permute-start.6) | collective-permute-done | bytes 1048608 | tf_op jit(solution)/shard_map/ppermute | solution.py:24
  50.8 1.1 collective-permute-start.23
  51.9 1.1 constant_dynamic-slice_fusion.2
  53.0 3.3 %collective-permute-done.24.w_c = bf16[1024,256]{1,0:T(8,128)(2,1)S(1)} collective-permute-done((bf16[1024,256]{1,0:T(8,128)(2,1)S(1)}, bf16[1024,256]{1,0:T(8,128)(2,1)S(1)}, u32[]{:S(2)}, u32[]{:S(2)}) %collective-permute-start.24) | collective-permute-done | bytes 524320 | tf_op jit(solution)/shard_map/ppermute | solution.py:24
  56.3 3.1 %collective-permute-start.8 = (bf16[1024,256]{1,0:T(8,128)(2,1)S(1)}, bf16[1024,256]{1,0:T(8,128)(2,1)}, u32[]{:S(2)}, u32[]{:S(2)}) collective-permute-start(bf16[1024,256]{1,0:T(8,128)(2,1)S(1)} %constant_dynamic-slice_fusion.2), channel_id=1, source_target_pairs={{0,32},{32,64},{64,96},{96,0},{1,97},{33,1},{65,33},{97,65},{2,34}... | collective-permute-start | bytes 1572872 | tf_op jit(solution)/shard_map/ppermute | solution.py:24
  59.4 2.5 %collective-permute-done.17.w_c = bf16[1024,256]{1,0:T(8,128)(2,1)} collective-permute-done((bf16[1024,256]{1,0:T(8,128)(2,1)S(1)}, bf16[1024,256]{1,0:T(8,128)(2,1)}, u32[]{:S(2)}, u32[]{:S(2)}) %collective-permute-start.17) | collective-permute-done | bytes 524320 | tf_op jit(solution)/shard_map/ppermute | solution.py:24
  61.9 1.2 collective-permute-start.25
  63.9 3.6 %collective-permute-done.8.w_c = bf16[1024,256]{1,0:T(8,128)(2,1)} collective-permute-done((bf16[1024,256]{1,0:T(8,128)(2,1)S(1)}, bf16[1024,256]{1,0:T(8,128)(2,1)}, u32[]{:S(2)}, u32[]{:S(2)}) %collective-permute-start.8) | collective-permute-done | bytes 524320 | tf_op jit(solution)/shard_map/ppermute | solution.py:24
  67.5 1.2 collective-permute-start.16
  70.3 1.3 copy-done.6
  71.6 1.0 copy-done.8
  72.6 8.3 %project.5 = (bf16[1024,256]{1,0:T(8,128)(2,1)S(1)}, bf16[2048,256]{1,0:T(8,128)(2,1)S(1)}, bf16[1024,256]{1,0:T(8,128)(2,1)S(1)}) custom-call(s32[8]{0:T(128)S(1)} %stack.44.where_ref, bf16[512,2048]{1,0:T(8,128)(2,1)} %copy-done.9, bf16[512,2048]{1,0:T(8,128)(2,1)} %collective-permute-done.1.t_a, bf16[512,2048]{1,0:T(8,128)(2,1)} %collective-permute-done.2.t_b, ...), custom_call_target="tpu_custom_call" | custom-call | flops 4294967296 | bytes 13631488 | tf_op jit(solution)/shard_map/project/pallas_call | solution.py:100
  81.0 3.9 %collective-permute-start.26 = (bf16[1024,256]{1,0:T(8,128)(2,1)S(1)}, bf16[1024,256]{1,0:T(8,128)(2,1)S(1)}, u32[]{:S(2)}, u32[]{:S(2)}) collective-permute-start(bf16[1024,256]{1,0:T(8,128)(2,1)S(1)} %get-tuple-element.27), channel_id=1, source_target_pairs={{0,2},{2,4},{4,6},{6,0},{1,7},{3,1},{5,3},{7,5},{8,10},{10,12},{12... | collective-permute-start | bytes 1572872 | tf_op jit(solution)/shard_map/ppermute | solution.py:24
  84.9 1.2 copy-done.1
  86.1 1.2 copy-done.4
  87.3 8.5 %project.4 = (bf16[1024,256]{1,0:T(8,128)(2,1)S(1)}, bf16[2048,256]{1,0:T(8,128)(2,1)S(1)}, bf16[1024,256]{1,0:T(8,128)(2,1)S(1)}) custom-call(s32[8]{0:T(128)S(1)} %stack.44.where_ref, bf16[512,2048]{1,0:T(8,128)(2,1)} %copy-done.9, bf16[512,2048]{1,0:T(8,128)(2,1)} %collective-permute-done.1.t_a, bf16[512,2048]{1,0:T(8,128)(2,1)} %collective-permute-done.2.t_b, ...), custom_call_target="tpu_custom_call" | custom-call | flops 4294967296 | bytes 13631488 | tf_op jit(solution)/shard_map/project/pallas_call | solution.py:100
  96.0 9.5 %project.3 = (bf16[1024,256]{1,0:T(8,128)(2,1)S(1)}, bf16[2048,256]{1,0:T(8,128)(2,1)}, bf16[1024,256]{1,0:T(8,128)(2,1)S(1)}) custom-call(s32[8]{0:T(128)S(1)} %stack.44.where_ref, bf16[512,2048]{1,0:T(8,128)(2,1)} %copy-done.9, bf16[512,2048]{1,0:T(8,128)(2,1)} %collective-permute-done.1.t_a, bf16[512,2048]{1,0:T(8,128)(2,1)} %collective-permute-done.2.t_b, ...), custom_call_target="tpu_custom_call" | custom-call | flops 4294967296 | bytes 13631488 | tf_op jit(solution)/shard_map/project/pallas_call | solution.py:100
  106.9 3.0 %collective-permute-start.20 = (bf16[2048,256]{1,0:T(8,128)(2,1)S(1)}, bf16[2048,256]{1,0:T(8,128)(2,1)}, u32[]{:S(2)}, u32[]{:S(2)}) collective-permute-start(bf16[2048,256]{1,0:T(8,128)(2,1)S(1)} %fusion.1), channel_id=1, source_target_pairs={{0,2},{2,4},{4,6},{6,0},{1,7},{3,1},{5,3},{7,5},{8,10},{10,12},{12... | collective-permute-start | bytes 3145736 | tf_op jit(solution)/shard_map/ppermute | solution.py:24
  109.9 4.1 %collective-permute-done.10 = bf16[1024,256]{1,0:T(8,128)(2,1)S(1)} collective-permute-done((bf16[1024,256]{1,0:T(8,128)(2,1)S(1)}, bf16[1024,256]{1,0:T(8,128)(2,1)S(1)}, u32[]{:S(2)}, u32[]{:S(2)}) %collective-permute-start.10) | collective-permute-done | bytes 524320 | tf_op jit(solution)/shard_map/ppermute | solution.py:24
  114.0 2.0 %fusion = bf16[2048,256]{1,0:T(8,128)(2,1)} fusion(bf16[2048,256]{1,0:T(8,128)(2,1)} %get-tuple-element.20, bf16[1024,256]{1,0:T(8,128)(2,1)S(1)} %collective-permute-done.10), kind=kLoop, calls=%fused_computation.14 | loop fusion | flops 1048576 | bytes 1572864 | tf_op jit(solution)/shard_map/dynamic_update_slice | solution.py:305
  116.0 1.5 collective-permute-start.11
  117.5 7.7 %collective-permute-done.27 = bf16[2048,256]{1,0:T(8,128)(2,1)S(1)} collective-permute-done((bf16[2048,256]{1,0:T(8,128)(2,1)S(1)}, bf16[2048,256]{1,0:T(8,128)(2,1)S(1)}, u32[]{:S(2)}, u32[]{:S(2)}) %collective-permute-start.27) | collective-permute-done | bytes 1048608 | tf_op jit(solution)/shard_map/ppermute | solution.py:24
  125.2 1.0 copy-done.11
  126.2 2.2 %collective-permute-start.28 = (bf16[1024,256]{1,0:T(8,128)(2,1)S(1)}, bf16[1024,256]{1,0:T(8,128)(2,1)}, u32[]{:S(2)}, u32[]{:S(2)}) collective-permute-start(bf16[1024,256]{1,0:T(8,128)(2,1)S(1)} %slice.101), channel_id=1, source_target_pairs={{0,1},{1,0},{2,3},{3,2},{4,5},{5,4},{6,7},{7,6},{8,9},{9,8},{10,11... | collective-permute-start | bytes 1572872 | tf_op jit(solution)/shard_map/ppermute | solution.py:28
  128.7 7.8 %collective-permute-done.20 = bf16[2048,256]{1,0:T(8,128)(2,1)} collective-permute-done((bf16[2048,256]{1,0:T(8,128)(2,1)S(1)}, bf16[2048,256]{1,0:T(8,128)(2,1)}, u32[]{:S(2)}, u32[]{:S(2)}) %collective-permute-start.20) | collective-permute-done | bytes 1048608 | tf_op jit(solution)/shard_map/ppermute | solution.py:24
  136.6 1.1 slice.97
  137.6 2.2 %collective-permute-start.21 = (bf16[1024,256]{1,0:T(8,128)(2,1)S(1)}, bf16[1024,256]{1,0:T(8,128)(2,1)S(1)}, u32[]{:S(2)}, u32[]{:S(2)}) collective-permute-start(bf16[1024,256]{1,0:T(8,128)(2,1)S(1)} %slice.97), channel_id=1, source_target_pairs={{0,1},{1,0},{2,3},{3,2},{4,5},{5,4},{6,7},{7,6},{8,9},{9,8},{10,11... | collective-permute-start | bytes 1572872 | tf_op jit(solution)/shard_map/ppermute | solution.py:28
  139.8 8.0 %collective-permute-done.11 = bf16[2048,256]{1,0:T(8,128)(2,1)} collective-permute-done((bf16[2048,256]{1,0:T(8,128)(2,1)}, bf16[2048,256]{1,0:T(8,128)(2,1)}, u32[]{:S(2)}, u32[]{:S(2)}) %collective-permute-start.11) | collective-permute-done | bytes 1048608 | tf_op jit(solution)/shard_map/ppermute | solution.py:24
  147.8 1.9 slice.91
  149.7 2.1 %collective-permute-start.12 = (bf16[1024,256]{1,0:T(8,128)(2,1)}, bf16[1024,256]{1,0:T(8,128)(2,1)}, u32[]{:S(2)}, u32[]{:S(2)}) collective-permute-start(bf16[1024,256]{1,0:T(8,128)(2,1)} %slice.91), channel_id=1, source_target_pairs={{0,1},{1,0},{2,3},{3,2},{4,5},{5,4},{6,7},{7,6},{8,9},{9,8},{10,11... | collective-permute-start | bytes 1572872 | tf_op jit(solution)/shard_map/ppermute | solution.py:28
  151.7 1.2 add_convert_fusion.second_ref
  153.0 1.2 add_convert_fusion.2.first_ref
  154.3 2.1 %collective-permute-start.29 = (bf16[2,8,256]{2,1,0:T(8,128)(2,1)S(1)}, bf16[2,8,256]{2,1,0:T(8,128)(2,1)S(1)}, u32[]{:S(2)}, u32[]{:S(2)}) collective-permute-start(bf16[2,8,256]{2,1,0:T(8,128)(2,1)S(1)} %pad_maximum_fusion.5), channel_id=1, source_target_pairs={{0,1},{32,33},{64,65},{96,97},{1,32},{33,64},{65,96},{2,3},{34,35}... | collective-permute-start | bytes 24584 | tf_op jit(solution)/shard_map/ppermute | solution.py:314
  156.4 0.9 collective-permute-done.29
  157.3 3.8 %states.1 = (f32[2,1024,128]{2,1,0:T(8,128)S(1)}, f32[16,8,256]{2,1,0:T(8,128)S(1)}, f32[16,256]{1,0:T(8,128)S(1)}) custom-call(bf16[1024,256]{1,0:T(8,128)(2,1)S(1)} %add_convert_fusion.2.first_ref, bf16[1024,256]{1,0:T(8,128)(2,1)S(1)} %add_convert_fusion.second_ref, f32[2,8,256]{2,1,0:T(8,128)S(1)} %convert_element_type.91.halo_ref, ...), custom_call_target="tpu_custom_call" | custom-call | flops 4000000 | bytes 4000000 | tf_op jit(solution)/shard_map/states/pallas_call | solution.py:237
  161.4 1.0 collective-permute-done.30.other_ref
  162.5 3.8 %collective-permute-start.31 = (f32[16,256]{1,0:T(8,128)S(1)}, f32[16,256]{1,0:T(8,128)S(1)}, u32[]{:S(2)}, u32[]{:S(2)}) collective-permute-start(f32[16,256]{1,0:T(8,128)S(1)} %add_select_fusion), channel_id=1, source_target_pairs={{0,32},{32,64},{64,96},{1,33},{33,65},{65,97},{2,34},{34,66},{66,9... | collective-permute-start | bytes 49160 | tf_op jit(solution)/shard_map/ppermute | solution.py:32
  166.3 0.9 collective-permute-done.31.one_ref
  167.1 5.9 %collective-permute-start.32 = (f32[16,256]{1,0:T(8,128)S(1)}, f32[16,256]{1,0:T(8,128)S(1)}, u32[]{:S(2)}, u32[]{:S(2)}) collective-permute-start(f32[16,256]{1,0:T(8,128)S(1)} %get-tuple-element.45), channel_id=1, source_target_pairs={{0,64},{32,96},{1,65},{33,97},{2,66},{34,98},{3,67},{35,99},{4,68}... | collective-permute-start | bytes 49160 | tf_op jit(solution)/shard_map/ppermute | solution.py:32
  173.1 1.4 add_convert_fusion.4.part_ref
  174.5 4.7 %collective-permute-start.13 = (bf16[8,256]{1,0:T(8,128)(2,1)S(1)}, bf16[8,256]{1,0:T(8,128)(2,1)S(1)}, u32[]{:S(2)}, u32[]{:S(2)}) collective-permute-start(bf16[8,256]{1,0:T(8,128)(2,1)S(1)} %slice.92), channel_id=1, source_target_pairs={{0,1},{32,33},{64,65},{96,97},{1,32},{33,64},{65,96},{2,3},{34,35}... | collective-permute-start | bytes 12296 | tf_op jit(solution)/shard_map/ppermute | solution.py:314
  179.9 3.5 %convolve.1.conv_ref = f32[2,1024,128]{2,1,0:T(8,128)S(1)} custom-call(s32[1]{0:T(128)} %bitcast.5.core_ref, f32[2,1024,128]{2,1,0:T(8,128)S(1)} %get-tuple-element.28.source_ref, f32[16,8,256]{2,1,0:T(8,128)S(1)} %get-tuple-element.29.init_ref, f32[16,256]{1,0:T(8,128)S(1)} %slice_multiply_fusion.1.rate_ref, f32[16,256]{1,0:T(8,128)S(1)} %get-tuple-element.46.weight_ref, ...), custom_call_target="tpu_custom_call" | custom-call | flops 8000000 | bytes 8000000 | tf_op jit(solution)/shard_map/convolve/pallas_call | solution.py:237
  183.4 1.0 gate.1
  184.5 2.2 %collective-permute-start.33 = (bf16[512,256]{1,0:T(8,128)(2,1)S(1)}, bf16[512,256]{1,0:T(8,128)(2,1)S(1)}, u32[]{:S(2)}, u32[]{:S(2)}) collective-permute-start(bf16[512,256]{1,0:T(8,128)(2,1)S(1)} %get-tuple-element.31), channel_id=1, source_target_pairs={{0,0},{1,16},{8,8},{9,24},{16,1},{17,17},{24,9},{25,25},{2,2},{3,1... | collective-permute-start | bytes 786440 | tf_op jit(solution)/shard_map/ppermute | solution.py:363
  186.7 2.9 %collective-permute-start.34 = (bf16[512,256]{1,0:T(8,128)(2,1)S(1)}, bf16[512,256]{1,0:T(8,128)(2,1)S(1)}, u32[]{:S(2)}, u32[]{:S(2)}) collective-permute-start(bf16[512,256]{1,0:T(8,128)(2,1)S(1)} %get-tuple-element.32), channel_id=1, source_target_pairs={{0,8},{1,24},{8,0},{9,16},{16,9},{17,25},{24,1},{25,17},{2,10},{3,... | collective-permute-start | bytes 786440 | tf_op jit(solution)/shard_map/ppermute | solution.py:363
  189.7 5.2 %collective-permute-done.33 = bf16[512,256]{1,0:T(8,128)(2,1)S(1)} collective-permute-done((bf16[512,256]{1,0:T(8,128)(2,1)S(1)}, bf16[512,256]{1,0:T(8,128)(2,1)S(1)}, u32[]{:S(2)}, u32[]{:S(2)}) %collective-permute-start.33) | collective-permute-done | bytes 262176 | tf_op jit(solution)/shard_map/ppermute | solution.py:363
  194.9 1.7 collective-permute-done.34
  (85 shorter events, 7.0 us)
Async XLA Ops:
  0.0 5.4 %collective-permute-start = (bf16[512,1024]{1,0:T(8,128)(2,1)}, bf16[512,1024]{1,0:T(8,128)(2,1)S(1)}, u32[]{:S(2)}, u32[]{:S(2)}) collective-permute-start(bf16[512,1024]{1,0:T(8,128)(2,1)} %param.6), channel_id=1, source_target_pairs={{0,1},{1,0},{2,3},{3,2},{4,5},{5,4},{6,7},{7,6},{8,9},{9,8},{10,11... | collective-permute-start | bytes 3145736 | tf_op jit(solution)/shard_map/ppermute | solution.py:28
  1.4 8.2 %collective-permute-start.5 = (bf16[3,1024,256]{2,1,0:T(8,128)(2,1)}, bf16[3,1024,256]{2,1,0:T(8,128)(2,1)}, u32[]{:S(2)}, u32[]{:S(2)}) collective-permute-start(bf16[3,1024,256]{2,1,0:T(8,128)(2,1)} %bitcast.29), channel_id=1, source_target_pairs={{0,1},{1,0},{2,3},{3,2},{4,5},{5,4},{6,7},{7,6},{8,9},{9,8},{10,11... | collective-permute-start | bytes 4718600 | tf_op jit(solution)/shard_map/ppermute | solution.py:28
  6.8 2.8 %copy-start.10 = (bf16[1024,3,256]{2,0,1:T(8,128)(2,1)S(1)}, bf16[1024,3,256]{2,0,1:T(8,128)(2,1)}, u32[]{:S(2)}) copy-start(bf16[1024,3,256]{2,0,1:T(8,128)(2,1)} %param.7) | copy-start | bytes 4718596
  7.0 4.3 %copy-start.9 = (bf16[512,2048]{1,0:T(8,128)(2,1)}, bf16[512,2048]{1,0:T(8,128)(2,1)S(1)}, u32[]{:S(2)}) copy-start(bf16[512,2048]{1,0:T(8,128)(2,1)S(1)} %pad_maximum_fusion.t_own) | copy-start | bytes 6291460
  7.0 25.6 %collective-permute-start.1 = (bf16[512,2048]{1,0:T(8,128)(2,1)S(1)}, bf16[512,2048]{1,0:T(8,128)(2,1)}, u32[]{:S(2)}, u32[]{:S(2)}) collective-permute-start(bf16[512,2048]{1,0:T(8,128)(2,1)S(1)} %pad_maximum_fusion.t_own), channel_id=1, source_target_pairs={{0,8},{8,16},{16,24},{24,0},{1,25},{9,1},{17,9},{25,17},{2,10},{10... | collective-permute-start | bytes 6291464 | tf_op jit(solution)/shard_map/ppermute | solution.py:24
  13.5 24.0 %collective-permute-start.22 = (bf16[2048,256]{1,0:T(8,128)(2,1)}, bf16[2048,256]{1,0:T(8,128)(2,1)}, u32[]{:S(2)}, u32[]{:S(2)}) collective-permute-start(bf16[2048,256]{1,0:T(8,128)(2,1)} %pad_maximum_fusion.3.w_own), channel_id=1, source_target_pairs={{0,32},{32,64},{64,96},{96,0},{1,97},{33,1},{65,33},{97,65},{2,34}... | collective-permute-start | bytes 3145736 | tf_op jit(solution)/shard_map/ppermute | solution.py:24
  18.5 22.6 %collective-permute-start.15 = (bf16[2048,256]{1,0:T(8,128)(2,1)}, bf16[2048,256]{1,0:T(8,128)(2,1)}, u32[]{:S(2)}, u32[]{:S(2)}) collective-permute-start(bf16[2048,256]{1,0:T(8,128)(2,1)} %pad_maximum_fusion.2.w_own), channel_id=1, source_target_pairs={{0,32},{32,64},{64,96},{96,0},{1,97},{33,1},{65,33},{97,65},{2,34}... | collective-permute-start | bytes 3145736 | tf_op jit(solution)/shard_map/ppermute | solution.py:24
  20.0 30.8 %collective-permute-start.6 = (bf16[2048,256]{1,0:T(8,128)(2,1)}, bf16[2048,256]{1,0:T(8,128)(2,1)}, u32[]{:S(2)}, u32[]{:S(2)}) collective-permute-start(bf16[2048,256]{1,0:T(8,128)(2,1)} %pad_maximum_fusion.1.w_own), channel_id=1, source_target_pairs={{0,32},{32,64},{64,96},{96,0},{1,97},{33,1},{65,33},{97,65},{2,34}... | collective-permute-start | bytes 3145736 | tf_op jit(solution)/shard_map/ppermute | solution.py:24
  33.9 25.5 %collective-permute-start.3 = (bf16[256,2048]{1,0:T(8,128)(2,1)S(1)}, bf16[256,2048]{1,0:T(8,128)(2,1)S(1)}, u32[]{:S(2)}, u32[]{:S(2)}) collective-permute-start(bf16[256,2048]{1,0:T(8,128)(2,1)S(1)} %constant_dynamic-slice_fusion.3), channel_id=1, source_target_pairs={{0,8},{8,16},{16,24},{24,0},{1,25},{9,1},{17,9},{25,17},{2,10},{10... | collective-permute-start | bytes 3145736 | tf_op jit(solution)/shard_map/ppermute | solution.py:24
  37.5 32.8 %collective-permute-start.2 = (bf16[512,2048]{1,0:T(8,128)(2,1)}, bf16[512,2048]{1,0:T(8,128)(2,1)}, u32[]{:S(2)}, u32[]{:S(2)}) collective-permute-start(bf16[512,2048]{1,0:T(8,128)(2,1)} %collective-permute-done.1.t_a), channel_id=1, source_target_pairs={{0,1},{1,0},{2,3},{3,2},{4,5},{5,4},{6,7},{7,6},{8,9},{9,8},{10,11... | collective-permute-start | bytes 6291464 | tf_op jit(solution)/shard_map/ppermute | solution.py:28
  38.5 17.7 %collective-permute-start.24 = (bf16[1024,256]{1,0:T(8,128)(2,1)S(1)}, bf16[1024,256]{1,0:T(8,128)(2,1)S(1)}, u32[]{:S(2)}, u32[]{:S(2)}) collective-permute-start(bf16[1024,256]{1,0:T(8,128)(2,1)S(1)} %constant_dynamic-slice_fusion), channel_id=1, source_target_pairs={{0,32},{32,64},{64,96},{96,0},{1,97},{33,1},{65,33},{97,65},{2,34}... | collective-permute-start | bytes 1572872 | tf_op jit(solution)/shard_map/ppermute | solution.py:24
  42.1 19.8 %collective-permute-start.17 = (bf16[1024,256]{1,0:T(8,128)(2,1)S(1)}, bf16[1024,256]{1,0:T(8,128)(2,1)}, u32[]{:S(2)}, u32[]{:S(2)}) collective-permute-start(bf16[1024,256]{1,0:T(8,128)(2,1)S(1)} %constant_dynamic-slice_fusion.1), channel_id=1, source_target_pairs={{0,32},{32,64},{64,96},{96,0},{1,97},{33,1},{65,33},{97,65},{2,34}... | collective-permute-start | bytes 1572872 | tf_op jit(solution)/shard_map/ppermute | solution.py:24
  50.8 18.8 %collective-permute-start.23 = (bf16[2048,256]{1,0:T(8,128)(2,1)}, bf16[2048,256]{1,0:T(8,128)(2,1)}, u32[]{:S(2)}, u32[]{:S(2)}) collective-permute-start(bf16[2048,256]{1,0:T(8,128)(2,1)} %collective-permute-done.22.w_a), channel_id=1, source_target_pairs={{0,1},{1,0},{2,3},{3,2},{4,5},{5,4},{6,7},{7,6},{8,9},{9,8},{10,11... | collective-permute-start | bytes 3145736 | tf_op jit(solution)/shard_map/ppermute | solution.py:28
  56.3 11.2 %collective-permute-start.8 = (bf16[1024,256]{1,0:T(8,128)(2,1)S(1)}, bf16[1024,256]{1,0:T(8,128)(2,1)}, u32[]{:S(2)}, u32[]{:S(2)}) collective-permute-start(bf16[1024,256]{1,0:T(8,128)(2,1)S(1)} %constant_dynamic-slice_fusion.2), channel_id=1, source_target_pairs={{0,32},{32,64},{64,96},{96,0},{1,97},{33,1},{65,33},{97,65},{2,34}... | collective-permute-start | bytes 1572872 | tf_op jit(solution)/shard_map/ppermute | solution.py:24
  59.4 21.5 %copy-start = (bf16[256,2048]{1,0:T(8,128)(2,1)}, bf16[256,2048]{1,0:T(8,128)(2,1)S(1)}, u32[]{:S(2)}) copy-start(bf16[256,2048]{1,0:T(8,128)(2,1)S(1)} %collective-permute-done.3.t_c) | copy-start | bytes 3145732
  59.4 10.7 %collective-permute-start.4 = (bf16[256,2048]{1,0:T(8,128)(2,1)S(1)}, bf16[256,2048]{1,0:T(8,128)(2,1)S(1)}, u32[]{:S(2)}, u32[]{:S(2)}) collective-permute-start(bf16[256,2048]{1,0:T(8,128)(2,1)S(1)} %collective-permute-done.3.t_c), channel_id=1, source_target_pairs={{0,1},{1,0},{2,3},{3,2},{4,5},{5,4},{6,7},{7,6},{8,9},{9,8},{10,11... | collective-permute-start | bytes 3145736 | tf_op jit(solution)/shard_map/ppermute | solution.py:28
  61.9 6.8 %collective-permute-start.25 = (bf16[1024,256]{1,0:T(8,128)(2,1)S(1)}, bf16[1024,256]{1,0:T(8,128)(2,1)S(1)}, u32[]{:S(2)}, u32[]{:S(2)}) collective-permute-start(bf16[1024,256]{1,0:T(8,128)(2,1)S(1)} %collective-permute-done.24.w_c), channel_id=1, source_target_pairs={{0,1},{1,0},{2,3},{3,2},{4,5},{5,4},{6,7},{7,6},{8,9},{9,8},{10,11... | collective-permute-start | bytes 1572872 | tf_op jit(solution)/shard_map/ppermute | solution.py:28
  63.1 0.8 copy-start.5
  67.5 17.4 %collective-permute-start.16 = (bf16[2048,256]{1,0:T(8,128)(2,1)}, bf16[2048,256]{1,0:T(8,128)(2,1)}, u32[]{:S(2)}, u32[]{:S(2)}) collective-permute-start(bf16[2048,256]{1,0:T(8,128)(2,1)} %collective-permute-done.15.w_a), channel_id=1, source_target_pairs={{0,1},{1,0},{2,3},{3,2},{4,5},{5,4},{6,7},{7,6},{8,9},{9,8},{10,11... | collective-permute-start | bytes 3145736 | tf_op jit(solution)/shard_map/ppermute | solution.py:28
  68.7 0.8 copy-start.7
  69.5 26.5 %collective-permute-start.7 = (bf16[2048,256]{1,0:T(8,128)(2,1)}, bf16[2048,256]{1,0:T(8,128)(2,1)}, u32[]{:S(2)}, u32[]{:S(2)}) collective-permute-start(bf16[2048,256]{1,0:T(8,128)(2,1)} %collective-permute-done.6.w_a), channel_id=1, source_target_pairs={{0,1},{1,0},{2,3},{3,2},{4,5},{5,4},{6,7},{7,6},{8,9},{9,8},{10,11... | collective-permute-start | bytes 3145736 | tf_op jit(solution)/shard_map/ppermute | solution.py:28
  69.5 15.3 %collective-permute-start.18 = (bf16[1024,256]{1,0:T(8,128)(2,1)}, bf16[1024,256]{1,0:T(8,128)(2,1)}, u32[]{:S(2)}, u32[]{:S(2)}) collective-permute-start(bf16[1024,256]{1,0:T(8,128)(2,1)} %collective-permute-done.17.w_c), channel_id=1, source_target_pairs={{0,1},{1,0},{2,3},{3,2},{4,5},{5,4},{6,7},{7,6},{8,9},{9,8},{10,11... | collective-permute-start | bytes 1572872 | tf_op jit(solution)/shard_map/ppermute | solution.py:28
  70.1 10.8 %copy-start.3 = (bf16[256,2048]{1,0:T(8,128)(2,1)}, bf16[256,2048]{1,0:T(8,128)(2,1)S(1)}, u32[]{:S(2)}) copy-start(bf16[256,2048]{1,0:T(8,128)(2,1)S(1)} %collective-permute-done.4.t_d) | copy-start | bytes 3145732
  70.2 25.8 %collective-permute-start.9 = (bf16[1024,256]{1,0:T(8,128)(2,1)}, bf16[1024,256]{1,0:T(8,128)(2,1)S(1)}, u32[]{:S(2)}, u32[]{:S(2)}) collective-permute-start(bf16[1024,256]{1,0:T(8,128)(2,1)} %collective-permute-done.8.w_c), channel_id=1, source_target_pairs={{0,1},{1,0},{2,3},{3,2},{4,5},{5,4},{6,7},{7,6},{8,9},{9,8},{10,11... | collective-permute-start | bytes 1572872 | tf_op jit(solution)/shard_map/ppermute | solution.py:28
  70.3 1.3 copy-start.6
  71.6 1.0 copy-start.8
  81.0 25.3 %collective-permute-start.26 = (bf16[1024,256]{1,0:T(8,128)(2,1)S(1)}, bf16[1024,256]{1,0:T(8,128)(2,1)S(1)}, u32[]{:S(2)}, u32[]{:S(2)}) collective-permute-start(bf16[1024,256]{1,0:T(8,128)(2,1)S(1)} %get-tuple-element.27), channel_id=1, source_target_pairs={{0,2},{2,4},{4,6},{6,0},{1,7},{3,1},{5,3},{7,5},{8,10},{10,12},{12... | collective-permute-start | bytes 1572872 | tf_op jit(solution)/shard_map/ppermute | solution.py:24
  84.9 1.2 copy-start.1
  86.1 1.2 copy-start.4
  87.3 8.7 %copy-start.2 = (bf16[256,2048]{1,0:T(8,128)(2,1)S(1)}, bf16[256,2048]{1,0:T(8,128)(2,1)}, u32[]{:S(2)}) copy-start(bf16[256,2048]{1,0:T(8,128)(2,1)} %copy-done) | copy-start | bytes 3145732
  95.9 10.8 %collective-permute-start.19 = (bf16[1024,256]{1,0:T(8,128)(2,1)S(1)}, bf16[1024,256]{1,0:T(8,128)(2,1)S(1)}, u32[]{:S(2)}, u32[]{:S(2)}) collective-permute-start(bf16[1024,256]{1,0:T(8,128)(2,1)S(1)} %get-tuple-element.24), channel_id=1, source_target_pairs={{0,2},{2,4},{4,6},{6,0},{1,7},{3,1},{5,3},{7,5},{8,10},{10,12},{12... | collective-permute-start | bytes 1572872 | tf_op jit(solution)/shard_map/ppermute | solution.py:24
  105.5 8.5 %collective-permute-start.10 = (bf16[1024,256]{1,0:T(8,128)(2,1)S(1)}, bf16[1024,256]{1,0:T(8,128)(2,1)S(1)}, u32[]{:S(2)}, u32[]{:S(2)}) collective-permute-start(bf16[1024,256]{1,0:T(8,128)(2,1)S(1)} %get-tuple-element.21), channel_id=1, source_target_pairs={{0,2},{2,4},{4,6},{6,0},{1,7},{3,1},{5,3},{7,5},{8,10},{10,12},{12... | collective-permute-start | bytes 1572872 | tf_op jit(solution)/shard_map/ppermute | solution.py:24
  106.5 18.7 %collective-permute-start.27 = (bf16[2048,256]{1,0:T(8,128)(2,1)S(1)}, bf16[2048,256]{1,0:T(8,128)(2,1)S(1)}, u32[]{:S(2)}, u32[]{:S(2)}) collective-permute-start(bf16[2048,256]{1,0:T(8,128)(2,1)S(1)} %fusion.2), channel_id=1, source_target_pairs={{0,2},{2,4},{4,6},{6,0},{1,7},{3,1},{5,3},{7,5},{8,10},{10,12},{12... | collective-permute-start | bytes 3145736 | tf_op jit(solution)/shard_map/ppermute | solution.py:24
  106.6 21.8 %copy-start.13 = (f32[7,3,512]{2,0,1:T(8,128)S(1)}, f32[7,3,512]{2,0,1:T(8,128)}, u32[]{:S(2)}) copy-start(f32[7,3,512]{2,0,1:T(8,128)} %param.8) | copy-start | bytes 129028
  106.6 21.8 %copy-start.14 = (f32[16,512]{1,0:T(8,128)S(1)}, f32[16,512]{1,0:T(8,128)}, u32[]{:S(2)}) copy-start(f32[16,512]{1,0:T(8,128)} %param.9) | copy-start | bytes 98308
  106.6 21.8 %copy-start.15 = (f32[16,512]{1,0:T(8,128)S(1)}, f32[16,512]{1,0:T(8,128)}, u32[]{:S(2)}) copy-start(f32[16,512]{1,0:T(8,128)} %param.10) | copy-start | bytes 98308
  106.7 21.8 %copy-start.16 = (f32[512]{0:T(512)S(1)}, f32[512]{0:T(512)}, u32[]{:S(2)}) copy-start(f32[512]{0:T(512)} %param.11) | copy-start | bytes 6148
  106.9 29.6 %collective-permute-start.20 = (bf16[2048,256]{1,0:T(8,128)(2,1)S(1)}, bf16[2048,256]{1,0:T(8,128)(2,1)}, u32[]{:S(2)}, u32[]{:S(2)}) collective-permute-start(bf16[2048,256]{1,0:T(8,128)(2,1)S(1)} %fusion.1), channel_id=1, source_target_pairs={{0,2},{2,4},{4,6},{6,0},{1,7},{3,1},{5,3},{7,5},{8,10},{10,12},{12... | collective-permute-start | bytes 3145736 | tf_op jit(solution)/shard_map/ppermute | solution.py:24
  116.0 31.8 %collective-permute-start.11 = (bf16[2048,256]{1,0:T(8,128)(2,1)}, bf16[2048,256]{1,0:T(8,128)(2,1)}, u32[]{:S(2)}, u32[]{:S(2)}) collective-permute-start(bf16[2048,256]{1,0:T(8,128)(2,1)} %fusion), channel_id=1, source_target_pairs={{0,2},{2,4},{4,6},{6,0},{1,7},{3,1},{5,3},{7,5},{8,10},{10,12},{12... | collective-permute-start | bytes 3145736 | tf_op jit(solution)/shard_map/ppermute | solution.py:24
  125.2 1.0 copy-start.11
  126.2 25.5 %collective-permute-start.28 = (bf16[1024,256]{1,0:T(8,128)(2,1)S(1)}, bf16[1024,256]{1,0:T(8,128)(2,1)}, u32[]{:S(2)}, u32[]{:S(2)}) collective-permute-start(bf16[1024,256]{1,0:T(8,128)(2,1)S(1)} %slice.101), channel_id=1, source_target_pairs={{0,1},{1,0},{2,3},{3,2},{4,5},{5,4},{6,7},{7,6},{8,9},{9,8},{10,11... | collective-permute-start | bytes 1572872 | tf_op jit(solution)/shard_map/ppermute | solution.py:28
  128.6 11.2 %collective-permute-start.14 = (f32[54,256]{1,0:T(8,128)S(1)}, f32[54,256]{1,0:T(8,128)S(1)}, u32[]{:S(2)}, u32[]{:S(2)}) collective-permute-start(f32[54,256]{1,0:T(8,128)S(1)} %fusion.5), channel_id=1, source_target_pairs={{0,1},{1,0},{2,3},{3,2},{4,5},{5,4},{6,7},{7,6},{8,9},{9,8},{10,11... | collective-permute-start | bytes 165896 | tf_op jit(solution)/shard_map/ppermute | solution.py:28
  128.7 23.0 %copy-start.12 = (bf16[2048,256]{1,0:T(8,128)(2,1)S(1)}, bf16[2048,256]{1,0:T(8,128)(2,1)}, u32[]{:S(2)}) copy-start(bf16[2048,256]{1,0:T(8,128)(2,1)} %copy-done.11) | copy-start | bytes 3145732
  137.6 15.4 %collective-permute-start.21 = (bf16[1024,256]{1,0:T(8,128)(2,1)S(1)}, bf16[1024,256]{1,0:T(8,128)(2,1)S(1)}, u32[]{:S(2)}, u32[]{:S(2)}) collective-permute-start(bf16[1024,256]{1,0:T(8,128)(2,1)S(1)} %slice.97), channel_id=1, source_target_pairs={{0,1},{1,0},{2,3},{3,2},{4,5},{5,4},{6,7},{7,6},{8,9},{9,8},{10,11... | collective-permute-start | bytes 1572872 | tf_op jit(solution)/shard_map/ppermute | solution.py:28
  149.7 23.4 %collective-permute-start.12 = (bf16[1024,256]{1,0:T(8,128)(2,1)}, bf16[1024,256]{1,0:T(8,128)(2,1)}, u32[]{:S(2)}, u32[]{:S(2)}) collective-permute-start(bf16[1024,256]{1,0:T(8,128)(2,1)} %slice.91), channel_id=1, source_target_pairs={{0,1},{1,0},{2,3},{3,2},{4,5},{5,4},{6,7},{7,6},{8,9},{9,8},{10,11... | collective-permute-start | bytes 1572872 | tf_op jit(solution)/shard_map/ppermute | solution.py:28
  154.3 3.1 %collective-permute-start.29 = (bf16[2,8,256]{2,1,0:T(8,128)(2,1)S(1)}, bf16[2,8,256]{2,1,0:T(8,128)(2,1)S(1)}, u32[]{:S(2)}, u32[]{:S(2)}) collective-permute-start(bf16[2,8,256]{2,1,0:T(8,128)(2,1)S(1)} %pad_maximum_fusion.5), channel_id=1, source_target_pairs={{0,1},{32,33},{64,65},{96,97},{1,32},{33,64},{65,96},{2,3},{34,35}... | collective-permute-start | bytes 24584 | tf_op jit(solution)/shard_map/ppermute | solution.py:314
  161.2 1.3 collective-permute-start.30
  162.5 4.7 %collective-permute-start.31 = (f32[16,256]{1,0:T(8,128)S(1)}, f32[16,256]{1,0:T(8,128)S(1)}, u32[]{:S(2)}, u32[]{:S(2)}) collective-permute-start(f32[16,256]{1,0:T(8,128)S(1)} %add_select_fusion), channel_id=1, source_target_pairs={{0,32},{32,64},{64,96},{1,33},{33,65},{65,97},{2,34},{34,66},{66,9... | collective-permute-start | bytes 49160 | tf_op jit(solution)/shard_map/ppermute | solution.py:32
  167.1 12.7 %collective-permute-start.32 = (f32[16,256]{1,0:T(8,128)S(1)}, f32[16,256]{1,0:T(8,128)S(1)}, u32[]{:S(2)}, u32[]{:S(2)}) collective-permute-start(f32[16,256]{1,0:T(8,128)S(1)} %get-tuple-element.45), channel_id=1, source_target_pairs={{0,64},{32,96},{1,65},{33,97},{2,66},{34,98},{3,67},{35,99},{4,68}... | collective-permute-start | bytes 49160 | tf_op jit(solution)/shard_map/ppermute | solution.py:32
  174.5 5.4 %collective-permute-start.13 = (bf16[8,256]{1,0:T(8,128)(2,1)S(1)}, bf16[8,256]{1,0:T(8,128)(2,1)S(1)}, u32[]{:S(2)}, u32[]{:S(2)}) collective-permute-start(bf16[8,256]{1,0:T(8,128)(2,1)S(1)} %slice.92), channel_id=1, source_target_pairs={{0,1},{32,33},{64,65},{96,97},{1,32},{33,64},{65,96},{2,3},{34,35}... | collective-permute-start | bytes 12296 | tf_op jit(solution)/shard_map/ppermute | solution.py:314
  184.5 10.4 %collective-permute-start.33 = (bf16[512,256]{1,0:T(8,128)(2,1)S(1)}, bf16[512,256]{1,0:T(8,128)(2,1)S(1)}, u32[]{:S(2)}, u32[]{:S(2)}) collective-permute-start(bf16[512,256]{1,0:T(8,128)(2,1)S(1)} %get-tuple-element.31), channel_id=1, source_target_pairs={{0,0},{1,16},{8,8},{9,24},{16,1},{17,17},{24,9},{25,25},{2,2},{3,1... | collective-permute-start | bytes 786440 | tf_op jit(solution)/shard_map/ppermute | solution.py:363
  186.7 9.9 %collective-permute-start.34 = (bf16[512,256]{1,0:T(8,128)(2,1)S(1)}, bf16[512,256]{1,0:T(8,128)(2,1)S(1)}, u32[]{:S(2)}, u32[]{:S(2)}) collective-permute-start(bf16[512,256]{1,0:T(8,128)(2,1)S(1)} %get-tuple-element.32), channel_id=1, source_target_pairs={{0,8},{1,24},{8,0},{9,16},{16,9},{17,25},{24,1},{25,17},{2,10},{3,... | collective-permute-start | bytes 786440 | tf_op jit(solution)/shard_map/ppermute | solution.py:363

commit v2 on v1

v2 whole, which is shorter than its diff:
```python
import functools

import jax
import jax.numpy as jnp
from jax import lax
from jax.experimental import pallas as pl
from jax.experimental.pallas import tpu as pltpu
from jax.sharding import Mesh
from jax.sharding import PartitionSpec as P

SHORT = 7
HALO = 8
SEGMENTS = 8
TILES = 2
LANES = 128
N = 4
F32 = jnp.float32
BF16 = jnp.bfloat16
VMEM_LIMIT = 48 * 1024 * 1024
OWN, RIGHT, LEFT, OPPOSITE = range(4)
KEEP, GIVE, FAR, SELF = range(4)


def ring(value, axis, steps):
    return lax.ppermute(value, axis, [(i, (i + steps) % N) for i in range(N)])


def split_ring(value, axis):
    up = [(2 * i, 2 * ((i + 1) % N)) for i in range(N)]
    down = [(2 * i + 1, 2 * ((i - 1) % N) + 1) for i in range(N)]
    return lax.ppermute(value, (axis, "c"), up + down)


def core_swap(value):
    return lax.ppermute(value, "c", [(0, 1), (1, 0)])


def later(value, steps):
    return lax.ppermute(value, "y", [(i, i + steps) for i in range(N - steps)])


def after(value, *others):
    return lax.optimization_barrier((value,) + others)[0]


def local_call(kernel, shapes, scalars, arrays, kept, scratch, flops, bytes_accessed, name):
    vmem = pl.BlockSpec(memory_space=pltpu.VMEM)
    return pl.pallas_call(
        kernel,
        out_shape=shapes,
        in_specs=[pl.BlockSpec(memory_space=pltpu.SMEM)] * len(scalars)
        + [vmem] * len(arrays)
        + [pl.BlockSpec(memory_space=pl.ANY)] * len(kept),
        out_specs=tuple(vmem for _ in shapes),
        scratch_shapes=scratch,
        compiler_params=pltpu.CompilerParams(vmem_limit_bytes=VMEM_LIMIT),
        cost_estimate=pl.CostEstimate(flops=flops, bytes_accessed=bytes_accessed, transcendentals=0),
        name=name,
    )(*scalars, *arrays, *kept)


def project_kernel(plan, slots, streams, n_after, where_ref, *refs):
    core = where_ref[4]
    tokens = refs[: len(slots)]
    all_weights = refs[len(slots)]
    passed = refs[len(slots) + 1 : len(slots) + 1 + 3 * len(streams)]
    base = len(slots) + 1 + 3 * len(streams) + n_after
    far_keep, far_give, near_ref, give_ref, t_buf, w_buf, t_sem, w_sem = refs[base:]
    rows = tokens[0].shape[0]
    total = len(plan) * rows
    middle = total // 2

    def token_copy(i):
        return pltpu.make_async_copy(tokens[i], t_buf.at[i], t_sem.at[i])

    def weight_copies(s):
        sources = (all_weights.at[streams[s]],) + tuple(passed[3 * s : 3 * s + 3])
        return [
            pltpu.make_async_copy(source, w_buf.at[s, where_ref[slot]], w_sem.at[s, slot])
            for slot, source in enumerate(sources)
        ]

    started_t, started_s = set(), set()
    for s, i in plan:
        if i not in started_t:
            started_t.add(i)
            token_copy(i).start()
        if s not in started_s:
            started_s.add(s)
            for copy in weight_copies(s):
                copy.start()
    ready_t, ready_s = set(), set()
    for number, (s, i) in enumerate(plan):
        if i not in ready_t:
            ready_t.add(i)
            token_copy(i).wait()
        if s not in ready_s:
            ready_s.add(s)
            for copy in weight_copies(s):
                copy.wait()
        at = number * rows

        def product(role):
            return jnp.dot(t_buf[i], w_buf[s, role], preferred_element_type=F32).astype(BF16)

        far = product(FAR)
        for piece in range(2):
            start = at + piece * (rows // 2)
            part = far[piece * (rows // 2) : (piece + 1) * (rows // 2)]
            side = 0 if start < middle else 1
            place = pl.ds(start - side * middle, rows // 2)

            @pl.when(core == side)
            def _():
                far_keep[place, :] = part

            @pl.when(core != side)
            def _():
                far_give[place, :] = part

        near_ref[pl.ds(at, rows), :] = product(KEEP)
        give_ref[pl.ds(at, rows), :] = product(GIVE)
        give_ref[pl.ds(total + at, rows), :] = product(SELF)


def project(where, plan, tokens, weights, passed, behind=()):
    slots = sorted({slot for _, slot in plan})
    streams = sorted({m for m, _ in plan})
    indexed = tuple((streams.index(m), slots.index(slot)) for m, slot in plan)
    rows, depth = tokens[OWN].shape
    width = weights.shape[2]
    total = len(plan) * rows
    shapes = tuple(jax.ShapeDtypeStruct((n, width), BF16) for n in (total // 2, total // 2, total, 2 * total))
    blocks = [passed[m][k] for m in streams for k in range(3)]
    return local_call(
        functools.partial(project_kernel, indexed, tuple(slots), tuple(streams), len(behind)),
        shapes,
        (where,),
        (),
        [tokens[s] for s in slots] + [weights] + blocks + list(behind),
        [
            pltpu.VMEM((len(slots), rows, depth), BF16),
            pltpu.VMEM((len(streams), 4, depth, width), BF16),
            pltpu.SemaphoreType.DMA((len(slots),)),
            pltpu.SemaphoreType.DMA((len(streams), 4)),
        ],
        2 * total * depth * 4 * width,
        2 * (len(slots) * rows * depth + 4 * len(streams) * depth * width + 4 * total * width),
        "project",
    )


def near_kernel(where_ref, keep_ref, got_ref, arrived_ref, out_ref):
    total = keep_ref.shape[0]
    half = total // 2
    step = 256
    core = where_ref[4]
    with_arrived = pl.multiple_of(core * half, half)
    without = pl.multiple_of((1 - core) * half, half)
    for start in range(0, half, step):
        here = pl.ds(with_arrived + start, step)
        out_ref[here, :] = (
            keep_ref[here, :].astype(F32)
            + got_ref[here, :].astype(F32)
            + arrived_ref[pl.ds(start, step), :].astype(F32)
        ).astype(BF16)
        here = pl.ds(without + start, step)
        out_ref[here, :] = (keep_ref[here, :].astype(F32) + got_ref[here, :].astype(F32)).astype(BF16)


def final_kernel(places, where_ref, *refs):
    *sources, out_ref, tail_ref, buf, sem = refs
    core = where_ref[4]
    rows = buf.shape[2]

    def copies(tile, side):
        piece, row = places[side][tile]
        give, got, reached, crossed = sources[4 * piece : 4 * piece + 4]
        total = reached.shape[0]
        parts = [
            give.at[pl.ds(total + row, rows)],
            got.at[pl.ds(total + row, rows)],
            reached.at[pl.ds(row, rows)],
            crossed.at[pl.ds(row, rows)],
        ]
        return [pltpu.make_async_copy(part, buf.at[tile, k], sem.at[tile, k]) for k, part in enumerate(parts)]

    for side in range(2):
        @pl.when(core == side)
        def _():
            for tile in range(TILES):
                for copy in copies(tile, side):
                    copy.start()
    for tile in range(TILES):
        for copy in copies(tile, 0):
            copy.wait()
        value = (
            buf[tile, 0].astype(F32) + buf[tile, 1].astype(F32) + buf[tile, 2].astype(F32) + buf[tile, 3].astype(F32)
        ).astype(BF16)
        out_ref[pl.ds(tile * rows, rows), :] = value
        tail_ref[tile] = value[rows - 16 :].astype(F32)[16 - HALO :]


def extend(ext, part_ref, halo_ref):
    rows = part_ref.shape[0] // TILES
    for tile in range(TILES):
        ext[tile, pl.ds(0, HALO), :] = halo_ref[tile]
        ext[tile, pl.ds(HALO, rows), :] = part_ref[pl.ds(tile * rows, rows), :].astype(F32)


def smooth(ext, tile, taps, start, count):
    total = taps[0][None, :] * ext[tile, pl.ds(HALO + start, count), :]
    for k in range(1, SHORT):
        total = total + taps[k][None, :] * ext[tile, pl.ds(HALO + start - k, count), :]
    return total


def states_kernel(first_ref, second_ref, halo1_ref, halo2_ref, taps_ref, rate_ref, source_ref, init_ref, end_ref, ext1, ext2, ends):
    length, width = first_ref.shape
    modes = rate_ref.shape[0]
    rows = length // TILES
    seg = length // SEGMENTS
    extend(ext1, first_ref, halo1_ref)
    extend(ext2, second_ref, halo2_ref)
    taps1 = [taps_ref[k, 1] for k in range(SHORT)]
    taps2 = [taps_ref[k, 2] for k in range(SHORT)]
    step = 64
    for tile in range(TILES):
        for start in range(0, rows, step):
            product = smooth(ext1, tile, taps1, start, step) * smooth(ext2, tile, taps2, start, step)
            for lane in range(0, width, LANES):
                source_ref[lane // LANES, pl.ds(tile * rows + start, step), :] = product[:, lane : lane + LANES]
    for lane in range(0, width, LANES):
        column = source_ref.at[lane // LANES]
        lanes = pl.ds(lane, LANES)
        fade = [jnp.broadcast_to(jnp.exp(-rate_ref[r, lanes])[None, :], (SEGMENTS, LANES)) for r in range(modes)]

        def body(i, states):
            for j in range(4):
                x = column[pl.ds(4 * i + j, SEGMENTS, stride=seg), :]
                states = tuple(f * s + x for f, s in zip(fade, states))
            return states

        zero = jnp.zeros((SEGMENTS, LANES), F32)
        states = lax.fori_loop(0, seg // 4, body, (zero,) * modes)
        for r in range(modes):
            ends[r, :, lanes] = states[r]
    passing = jnp.exp(-rate_ref[...] * float(seg))
    for tile in range(TILES):
        state = jnp.zeros((modes, width), F32)
        for k in range(SEGMENTS // TILES):
            s = tile * (SEGMENTS // TILES) + k
            init_ref[:, s, :] = state
            state = passing * state + ends[:, s, :]
        end_ref[tile] = state


def convolve_kernel(source_ref, init_ref, rate_ref, weight_ref, skip_ref, incoming_ref, out_ref):
    modes = rate_ref.shape[0]
    width, length = rate_ref.shape[1], source_ref.shape[1]
    seg = length // SEGMENTS
    per_tile = SEGMENTS // TILES
    number = lax.broadcasted_iota(jnp.int32, (SEGMENTS, LANES), 0)
    is_first = number < per_tile
    index = jnp.where(is_first, number, number - per_tile).astype(F32) * float(seg)
    for lane in range(0, width, LANES):
        lanes = pl.ds(lane, LANES)
        column, result = source_ref.at[lane // LANES], out_ref.at[lane // LANES]

        def spread(row):
            return jnp.broadcast_to(row[None, :], (SEGMENTS, LANES))

        rates = [spread(rate_ref[r, lanes]) for r in range(modes)]
        fade = [jnp.exp(-v) for v in rates]
        weight = [spread(weight_ref[r, lanes]) for r in range(modes)]
        skip = spread(skip_ref[0, lanes])
        states = tuple(
            init_ref[r, :, lanes]
            + jnp.exp(-rates[r] * index)
            * jnp.where(is_first, spread(incoming_ref[0, r, lanes]), spread(incoming_ref[1, r, lanes]))
            for r in range(modes)
        )

        def body(i, states):
            for j in range(4):
                at = pl.ds(4 * i + j, SEGMENTS, stride=seg)
                x = column[at, :]
                states = tuple(f * s + x for f, s in zip(fade, states))
                terms = [w * s for w, s in zip(weight, states)] + [skip * x]
                while len(terms) > 1:
                    terms = [a + b for a, b in zip(terms[::2], terms[1::2])] + ([terms[-1]] if len(terms) % 2 else [])
                result[at, :] = terms[0]
            return states

        lax.fori_loop(0, seg // 4, body, states)


def gate_kernel(part_ref, halo_ref, taps_ref, conv_ref, first_ref, second_ref, ext):
    length, width = part_ref.shape
    rows = length // TILES
    extend(ext, part_ref, halo_ref)
    taps = [taps_ref[k, 0] for k in range(SHORT)]
    step = 64
    for tile, out_ref in enumerate((first_ref, second_ref)):
        for start in range(0, rows, step):
            gate = smooth(ext, tile, taps, start, step)
            for lane in range(0, width, LANES):
                lanes = slice(lane, lane + LANES)
                filtered = gate[:, lanes] * conv_ref[lane // LANES, pl.ds(tile * rows + start, step), :]
                out_ref[pl.ds(start, step), lanes] = filtered.astype(BF16)


def on_device(tokens, in_weight, short_taps, residues, decay_scale, skip_gain):
    y, x, z, c = (lax.axis_index(a) for a in ("y", "x", "z", "c"))
    rows, _ = tokens.shape
    width = in_weight.shape[2]
    channels = short_taps.shape[2]
    modes = residues.shape[0]
    seq_total = rows * N * N
    length = TILES * rows
    first_core = c == 0
    weights = jnp.transpose(in_weight, (1, 0, 2))

    def role(row):
        ahead = (row - z) % N
        near = jnp.where(ahead == 1 + 2 * c, KEEP, GIVE)
        return jnp.where(ahead == 0, SELF, jnp.where(ahead == 2, FAR, near))

    where = jnp.stack([role(y), role(y + 1), role(y - 1), role(y + 2), c]).astype(jnp.int32)

    def around(value, axis):
        left, right = ring(value, axis, 1), ring(value, axis, -1)
        return right, left, split_ring(jnp.where(first_core, left, right), axis)

    t_right, t_left, t_opposite = around(tokens, "x")
    held = {OWN: tokens, RIGHT: t_right, LEFT: t_left, OPPOSITE: t_opposite}
    passed = {}
    passed[1] = around(weights[1], "y")
    passed[2] = around(after(weights[2], passed[1][0], passed[1][1]), "y")
    passed[0] = around(after(weights[0], passed[2][0], passed[2][1]), "y")

    packed = jnp.concatenate(
        [short_taps.reshape(SHORT * 3, channels), residues, decay_scale, skip_gain[None]], axis=0
    )
    packed = lax.dynamic_slice_in_dim(packed, (x % 2) * width, width, axis=1)
    packed = jnp.where(c == x // 2, packed, core_swap(packed))
    taps = packed[: SHORT * 3].reshape(SHORT, 3, width)
    rate = packed[SHORT * 3 + modes : SHORT * 3 + 2 * modes] / seq_total
    mode_weight = packed[SHORT * 3 : SHORT * 3 + modes] * jnp.sqrt(-jnp.expm1(-2.0 * rate))
    skip = packed[SHORT * 3 + 2 * modes :]

    def begin(plan, behind=()):
        far_keep, far_give, near, give = project(where, plan, held, weights, passed, behind)
        far = (far_keep.astype(F32) + core_swap(far_give).astype(F32)).astype(BF16)
        return far, near, give

    def middle(far, near, give):
        total = near.shape[0]
        arrived = split_ring(far, "z")
        got = core_swap(give)
        (summed,) = local_call(
            near_kernel,
            (jax.ShapeDtypeStruct(near.shape, BF16),),
            (where,),
            (near, got, arrived),
            (),
            [],
            4 * total * width,
            9 * total * width,
            "near",
        )
        return summed, got

    def end(summed, give, got):
        reached = split_ring(summed, "z")
        return give, got, reached, core_swap(reached)

    tile_shapes = (jax.ShapeDtypeStruct((length, width), BF16), jax.ShapeDtypeStruct((TILES, HALO, width), F32))

    def finish(places, pieces):
        return local_call(
            functools.partial(final_kernel, places),
            tile_shapes,
            (where,),
            (),
            [array for piece in pieces for array in piece],
            [pltpu.VMEM((TILES, 4, rows, width), BF16), pltpu.SemaphoreType.DMA((TILES, 4))],
            4 * length * width,
            10 * length * width,
            "final",
        )

    plan_a = [(1, OWN), (1, RIGHT), (1, LEFT)]
    plan_b = [(1, OPPOSITE), (2, OWN), (2, RIGHT), (2, LEFT), (2, OPPOSITE)]
    plan_c = [(0, OWN), (0, RIGHT), (0, LEFT), (0, OPPOSITE)]
    far_a, near_a, give_a = begin(plan_a)
    far_b, near_b, give_b = begin(plan_b, (far_a,))
    sum_a, got_a = middle(far_a, near_a, give_a)
    far_c, near_c, give_c = begin(plan_c, (far_b, sum_a))
    sum_b, got_b = middle(far_b, near_b, give_b)
    piece_a = end(sum_a, give_a, got_a)
    sum_c, got_c = middle(far_c, near_c, give_c)
    piece_b = end(sum_b, give_b, got_b)
    piece_c = end(sum_c, give_c, got_c)

    spot = (x + 2 * c) % N
    spots = [(spot + i) % N for i in range(N)]

    def halos(tails):
        beside = core_swap(tails[1])
        holders = {xs: divmod((N - 1 - xs) % N, TILES)[0] for xs in range(N)}
        starts = {xs: divmod((-xs) % N, TILES)[0] for xs in range(N)}
        moves = [
            ((yy * N + xs) * 2 + holders[xs], ((yy + 1) * N + xs) * 2 + starts[xs])
            for yy in range(N - 1)
            for xs in range(N)
        ]
        last = jnp.where(spots[0] == N - 1, tails[0], tails[1])
        below = lax.ppermute(last, ("y", "x", "c"), moves)
        return jnp.stack(
            [jnp.where(spots[0] == 0, below, beside), jnp.where(spots[1] == 0, below, tails[0])]
        )

    first, tails1 = finish((((0, 0), (0, 512)), ((1, 0), (0, 1024))), (piece_a, piece_b))
    second, tails2 = finish((((0, 512), (0, 1024)), ((0, 2048), (0, 1536))), (piece_b,))
    tails12 = halos(jnp.concatenate([tails1, tails2], axis=1))
    state = jax.ShapeDtypeStruct((TILES, modes, width), F32)
    full = jax.ShapeDtypeStruct((width // LANES, length, LANES), F32)
    extended = pltpu.VMEM((TILES, HALO + rows, width), F32)
    source, init, ends = local_call(
        states_kernel,
        (full, jax.ShapeDtypeStruct((modes, SEGMENTS, width), F32), state),
        (),
        (first, second, tails12[:, :HALO], tails12[:, HALO:], taps, rate),
        (),
        [extended, extended, pltpu.VMEM((modes, SEGMENTS, width), F32)],
        1_000_000_000,
        8_000_000,
        "states",
    )
    others = core_swap(ends)
    tile_ends = [ends[0], ends[1], others[0], others[1]]

    def fade(tiles):
        return jnp.exp(-rate * (tiles * float(rows)).astype(F32))

    chip = sum(fade(N - 1 - q) * e for q, e in zip(spots, tile_ends))
    one = later(chip, 1)
    two = later(chip + jnp.exp(-rate * float(N * rows)) * one, 2)
    before = one + jnp.exp(-rate * float(N * rows)) * two

    def incoming(i):
        total = fade(spots[i]) * before
        for q, e in zip(spots, tile_ends):
            gap = spots[i] - 1 - q
            total = total + jnp.where(gap >= 0, fade(jnp.maximum(gap, 0)), 0.0) * e
        return total

    (convolved,) = local_call(
        convolve_kernel,
        (full,),
        (),
        (source, init, rate, mode_weight, skip, jnp.stack([incoming(0), incoming(1)])),
        (),
        [],
        1_000_000_000,
        8_000_000,
        "convolve",
    )
    gate, tails0 = finish((((0, 0), (0, 512)), ((0, 1536), (0, 1024))), (piece_c,))
    block = jax.ShapeDtypeStruct((rows, width), BF16)
    blocks = local_call(
        gate_kernel,
        (block, block),
        (),
        (gate, halos(tails0), taps, convolved),
        (),
        [extended],
        10_000_000,
        2_000_000,
        "gate",
    )
    steps = ((0, 2), (1, -1))
    placed = []
    for r in range(TILES):
        moves = [(2 * xs + cs, 2 * ((xs + steps[r][cs]) % N) + xs // 2) for xs in range(N) for cs in range(2)]
        placed.append(lax.ppermute(blocks[r], ("x", "c"), moves))
    even = x % 2 == 0
    return jnp.concatenate(
        [jnp.where(even, placed[0], placed[1]), jnp.where(even, placed[1], placed[0])], axis=1
    )


def solution(mesh):
    grid = Mesh(mesh.devices.reshape(N, N, N, 2), ("y", "x", "z", "c"))
    ctx, ch = ("y", "x"), ("z", "c")
    return jax.shard_map(
        on_device,
        mesh=grid,
        in_specs=(
            P(ctx, ch),
            P(ch, None, ctx),
            P(None, None, ch),
            P(None, ch),
            P(None, ch),
            P(ch),
        ),
        out_specs=P(ctx, ch),
        check_vma=False,
    )
```

time: 198 us -> 201 us (1.015)
  Pallas kernels: 34.8 us -> 49.9 us
  waiting for transfers between devices: 70.9 us -> 84.8 us
  local copies, waits for them, and re-layouts: 16.3 us -> 4.54 us
  other arithmetic: 14.9 us -> 3.44 us
  starting transfers between devices: 60.2 us -> 56.2 us
    pallas_call x3 -> x12, Pallas kernels: 8.43 us -> 49.9 us  [local_call(): pl.pallas_call(kernel, out_shape=shapes, in_specs=[pl.BlockSpec(memory_sp...]
    pallas_call x3 -> x0, Pallas kernels: 26.3 us -> none  [project(): pl.pallas_call(project_kernel, out_shape=(jax.ShapeDtypeStruct((2 * rows,...]
    ppermute x14 -> x10, starting transfers between devices: 26.2 us -> 7.93 us  [split_ring(): return lax.ppermute(value, (axis, 'c'), up + down)]
    ppermute x2 -> x10, waiting for transfers between devices: 1.61 us -> 18.8 us  [the longest x8 18.1 us: ring(): return lax.ppermute(value, axis, [(i, (i + steps) % N) for i in range(N)])]
    ppermute x15 -> x13, starting transfers between devices: 12.3 us -> 20.2 us  [core_swap(): return lax.ppermute(value, 'c', [(0, 1), (1, 0)])]
    ppermute x2 -> x10, starting transfers between devices: 6.81 us -> 14.3 us  [the longest x8 9.33 us: ring(): return lax.ppermute(value, axis, [(i, (i + steps) % N) for i in range(N)])]
    unnamed x35 -> x30, local copies, waits for them, and re-layouts: 7.46 us -> 1.96 us
    concatenate x4 -> x0, other arithmetic: 4.58 us -> none  [the longest x3 4.4 us: on_device(): own_weights = [jnp.concatenate([low[m], high[m]], axis=0) for m in range(3)]]
  transfers between devices with their start and end apart: 35 -> 37, of which waited for: 16 -> 21; matrix products, arithmetic and copies ran while one was open for 12% -> 3% of each run, Pallas kernels for 15% -> 19%
where the time goes in v2:
time: 201 us; the launch traced here: 200 us
  waiting for transfers between devices  84.8 us (42%)
  starting transfers between devices  56.2 us (28%)
  Pallas kernels  49.9 us (25%)
  local copies, waits for them, and re-layouts  4.54 us (2%)
  other arithmetic  3.44 us (2%)
    ppermute x10, waiting for transfers between devices, split_ring(): return lax.ppermute(value, (axis, 'c'), up + down)  52.8 us
    pallas_call x12, Pallas kernels, local_call(): pl.pallas_call(kernel, out_shape=shapes, in_specs=[pl.BlockSpec(memory_sp...  49.9 us
    ppermute x13, starting transfers between devices, core_swap(): return lax.ppermute(value, 'c', [(0, 1), (1, 0)])  20.2 us
    ppermute x8, waiting for transfers between devices, ring(): return lax.ppermute(value, axis, [(i, (i + steps) % N) for i in range(N)])  18.1 us
    ppermute x8, starting transfers between devices, ring(): return lax.ppermute(value, axis, [(i, (i + steps) % N) for i in range(N)])  9.33 us
    ppermute x10, starting transfers between devices, split_ring(): return lax.ppermute(value, (axis, 'c'), up + down)  7.93 us
    ppermute x2, starting transfers between devices, on_device(): placed.append(lax.ppermute(blocks[r], ('x', 'c'), moves))  7.12 us
    ppermute x2, starting transfers between devices, later(): return lax.ppermute(value, 'y', [(i, i + steps) for i in range(N - steps)])  6.71 us
  transfers between devices with their start and end apart: 37, of which 21 were waited for; matrix products, arithmetic and copies ran while one was open for 3% of the time, Pallas kernels for 19%

profile of v2, /device:TPU:1, one launch (start us, length us, event | category | flops | bytes accessed | tf_op | source)
XLA Modules:
  0.0 199.5 jit_solution(14825003048280378426)
XLA Ops:
  0.0 3.3 %collective-permute-start = (bf16[512,1024]{1,0:T(8,128)(2,1)}, bf16[512,1024]{1,0:T(8,128)(2,1)S(1)}, u32[]{:S(2)}, u32[]{:S(2)}) collective-permute-start(bf16[512,1024]{1,0:T(8,128)(2,1)} %refs_0_.5), channel_id=1, source_target_pairs={{0,24},{8,0},{16,8},{24,16},{1,25},{9,1},{17,9},{25,17},{2,26},{10... | collective-permute-start | bytes 3145736 | tf_op jit(solution)/shard_map/ppermute | solution.py:25
  3.3 2.4 %slice_bitcast_fusion = (bf16[1024,256]{1,0:T(8,128)(2,1)S(1)}, bf16[1024,256]{1,0:T(8,128)(2,1)}, bf16[1024,256]{1,0:T(8,128)(2,1)}) fusion(bf16[3,1024,256]{2,1,0:T(8,128)(2,1)} %bitcast.100), kind=kLoop, calls=%fused_computation.4 | loop fusion | bytes 3145728 | tf_op jit(solution)/shard_map/squeeze | solution.py:338
  5.8 2.7 %collective-permute-start.3 = (bf16[1024,256]{1,0:T(8,128)(2,1)S(1)}, bf16[1024,256]{1,0:T(8,128)(2,1)S(1)}, u32[]{:S(2)}, u32[]{:S(2)}) collective-permute-start(bf16[1024,256]{1,0:T(8,128)(2,1)S(1)} %get-tuple-element.55), channel_id=1, source_target_pairs={{0,96},{32,0},{64,32},{96,64},{1,97},{33,1},{65,33},{97,65},{2,98}... | collective-permute-start | bytes 1572872 | tf_op jit(solution)/shard_map/ppermute | solution.py:25
  8.5 10.3 %collective-permute-done.3.refs_4_.refs_5_ = bf16[1024,256]{1,0:T(8,128)(2,1)S(1)} collective-permute-done((bf16[1024,256]{1,0:T(8,128)(2,1)S(1)}, bf16[1024,256]{1,0:T(8,128)(2,1)S(1)}, u32[]{:S(2)}, u32[]{:S(2)}) %collective-permute-start.3) | collective-permute-done | bytes 524320 | tf_op jit(solution)/shard_map/ppermute | solution.py:25
  18.8 3.2 %collective-permute-done.4.refs_5_.refs_6_ = bf16[1024,256]{1,0:T(8,128)(2,1)S(1)} collective-permute-done((bf16[1024,256]{1,0:T(8,128)(2,1)S(1)}, bf16[1024,256]{1,0:T(8,128)(2,1)S(1)}, u32[]{:S(2)}, u32[]{:S(2)}) %collective-permute-start.4) | collective-permute-done | bytes 524320 | tf_op jit(solution)/shard_map/ppermute | solution.py:25
  22.0 0.4 collective-permute-start.10
  22.6 1.3 collective-permute-start.6
  24.0 1.5 collective-permute-done.refs_1_
  25.5 3.1 %collective-permute-done.1.refs_2_ = bf16[512,1024]{1,0:T(8,128)(2,1)} collective-permute-done((bf16[512,1024]{1,0:T(8,128)(2,1)}, bf16[512,1024]{1,0:T(8,128)(2,1)}, u32[]{:S(2)}, u32[]{:S(2)}) %collective-permute-start.1) | collective-permute-done | bytes 1048608 | tf_op jit(solution)/shard_map/ppermute | solution.py:25
  29.0 4.0 %collective-permute-done.10.refs_6_.refs_7_ = bf16[1024,256]{1,0:T(8,128)(2,1)S(1)} collective-permute-done((bf16[1024,256]{1,0:T(8,128)(2,1)S(1)}, bf16[1024,256]{1,0:T(8,128)(2,1)S(1)}, u32[]{:S(2)}, u32[]{:S(2)}) %collective-permute-start.10) | collective-permute-done | bytes 524320 | tf_op jit(solution)/shard_map/ppermute | solution.py:31
  33.0 8.7 %project.3 = (bf16[768,256]{1,0:T(8,128)(2,1)S(1)}, bf16[768,256]{1,0:T(8,128)(2,1)S(1)}, bf16[1536,256]{1,0:T(8,128)(2,1)S(1)}, bf16[3072,256]{1,0:T(8,128)(2,1)}) custom-call(s32[5]{0:T(128)S(1)} %stack.50.where_ref, bf16[512,1024]{1,0:T(8,128)(2,1)S(1)} %copy-done.7, bf16[512,1024]{1,0:T(8,128)(2,1)S(1)} %collective-permute-done.refs_1_, ...), custom_call_target="tpu_custom_call" | custom-call | flops 3221225472 | bytes 8388608 | tf_op jit(solution)/shard_map/project/pallas_call | solution.py:48
  41.8 5.4 %collective-permute-start.12 = (bf16[768,256]{1,0:T(8,128)(2,1)S(1)}, bf16[768,256]{1,0:T(8,128)(2,1)S(1)}, u32[]{:S(2)}, u32[]{:S(2)}) collective-permute-start(bf16[768,256]{1,0:T(8,128)(2,1)S(1)} %get-tuple-element.33), channel_id=1, source_target_pairs={{0,1},{1,0},{2,3},{3,2},{4,5},{5,4},{6,7},{7,6},{8,9},{9,8},{10,11... | collective-permute-start | bytes 1179656 | tf_op jit(solution)/shard_map/ppermute | solution.py:35
  47.3 0.5 collective-permute-start.11
  47.8 0.7 collective-permute-start.14
  48.6 1.8 collective-permute-start.7
  50.5 9.1 %collective-permute-done.11.refs_10_ = bf16[1024,256]{1,0:T(8,128)(2,1)S(1)} collective-permute-done((bf16[1024,256]{1,0:T(8,128)(2,1)S(1)}, bf16[1024,256]{1,0:T(8,128)(2,1)S(1)}, u32[]{:S(2)}, u32[]{:S(2)}) %collective-permute-start.11) | collective-permute-done | bytes 524320 | tf_op jit(solution)/shard_map/ppermute | solution.py:31
  59.6 12.8 %project.4 = (bf16[1280,256]{1,0:T(8,128)(2,1)S(1)}, bf16[1280,256]{1,0:T(8,128)(2,1)S(1)}, bf16[2560,256]{1,0:T(8,128)(2,1)}, bf16[5120,256]{1,0:T(8,128)(2,1)}) custom-call(s32[5]{0:T(128)S(1)} %stack.50.where_ref, bf16[512,1024]{1,0:T(8,128)(2,1)S(1)} %copy-done.7, bf16[512,1024]{1,0:T(8,128)(2,1)} %copy-done.6, ...), custom_call_target="tpu_custom_call" | custom-call | flops 5368709120 | bytes 13631488 | tf_op jit(solution)/shard_map/project/pallas_call | solution.py:48
  72.4 1.3 collective-permute-start.13
  73.7 3.8 %collective-permute-start.15 = (bf16[768,256]{1,0:T(8,128)(2,1)S(1)}, bf16[768,256]{1,0:T(8,128)(2,1)S(1)}, u32[]{:S(2)}, u32[]{:S(2)}) collective-permute-start(bf16[768,256]{1,0:T(8,128)(2,1)S(1)} %add_convert_fusion.2.refs_11_), channel_id=1, source_target_pairs={{0,2},{2,4},{4,6},{6,0},{1,7},{3,1},{5,3},{7,5},{8,10},{10,12},{12... | collective-permute-start | bytes 1179656 | tf_op jit(solution)/shard_map/ppermute | solution.py:31
  77.6 4.6 %collective-permute-done.15.arrived_ref = bf16[768,256]{1,0:T(8,128)(2,1)S(1)} collective-permute-done((bf16[768,256]{1,0:T(8,128)(2,1)S(1)}, bf16[768,256]{1,0:T(8,128)(2,1)S(1)}, u32[]{:S(2)}, u32[]{:S(2)}) %collective-permute-start.15) | collective-permute-done | bytes 393248 | tf_op jit(solution)/shard_map/ppermute | solution.py:31
  82.2 0.8 near.3.refs_9_
  83.0 0.4 copy-done.3
  83.6 2.3 %collective-permute-done.9.refs_7_ = bf16[1024,256]{1,0:T(8,128)(2,1)S(1)} collective-permute-done((bf16[1024,256]{1,0:T(8,128)(2,1)S(1)}, bf16[1024,256]{1,0:T(8,128)(2,1)S(1)}, u32[]{:S(2)}, u32[]{:S(2)}) %collective-permute-start.9) | collective-permute-done | bytes 524320 | tf_op jit(solution)/shard_map/ppermute | solution.py:31
  85.9 10.9 %project.5 = (bf16[1024,256]{1,0:T(8,128)(2,1)S(1)}, bf16[1024,256]{1,0:T(8,128)(2,1)S(1)}, bf16[2048,256]{1,0:T(8,128)(2,1)S(1)}, bf16[4096,256]{1,0:T(8,128)(2,1)}) custom-call(s32[5]{0:T(128)S(1)} %stack.50.where_ref, bf16[512,1024]{1,0:T(8,128)(2,1)S(1)} %copy-done.7, bf16[512,1024]{1,0:T(8,128)(2,1)} %copy-done.6, ...), custom_call_target="tpu_custom_call" | custom-call | flops 4294967296 | bytes 10485760 | tf_op jit(solution)/shard_map/project/pallas_call | solution.py:48
  96.8 2.6 %collective-permute-start.16 = (bf16[4096,256]{1,0:T(8,128)(2,1)}, bf16[4096,256]{1,0:T(8,128)(2,1)S(1)}, u32[]{:S(2)}, u32[]{:S(2)}) collective-permute-start(bf16[4096,256]{1,0:T(8,128)(2,1)} %get-tuple-element.38.refs_0_), channel_id=1, source_target_pairs={{0,1},{1,0},{2,3},{3,2},{4,5},{5,4},{6,7},{7,6},{8,9},{9,8},{10,11... | collective-permute-start | bytes 6291464 | tf_op jit(solution)/shard_map/ppermute | solution.py:35
  99.7 4.2 %collective-permute-done.17 = bf16[1024,256]{1,0:T(8,128)(2,1)S(1)} collective-permute-done((bf16[1024,256]{1,0:T(8,128)(2,1)S(1)}, bf16[1024,256]{1,0:T(8,128)(2,1)S(1)}, u32[]{:S(2)}, u32[]{:S(2)}) %collective-permute-start.17) | collective-permute-done | bytes 524320 | tf_op jit(solution)/shard_map/ppermute | solution.py:35
  104.0 0.4 collective-permute-start.18
  104.4 4.9 %collective-permute-done.27.arrived_ref = bf16[1280,256]{1,0:T(8,128)(2,1)S(1)} collective-permute-done((bf16[1280,256]{1,0:T(8,128)(2,1)S(1)}, bf16[1280,256]{1,0:T(8,128)(2,1)S(1)}, u32[]{:S(2)}, u32[]{:S(2)}) %collective-permute-start.27) | collective-permute-done | bytes 655392 | tf_op jit(solution)/shard_map/ppermute | solution.py:31
  109.3 0.9 near.5
  110.2 0.6 copy-done
  110.8 1.0 collective-permute-start.28
  111.8 3.1 %collective-permute-done.18.arrived_ref = bf16[1024,256]{1,0:T(8,128)(2,1)S(1)} collective-permute-done((bf16[1024,256]{1,0:T(8,128)(2,1)S(1)}, bf16[1024,256]{1,0:T(8,128)(2,1)S(1)}, u32[]{:S(2)}, u32[]{:S(2)}) %collective-permute-start.18) | collective-permute-done | bytes 524320 | tf_op jit(solution)/shard_map/ppermute | solution.py:31
  115.0 0.8 near.4
  115.8 0.5 copy-done.2
  116.3 1.0 collective-permute-start.19
  117.6 11.4 %collective-permute-done.28.refs_6_.refs_2_ = bf16[2560,256]{1,0:T(8,128)(2,1)} collective-permute-done((bf16[2560,256]{1,0:T(8,128)(2,1)S(1)}, bf16[2560,256]{1,0:T(8,128)(2,1)}, u32[]{:S(2)}, u32[]{:S(2)}) %collective-permute-start.28) | collective-permute-done | bytes 1310752 | tf_op jit(solution)/shard_map/ppermute | solution.py:31
  129.1 3.1 %collective-permute-start.29 = (bf16[2560,256]{1,0:T(8,128)(2,1)}, bf16[2560,256]{1,0:T(8,128)(2,1)S(1)}, u32[]{:S(2)}, u32[]{:S(2)}) collective-permute-start(bf16[2560,256]{1,0:T(8,128)(2,1)} %collective-permute-done.28.refs_6_.refs_2_), channel_id=1, source_target_pairs={{0,1},{1,0},{2,3},{3,2},{4,5},{5,4},{6,7},{7,6},{8,9},{9,8},{10,11... | collective-permute-start | bytes 3932168 | tf_op jit(solution)/shard_map/ppermute | solution.py:35
  132.2 8.1 %collective-permute-done.19.refs_2_ = bf16[2048,256]{1,0:T(8,128)(2,1)} collective-permute-done((bf16[2048,256]{1,0:T(8,128)(2,1)S(1)}, bf16[2048,256]{1,0:T(8,128)(2,1)}, u32[]{:S(2)}, u32[]{:S(2)}) %collective-permute-start.19) | collective-permute-done | bytes 1048608 | tf_op jit(solution)/shard_map/ppermute | solution.py:31
  140.3 3.1 %collective-permute-start.20 = (bf16[2048,256]{1,0:T(8,128)(2,1)}, bf16[2048,256]{1,0:T(8,128)(2,1)}, u32[]{:S(2)}, u32[]{:S(2)}) collective-permute-start(bf16[2048,256]{1,0:T(8,128)(2,1)} %collective-permute-done.19.refs_2_), channel_id=1, source_target_pairs={{0,1},{1,0},{2,3},{3,2},{4,5},{5,4},{6,7},{7,6},{8,9},{9,8},{10,11... | collective-permute-start | bytes 3145736 | tf_op jit(solution)/shard_map/ppermute | solution.py:35
  143.4 5.3 %collective-permute-done.24.refs_2_ = bf16[1536,256]{1,0:T(8,128)(2,1)} collective-permute-done((bf16[1536,256]{1,0:T(8,128)(2,1)S(1)}, bf16[1536,256]{1,0:T(8,128)(2,1)}, u32[]{:S(2)}, u32[]{:S(2)}) %collective-permute-start.24) | collective-permute-done | bytes 786464 | tf_op jit(solution)/shard_map/ppermute | solution.py:31
  148.7 3.1 %collective-permute-start.25 = (bf16[1536,256]{1,0:T(8,128)(2,1)}, bf16[1536,256]{1,0:T(8,128)(2,1)}, u32[]{:S(2)}, u32[]{:S(2)}) collective-permute-start(bf16[1536,256]{1,0:T(8,128)(2,1)} %collective-permute-done.24.refs_2_), channel_id=1, source_target_pairs={{0,1},{1,0},{2,3},{3,2},{4,5},{5,4},{6,7},{7,6},{8,9},{9,8},{10,11... | collective-permute-start | bytes 2359304 | tf_op jit(solution)/shard_map/ppermute | solution.py:35
  152.0 0.8 fusion.2
  153.0 0.4 copy-done.10
  153.4 0.8 collective-permute-done.23
  154.2 0.8 broadcast_select_fusion.6
  155.1 2.1 %final.3 = (bf16[1024,256]{1,0:T(8,128)(2,1)S(1)}, f32[2,8,256]{2,1,0:T(8,128)S(1)}) custom-call(s32[5]{0:T(128)S(1)} %stack.50.where_ref, bf16[4096,256]{1,0:T(8,128)(2,1)S(1)} %copy-done.4, bf16[4096,256]{1,0:T(8,128)(2,1)} %copy-done.2, bf16[2048,256]{1,0:T(8,128)(2,1)} %collective-permute-done.19.refs_2_, bf16[2048,256]{1,0:T(8,128)(2,1)} %collective-permute-done.20.refs_3_), custom_call_target="tpu_custom_call" | custom-call | flops 1048576 | bytes 2621440 | tf_op jit(solution)/shard_map/final/pallas_call | solution.py:48
  157.3 2.4 %final.4 = (bf16[1024,256]{1,0:T(8,128)(2,1)S(1)}, f32[2,8,256]{2,1,0:T(8,128)S(1)}) custom-call(s32[5]{0:T(128)S(1)} %stack.50.where_ref, bf16[3072,256]{1,0:T(8,128)(2,1)} %get-tuple-element.37.refs_0_, bf16[3072,256]{1,0:T(8,128)(2,1)} %copy-done.3, bf16[1536,256]{1,0:T(8,128)(2,1)} %collective-permute-done.24.refs_2_, ...), custom_call_target="tpu_custom_call" | custom-call | flops 1048576 | bytes 2621440 | tf_op jit(solution)/shard_map/final/pallas_call | solution.py:48
  159.7 2.0 final.5
  161.7 1.3 collective-permute-start.30
  163.2 0.7 collective-permute-done.30
  163.9 0.4 collective-permute-done.31
  164.3 3.9 %states.1 = (f32[2,1024,128]{2,1,0:T(8,128)S(1)}, f32[16,8,256]{2,1,0:T(8,128)S(1)}, f32[2,16,256]{2,1,0:T(8,128)S(1)}) custom-call(bf16[1024,256]{1,0:T(8,128)(2,1)S(1)} %get-tuple-element.46.first_ref, bf16[1024,256]{1,0:T(8,128)(2,1)S(1)} %get-tuple-element.47.second_ref, f32[2,8,256]{2,1,0:T(8,128)S(1)} %get-tuple-element.63.halo1_ref, ...), custom_call_target="tpu_custom_call" | custom-call | flops 1000000000 | bytes 8000000 | tf_op jit(solution)/shard_map/states/pallas_call | solution.py:48
  168.4 3.7 %collective-permute-start.21 = (f32[8,256]{1,0:T(8,128)S(1)}, f32[8,256]{1,0:T(8,128)S(1)}, u32[]{:S(2)}, u32[]{:S(2)}) collective-permute-start(f32[8,256]{1,0:T(8,128)S(1)} %bitcast_select_fusion.1), channel_id=1, source_target_pairs={{1,32},{9,41},{16,49},{24,56},{33,64},{41,73},{48,81},{56,88},{65,... | collective-permute-start | bytes 24584 | tf_op jit(solution)/shard_map/ppermute | solution.py:419
  172.2 1.4 collective-permute-start.33
  173.7 0.8 collective-permute-done.33
  174.5 5.3 %collective-permute-start.34 = (f32[16,256]{1,0:T(8,128)S(1)}, f32[16,256]{1,0:T(8,128)S(1)}, u32[]{:S(2)}, u32[]{:S(2)}) collective-permute-start(f32[16,256]{1,0:T(8,128)S(1)} %multiply_add_fusion.1), channel_id=1, source_target_pairs={{0,64},{32,96},{1,65},{33,97},{2,66},{34,98},{3,67},{35,99},{4,68}... | collective-permute-start | bytes 49160 | tf_op jit(solution)/shard_map/ppermute | solution.py:39
  179.9 0.8 collective-permute-done.34
  180.8 3.5 %convolve.1.conv_ref = f32[2,1024,128]{2,1,0:T(8,128)S(1)} custom-call(f32[2,1024,128]{2,1,0:T(8,128)S(1)} %get-tuple-element.50.source_ref, f32[16,8,256]{2,1,0:T(8,128)S(1)} %get-tuple-element.51.init_ref, f32[16,256]{1,0:T(8,128)S(1)} %slice_multiply_fusion.1.rate_ref, f32[16,256]{1,0:T(8,128)S(1)} %get-tuple-element.61.weight_ref, ...), custom_call_target="tpu_custom_call" | custom-call | flops 1000000000 | bytes 8000000 | tf_op jit(solution)/shard_map/convolve/pallas_call | solution.py:48
  184.3 1.1 gate.1
  185.4 5.4 %collective-permute-start.35 = (bf16[512,256]{1,0:T(8,128)(2,1)S(1)}, bf16[512,256]{1,0:T(8,128)(2,1)S(1)}, u32[]{:S(2)}, u32[]{:S(2)}) collective-permute-start(bf16[512,256]{1,0:T(8,128)(2,1)S(1)} %get-tuple-element.53), channel_id=1, source_target_pairs={{0,0},{1,16},{8,8},{9,24},{16,17},{17,1},{24,25},{25,9},{2,2},{3,1... | collective-permute-start | bytes 786440 | tf_op jit(solution)/shard_map/ppermute | solution.py:487
  190.8 1.7 collective-permute-start.36
  192.5 2.5 %collective-permute-done.35 = bf16[512,256]{1,0:T(8,128)(2,1)S(1)} collective-permute-done((bf16[512,256]{1,0:T(8,128)(2,1)S(1)}, bf16[512,256]{1,0:T(8,128)(2,1)S(1)}, u32[]{:S(2)}, u32[]{:S(2)}) %collective-permute-start.35) | collective-permute-done | bytes 262176 | tf_op jit(solution)/shard_map/ppermute | solution.py:487
  195.0 3.7 %collective-permute-done.36 = bf16[512,256]{1,0:T(8,128)(2,1)S(1)} collective-permute-done((bf16[512,256]{1,0:T(8,128)(2,1)S(1)}, bf16[512,256]{1,0:T(8,128)(2,1)S(1)}, u32[]{:S(2)}, u32[]{:S(2)}) %collective-permute-start.36) | collective-permute-done | bytes 262176 | tf_op jit(solution)/shard_map/ppermute | solution.py:487
  198.7 0.8 pad_maximum_fusion
  (84 shorter events, 2.8 us)
Async XLA Ops:
  0.0 25.5 %collective-permute-start = (bf16[512,1024]{1,0:T(8,128)(2,1)}, bf16[512,1024]{1,0:T(8,128)(2,1)S(1)}, u32[]{:S(2)}, u32[]{:S(2)}) collective-permute-start(bf16[512,1024]{1,0:T(8,128)(2,1)} %refs_0_.5), channel_id=1, source_target_pairs={{0,24},{8,0},{16,8},{24,16},{1,25},{9,1},{17,9},{25,17},{2,26},{10... | collective-permute-start | bytes 3145736 | tf_op jit(solution)/shard_map/ppermute | solution.py:25
  3.3 25.2 %collective-permute-start.1 = (bf16[512,1024]{1,0:T(8,128)(2,1)}, bf16[512,1024]{1,0:T(8,128)(2,1)}, u32[]{:S(2)}, u32[]{:S(2)}) collective-permute-start(bf16[512,1024]{1,0:T(8,128)(2,1)} %refs_0_.5), channel_id=1, source_target_pairs={{0,8},{8,16},{16,24},{24,0},{1,9},{9,17},{17,25},{25,1},{2,10},{10... | collective-permute-start | bytes 3145736 | tf_op jit(solution)/shard_map/ppermute | solution.py:25
  5.8 13.0 %collective-permute-start.3 = (bf16[1024,256]{1,0:T(8,128)(2,1)S(1)}, bf16[1024,256]{1,0:T(8,128)(2,1)S(1)}, u32[]{:S(2)}, u32[]{:S(2)}) collective-permute-start(bf16[1024,256]{1,0:T(8,128)(2,1)S(1)} %get-tuple-element.55), channel_id=1, source_target_pairs={{0,96},{32,0},{64,32},{96,64},{1,97},{33,1},{65,33},{97,65},{2,98}... | collective-permute-start | bytes 1572872 | tf_op jit(solution)/shard_map/ppermute | solution.py:25
  8.5 13.5 %collective-permute-start.4 = (bf16[1024,256]{1,0:T(8,128)(2,1)S(1)}, bf16[1024,256]{1,0:T(8,128)(2,1)S(1)}, u32[]{:S(2)}, u32[]{:S(2)}) collective-permute-start(bf16[1024,256]{1,0:T(8,128)(2,1)S(1)} %get-tuple-element.55), channel_id=1, source_target_pairs={{0,32},{32,64},{64,96},{96,0},{1,33},{33,65},{65,97},{97,1},{2,34}... | collective-permute-start | bytes 1572872 | tf_op jit(solution)/shard_map/ppermute | solution.py:25
  22.0 11.0 %collective-permute-start.10 = (bf16[1024,256]{1,0:T(8,128)(2,1)S(1)}, bf16[1024,256]{1,0:T(8,128)(2,1)S(1)}, u32[]{:S(2)}, u32[]{:S(2)}) collective-permute-start(bf16[1024,256]{1,0:T(8,128)(2,1)S(1)} %broadcast_select_fusion.2), channel_id=1, source_target_pairs={{0,32},{32,64},{64,96},{96,0},{1,97},{33,1},{65,33},{97,65},{2,34}... | collective-permute-start | bytes 1572872 | tf_op jit(solution)/shard_map/ppermute | solution.py:31
  22.5 10.5 %copy-start.7 = (bf16[512,1024]{1,0:T(8,128)(2,1)S(1)}, bf16[512,1024]{1,0:T(8,128)(2,1)}, u32[]{:S(2)}) copy-start(bf16[512,1024]{1,0:T(8,128)(2,1)} %refs_0_.5) | copy-start | bytes 3145732
  22.5 24.7 %collective-permute-start.5 = (bf16[1024,256]{1,0:T(8,128)(2,1)}, bf16[1024,256]{1,0:T(8,128)(2,1)S(1)}, u32[]{:S(2)}, u32[]{:S(2)}) collective-permute-start(bf16[1024,256]{1,0:T(8,128)(2,1)} %get-tuple-element.30), channel_id=1, source_target_pairs={{0,96},{32,0},{64,32},{96,64},{1,97},{33,1},{65,33},{97,65},{2,98}... | collective-permute-start | bytes 1572872 | tf_op jit(solution)/shard_map/ppermute | solution.py:25
  22.6 24.6 %collective-permute-start.6 = (bf16[1024,256]{1,0:T(8,128)(2,1)}, bf16[1024,256]{1,0:T(8,128)(2,1)S(1)}, u32[]{:S(2)}, u32[]{:S(2)}) collective-permute-start(bf16[1024,256]{1,0:T(8,128)(2,1)} %get-tuple-element.30), channel_id=1, source_target_pairs={{0,32},{32,64},{64,96},{96,0},{1,33},{33,65},{65,97},{97,1},{2,34}... | collective-permute-start | bytes 1572872 | tf_op jit(solution)/shard_map/ppermute | solution.py:25
  25.5 7.6 %copy-start.6 = (bf16[512,1024]{1,0:T(8,128)(2,1)}, bf16[512,1024]{1,0:T(8,128)(2,1)S(1)}, u32[]{:S(2)}) copy-start(bf16[512,1024]{1,0:T(8,128)(2,1)S(1)} %collective-permute-done.refs_1_) | copy-start | bytes 3145732
  28.7 30.9 %collective-permute-start.2 = (bf16[512,1024]{1,0:T(8,128)(2,1)S(1)}, bf16[512,1024]{1,0:T(8,128)(2,1)}, u32[]{:S(2)}, u32[]{:S(2)}) collective-permute-start(bf16[512,1024]{1,0:T(8,128)(2,1)S(1)} %broadcast_select_fusion), channel_id=1, source_target_pairs={{0,8},{8,16},{16,24},{24,0},{1,25},{9,1},{17,9},{25,17},{2,10},{10... | collective-permute-start | bytes 3145736 | tf_op jit(solution)/shard_map/ppermute | solution.py:31
  33.0 15.5 %copy-start.9 = (bf16[1024,256]{1,0:T(8,128)(2,1)S(1)}, bf16[1024,256]{1,0:T(8,128)(2,1)}, u32[]{:S(2)}) copy-start(bf16[1024,256]{1,0:T(8,128)(2,1)} %get-tuple-element.31) | copy-start | bytes 1572868
  41.8 6.1 %copy-start.8 = (bf16[3072,256]{1,0:T(8,128)(2,1)S(1)}, bf16[3072,256]{1,0:T(8,128)(2,1)}, u32[]{:S(2)}) copy-start(bf16[3072,256]{1,0:T(8,128)(2,1)} %get-tuple-element.37.refs_0_) | copy-start | bytes 4718596
  41.8 8.6 %collective-permute-start.12 = (bf16[768,256]{1,0:T(8,128)(2,1)S(1)}, bf16[768,256]{1,0:T(8,128)(2,1)S(1)}, u32[]{:S(2)}, u32[]{:S(2)}) collective-permute-start(bf16[768,256]{1,0:T(8,128)(2,1)S(1)} %get-tuple-element.33), channel_id=1, source_target_pairs={{0,1},{1,0},{2,3},{3,2},{4,5},{5,4},{6,7},{7,6},{8,9},{9,8},{10,11... | collective-permute-start | bytes 1179656 | tf_op jit(solution)/shard_map/ppermute | solution.py:35
  47.3 12.3 %collective-permute-start.11 = (bf16[1024,256]{1,0:T(8,128)(2,1)S(1)}, bf16[1024,256]{1,0:T(8,128)(2,1)S(1)}, u32[]{:S(2)}, u32[]{:S(2)}) collective-permute-start(bf16[1024,256]{1,0:T(8,128)(2,1)S(1)} %broadcast_select_fusion.1), channel_id=1, source_target_pairs={{0,32},{32,64},{64,96},{96,0},{1,97},{33,1},{65,33},{97,65},{2,34}... | collective-permute-start | bytes 1572872 | tf_op jit(solution)/shard_map/ppermute | solution.py:31
  47.8 34.3 %collective-permute-start.14 = (bf16[3072,256]{1,0:T(8,128)(2,1)S(1)}, bf16[3072,256]{1,0:T(8,128)(2,1)S(1)}, u32[]{:S(2)}, u32[]{:S(2)}) collective-permute-start(bf16[3072,256]{1,0:T(8,128)(2,1)S(1)} %copy-done.8), channel_id=1, source_target_pairs={{0,1},{1,0},{2,3},{3,2},{4,5},{5,4},{6,7},{7,6},{8,9},{9,8},{10,11... | collective-permute-start | bytes 4718600 | tf_op jit(solution)/shard_map/ppermute | solution.py:35
  48.6 28.9 %collective-permute-start.7 = (bf16[1024,256]{1,0:T(8,128)(2,1)S(1)}, bf16[1024,256]{1,0:T(8,128)(2,1)S(1)}, u32[]{:S(2)}, u32[]{:S(2)}) collective-permute-start(bf16[1024,256]{1,0:T(8,128)(2,1)S(1)} %copy-done.9), channel_id=1, source_target_pairs={{0,96},{32,0},{64,32},{96,64},{1,97},{33,1},{65,33},{97,65},{2,98}... | collective-permute-start | bytes 1572872 | tf_op jit(solution)/shard_map/ppermute | solution.py:25
  50.4 27.1 %collective-permute-start.8 = (bf16[1024,256]{1,0:T(8,128)(2,1)S(1)}, bf16[1024,256]{1,0:T(8,128)(2,1)S(1)}, u32[]{:S(2)}, u32[]{:S(2)}) collective-permute-start(bf16[1024,256]{1,0:T(8,128)(2,1)S(1)} %copy-done.9), channel_id=1, source_target_pairs={{0,32},{32,64},{64,96},{96,0},{1,33},{33,65},{65,97},{97,1},{2,34}... | collective-permute-start | bytes 1572872 | tf_op jit(solution)/shard_map/ppermute | solution.py:25
  72.4 11.0 %collective-permute-start.13 = (bf16[1280,256]{1,0:T(8,128)(2,1)S(1)}, bf16[1280,256]{1,0:T(8,128)(2,1)S(1)}, u32[]{:S(2)}, u32[]{:S(2)}) collective-permute-start(bf16[1280,256]{1,0:T(8,128)(2,1)S(1)} %get-tuple-element.35), channel_id=1, source_target_pairs={{0,1},{1,0},{2,3},{3,2},{4,5},{5,4},{6,7},{7,6},{8,9},{9,8},{10,11... | collective-permute-start | bytes 1966088 | tf_op jit(solution)/shard_map/ppermute | solution.py:35
  73.7 8.5 %collective-permute-start.15 = (bf16[768,256]{1,0:T(8,128)(2,1)S(1)}, bf16[768,256]{1,0:T(8,128)(2,1)S(1)}, u32[]{:S(2)}, u32[]{:S(2)}) collective-permute-start(bf16[768,256]{1,0:T(8,128)(2,1)S(1)} %add_convert_fusion.2.refs_11_), channel_id=1, source_target_pairs={{0,2},{2,4},{4,6},{6,0},{1,7},{3,1},{5,3},{7,5},{8,10},{10,12},{12... | collective-permute-start | bytes 1179656 | tf_op jit(solution)/shard_map/ppermute | solution.py:31
  77.5 31.8 %collective-permute-start.26 = (bf16[5120,256]{1,0:T(8,128)(2,1)}, bf16[5120,256]{1,0:T(8,128)(2,1)S(1)}, u32[]{:S(2)}, u32[]{:S(2)}) collective-permute-start(bf16[5120,256]{1,0:T(8,128)(2,1)} %get-tuple-element.44.refs_4_.refs_0_), channel_id=1, source_target_pairs={{0,1},{1,0},{2,3},{3,2},{4,5},{5,4},{6,7},{7,6},{8,9},{9,8},{10,11... | collective-permute-start | bytes 7864328 | tf_op jit(solution)/shard_map/ppermute | solution.py:35
  77.5 8.4 %collective-permute-start.9 = (bf16[1024,256]{1,0:T(8,128)(2,1)S(1)}, bf16[1024,256]{1,0:T(8,128)(2,1)S(1)}, u32[]{:S(2)}, u32[]{:S(2)}) collective-permute-start(bf16[1024,256]{1,0:T(8,128)(2,1)S(1)} %broadcast_select_fusion.3), channel_id=1, source_target_pairs={{0,32},{32,64},{64,96},{96,0},{1,97},{33,1},{65,33},{97,65},{2,34}... | collective-permute-start | bytes 1572872 | tf_op jit(solution)/shard_map/ppermute | solution.py:31
  82.2 1.2 copy-start.3
  96.8 12.5 %copy-start.5 = (bf16[2560,256]{1,0:T(8,128)(2,1)S(1)}, bf16[2560,256]{1,0:T(8,128)(2,1)}, u32[]{:S(2)}) copy-start(bf16[2560,256]{1,0:T(8,128)(2,1)} %get-tuple-element.45.keep_ref) | copy-start | bytes 3932164
  96.8 18.1 %collective-permute-start.16 = (bf16[4096,256]{1,0:T(8,128)(2,1)}, bf16[4096,256]{1,0:T(8,128)(2,1)S(1)}, u32[]{:S(2)}, u32[]{:S(2)}) collective-permute-start(bf16[4096,256]{1,0:T(8,128)(2,1)} %get-tuple-element.38.refs_0_), channel_id=1, source_target_pairs={{0,1},{1,0},{2,3},{3,2},{4,5},{5,4},{6,7},{7,6},{8,9},{9,8},{10,11... | collective-permute-start | bytes 6291464 | tf_op jit(solution)/shard_map/ppermute | solution.py:35
  99.5 4.4 %collective-permute-start.17 = (bf16[1024,256]{1,0:T(8,128)(2,1)S(1)}, bf16[1024,256]{1,0:T(8,128)(2,1)S(1)}, u32[]{:S(2)}, u32[]{:S(2)}) collective-permute-start(bf16[1024,256]{1,0:T(8,128)(2,1)S(1)} %get-tuple-element.41), channel_id=1, source_target_pairs={{0,1},{1,0},{2,3},{3,2},{4,5},{5,4},{6,7},{7,6},{8,9},{9,8},{10,11... | collective-permute-start | bytes 1572872 | tf_op jit(solution)/shard_map/ppermute | solution.py:35
  99.6 9.7 %collective-permute-start.27 = (bf16[1280,256]{1,0:T(8,128)(2,1)S(1)}, bf16[1280,256]{1,0:T(8,128)(2,1)S(1)}, u32[]{:S(2)}, u32[]{:S(2)}) collective-permute-start(bf16[1280,256]{1,0:T(8,128)(2,1)S(1)} %add_convert_fusion.refs_8_), channel_id=1, source_target_pairs={{0,2},{2,4},{4,6},{6,0},{1,7},{3,1},{5,3},{7,5},{8,10},{10,12},{12... | collective-permute-start | bytes 1966088 | tf_op jit(solution)/shard_map/ppermute | solution.py:31
  104.0 10.9 %collective-permute-start.18 = (bf16[1024,256]{1,0:T(8,128)(2,1)S(1)}, bf16[1024,256]{1,0:T(8,128)(2,1)S(1)}, u32[]{:S(2)}, u32[]{:S(2)}) collective-permute-start(bf16[1024,256]{1,0:T(8,128)(2,1)S(1)} %add_convert_fusion.1), channel_id=1, source_target_pairs={{0,2},{2,4},{4,6},{6,0},{1,7},{3,1},{5,3},{7,5},{8,10},{10,12},{12... | collective-permute-start | bytes 1572872 | tf_op jit(solution)/shard_map/ppermute | solution.py:31
  109.3 1.5 copy-start
  110.8 18.3 %collective-permute-start.28 = (bf16[2560,256]{1,0:T(8,128)(2,1)S(1)}, bf16[2560,256]{1,0:T(8,128)(2,1)}, u32[]{:S(2)}, u32[]{:S(2)}) collective-permute-start(bf16[2560,256]{1,0:T(8,128)(2,1)S(1)} %near.5), channel_id=1, source_target_pairs={{0,2},{2,4},{4,6},{6,0},{1,7},{3,1},{5,3},{7,5},{8,10},{10,12},{12... | collective-permute-start | bytes 3932168 | tf_op jit(solution)/shard_map/ppermute | solution.py:31
  114.9 1.4 copy-start.2
  114.9 37.0 %copy-start.11 = (f32[7,3,512]{2,0,1:T(8,128)S(1)}, f32[7,3,512]{2,0,1:T(8,128)}, u32[]{:S(2)}) copy-start(f32[7,3,512]{2,0,1:T(8,128)} %param.8) | copy-start | bytes 129028
  114.9 37.0 %copy-start.12 = (f32[16,512]{1,0:T(8,128)S(1)}, f32[16,512]{1,0:T(8,128)}, u32[]{:S(2)}) copy-start(f32[16,512]{1,0:T(8,128)} %param.9) | copy-start | bytes 98308
  114.9 37.0 %copy-start.13 = (f32[512]{0:T(512)S(1)}, f32[512]{0:T(512)}, u32[]{:S(2)}) copy-start(f32[512]{0:T(512)} %param.11) | copy-start | bytes 6148
  114.9 40.2 %copy-start.4 = (bf16[4096,256]{1,0:T(8,128)(2,1)S(1)}, bf16[4096,256]{1,0:T(8,128)(2,1)}, u32[]{:S(2)}) copy-start(bf16[4096,256]{1,0:T(8,128)(2,1)} %get-tuple-element.38.refs_0_) | copy-start | bytes 6291460
  116.3 24.0 %collective-permute-start.19 = (bf16[2048,256]{1,0:T(8,128)(2,1)S(1)}, bf16[2048,256]{1,0:T(8,128)(2,1)}, u32[]{:S(2)}, u32[]{:S(2)}) collective-permute-start(bf16[2048,256]{1,0:T(8,128)(2,1)S(1)} %near.4), channel_id=1, source_target_pairs={{0,2},{2,4},{4,6},{6,0},{1,7},{3,1},{5,3},{7,5},{8,10},{10,12},{12... | collective-permute-start | bytes 3145736 | tf_op jit(solution)/shard_map/ppermute | solution.py:31
  117.4 31.4 %collective-permute-start.24 = (bf16[1536,256]{1,0:T(8,128)(2,1)S(1)}, bf16[1536,256]{1,0:T(8,128)(2,1)}, u32[]{:S(2)}, u32[]{:S(2)}) collective-permute-start(bf16[1536,256]{1,0:T(8,128)(2,1)S(1)} %near.3.refs_9_), channel_id=1, source_target_pairs={{0,2},{2,4},{4,6},{6,0},{1,7},{3,1},{5,3},{7,5},{8,10},{10,12},{12... | collective-permute-start | bytes 2359304 | tf_op jit(solution)/shard_map/ppermute | solution.py:31
  129.1 28.2 %collective-permute-start.29 = (bf16[2560,256]{1,0:T(8,128)(2,1)}, bf16[2560,256]{1,0:T(8,128)(2,1)S(1)}, u32[]{:S(2)}, u32[]{:S(2)}) collective-permute-start(bf16[2560,256]{1,0:T(8,128)(2,1)} %collective-permute-done.28.refs_6_.refs_2_), channel_id=1, source_target_pairs={{0,1},{1,0},{2,3},{3,2},{4,5},{5,4},{6,7},{7,6},{8,9},{9,8},{10,11... | collective-permute-start | bytes 3932168 | tf_op jit(solution)/shard_map/ppermute | solution.py:35
  140.3 14.8 %collective-permute-start.20 = (bf16[2048,256]{1,0:T(8,128)(2,1)}, bf16[2048,256]{1,0:T(8,128)(2,1)}, u32[]{:S(2)}, u32[]{:S(2)}) collective-permute-start(bf16[2048,256]{1,0:T(8,128)(2,1)} %collective-permute-done.19.refs_2_), channel_id=1, source_target_pairs={{0,1},{1,0},{2,3},{3,2},{4,5},{5,4},{6,7},{7,6},{8,9},{9,8},{10,11... | collective-permute-start | bytes 3145736 | tf_op jit(solution)/shard_map/ppermute | solution.py:35
  148.7 8.5 %collective-permute-start.25 = (bf16[1536,256]{1,0:T(8,128)(2,1)}, bf16[1536,256]{1,0:T(8,128)(2,1)}, u32[]{:S(2)}, u32[]{:S(2)}) collective-permute-start(bf16[1536,256]{1,0:T(8,128)(2,1)} %collective-permute-done.24.refs_2_), channel_id=1, source_target_pairs={{0,1},{1,0},{2,3},{3,2},{4,5},{5,4},{6,7},{7,6},{8,9},{9,8},{10,11... | collective-permute-start | bytes 2359304 | tf_op jit(solution)/shard_map/ppermute | solution.py:35
  152.8 0.6 copy-start.10
  152.8 1.5 collective-permute-start.23
  157.3 2.4 %copy-start.1 = (bf16[5120,256]{1,0:T(8,128)(2,1)S(1)}, bf16[5120,256]{1,0:T(8,128)(2,1)}, u32[]{:S(2)}) copy-start(bf16[5120,256]{1,0:T(8,128)(2,1)} %get-tuple-element.44.refs_4_.refs_0_) | copy-start | bytes 7864324
  161.7 2.1 %collective-permute-start.30 = (f32[16,256]{1,0:T(8,128)S(1)}, f32[16,256]{1,0:T(8,128)S(1)}, u32[]{:S(2)}, u32[]{:S(2)}) collective-permute-start(f32[16,256]{1,0:T(8,128)S(1)} %fusion.17), channel_id=1, source_target_pairs={{1,32},{9,41},{16,49},{24,56},{33,64},{41,73},{48,81},{56,88},{65,... | collective-permute-start | bytes 49160 | tf_op jit(solution)/shard_map/ppermute | solution.py:419
  163.0 1.3 collective-permute-start.31
  168.2 4.0 %collective-permute-start.32 = (f32[2,16,256]{2,1,0:T(8,128)S(1)}, f32[2,16,256]{2,1,0:T(8,128)S(1)}, u32[]{:S(2)}, u32[]{:S(2)}) collective-permute-start(f32[2,16,256]{2,1,0:T(8,128)S(1)} %get-tuple-element.52), channel_id=1, source_target_pairs={{0,1},{1,0},{2,3},{3,2},{4,5},{5,4},{6,7},{7,6},{8,9},{9,8},{10,11... | collective-permute-start | bytes 98312 | tf_op jit(solution)/shard_map/ppermute | solution.py:35
  168.4 5.2 %collective-permute-start.21 = (f32[8,256]{1,0:T(8,128)S(1)}, f32[8,256]{1,0:T(8,128)S(1)}, u32[]{:S(2)}, u32[]{:S(2)}) collective-permute-start(f32[8,256]{1,0:T(8,128)S(1)} %bitcast_select_fusion.1), channel_id=1, source_target_pairs={{1,32},{9,41},{16,49},{24,56},{33,64},{41,73},{48,81},{56,88},{65,... | collective-permute-start | bytes 24584 | tf_op jit(solution)/shard_map/ppermute | solution.py:419
  172.1 1.5 collective-permute-start.22
  172.2 2.2 %collective-permute-start.33 = (f32[16,256]{1,0:T(8,128)S(1)}, f32[16,256]{1,0:T(8,128)S(1)}, u32[]{:S(2)}, u32[]{:S(2)}) collective-permute-start(f32[16,256]{1,0:T(8,128)S(1)} %fusion.6), channel_id=1, source_target_pairs={{0,32},{32,64},{64,96},{1,33},{33,65},{65,97},{2,34},{34,66},{66,9... | collective-permute-start | bytes 49160 | tf_op jit(solution)/shard_map/ppermute | solution.py:39
  174.5 6.2 %collective-permute-start.34 = (f32[16,256]{1,0:T(8,128)S(1)}, f32[16,256]{1,0:T(8,128)S(1)}, u32[]{:S(2)}, u32[]{:S(2)}) collective-permute-start(f32[16,256]{1,0:T(8,128)S(1)} %multiply_add_fusion.1), channel_id=1, source_target_pairs={{0,64},{32,96},{1,65},{33,97},{2,66},{34,98},{3,67},{35,99},{4,68}... | collective-permute-start | bytes 49160 | tf_op jit(solution)/shard_map/ppermute | solution.py:39
  185.4 9.6 %collective-permute-start.35 = (bf16[512,256]{1,0:T(8,128)(2,1)S(1)}, bf16[512,256]{1,0:T(8,128)(2,1)S(1)}, u32[]{:S(2)}, u32[]{:S(2)}) collective-permute-start(bf16[512,256]{1,0:T(8,128)(2,1)S(1)} %get-tuple-element.53), channel_id=1, source_target_pairs={{0,0},{1,16},{8,8},{9,24},{16,17},{17,1},{24,25},{25,9},{2,2},{3,1... | collective-permute-start | bytes 786440 | tf_op jit(solution)/shard_map/ppermute | solution.py:487
  190.8 7.8 %collective-permute-start.36 = (bf16[512,256]{1,0:T(8,128)(2,1)S(1)}, bf16[512,256]{1,0:T(8,128)(2,1)S(1)}, u32[]{:S(2)}, u32[]{:S(2)}) collective-permute-start(bf16[512,256]{1,0:T(8,128)(2,1)S(1)} %get-tuple-element.54), channel_id=1, source_target_pairs={{0,8},{1,24},{8,16},{9,0},{16,25},{17,9},{24,1},{25,17},{2,10},{3,... | collective-permute-start | bytes 786440 | tf_op jit(solution)/shard_map/ppermute | solution.py:487

commit v3 on v2

v3 whole, which is shorter than its diff:
```python
import functools

import jax
import jax.numpy as jnp
from jax import lax
from jax.experimental import pallas as pl
from jax.experimental.pallas import tpu as pltpu
from jax.sharding import Mesh
from jax.sharding import PartitionSpec as P

SHORT = 7
HALO = 8
SEGMENTS = 8
TILES = 2
LANES = 128
N = 4
F32 = jnp.float32
BF16 = jnp.bfloat16
VMEM_LIMIT = 32 * 1024 * 1024
KEEP, GIVE, SELF, FAR = range(4)
CORE, SPOT0, SPOT1, ROW = range(4, 8)
COST = 1_000


def split_ring(value, axis, reverse=False):
    moves = [
        (2 * i + core, 2 * ((i + (1 if core == reverse else -1)) % N) + core) for i in range(N) for core in range(2)
    ]
    return lax.ppermute(value, (axis, "c"), moves)


def core_swap(value):
    return lax.ppermute(value, "c", [(0, 1), (1, 0)])


def after(value, *others):
    return lax.optimization_barrier((value,) + others)[0]


def local_call(kernel, shapes, scalars, arrays, kept, scratch, name):
    vmem = pl.BlockSpec(memory_space=pltpu.VMEM)
    return pl.pallas_call(
        kernel,
        out_shape=shapes,
        in_specs=[pl.BlockSpec(memory_space=pltpu.SMEM)] * len(scalars)
        + [vmem] * len(arrays)
        + [pl.BlockSpec(memory_space=pl.ANY)] * len(kept),
        out_specs=tuple(vmem for _ in shapes),
        scratch_shapes=scratch,
        compiler_params=pltpu.CompilerParams(vmem_limit_bytes=VMEM_LIMIT),
        cost_estimate=pl.CostEstimate(flops=COST, bytes_accessed=COST, transcendentals=0),
        name=name,
    )(*scalars, *arrays, *kept)


def project_kernel(streams, n_after, where_ref, *refs):
    core = where_ref[CORE]
    tokens = refs[:4]
    all_weights = refs[4]
    blocks = refs[5 : -9 - n_after]
    far_keep, far_give, near_ref, give_ref, w_buf, o_buf, w_sem, o_sem, f_sem = refs[-9:]
    rows = tokens[0].shape[0]
    middle = TILES * len(streams) * rows
    sides = (0, 1 - core, core, 1)
    withins = (0, core, 1 - core, 1)

    def weight_copies(s):
        stream, group, place = streams[s]
        sources = [all_weights.at[stream]] + [block.at[place] for block in blocks[3 * group : 3 * group + 3]]
        return [
            pltpu.make_async_copy(source, w_buf.at[s, where_ref[slot]], w_sem.at[s, slot])
            for slot, source in enumerate(sources)
        ]

    for s in range(len(streams)):
        for copy in weight_copies(s):
            copy.start()
    outgoing = []
    for s in range(len(streams)):
        for copy in weight_copies(s):
            copy.wait()
        for slot in range(4):
            place = pl.multiple_of(s * TILES * rows + withins[slot] * rows, rows)
            at = pl.multiple_of(sides[slot] * middle + place, rows)
            staged = (4 * s + slot) * rows
            for role, target, start in (
                (FAR, None, place),
                (KEEP, near_ref, at),
                (GIVE, give_ref, at),
                (SELF, give_ref, pl.multiple_of(2 * middle + at, rows)),
            ):
                here = o_buf.at[role, pl.ds(staged, rows)]
                here[...] = jnp.dot(tokens[slot][...], w_buf[s, role], preferred_element_type=F32).astype(BF16)
                if target is not None:
                    copy = pltpu.make_async_copy(here, target.at[pl.ds(start, rows)], o_sem.at[4 * s + slot, role])
                    copy.start()
                    outgoing.append(copy)
                    continue

                def far_copy(ref):
                    return pltpu.make_async_copy(here, ref.at[pl.ds(start, rows)], f_sem.at[4 * s + slot])

                if slot == 1:
                    far_copy(far_give).start()
                elif slot == 2:
                    far_copy(far_keep).start()
                else:

                    @pl.when(core == sides[slot])
                    def _():
                        far_copy(far_keep).start()

                    @pl.when(core != sides[slot])
                    def _():
                        far_copy(far_give).start()

                outgoing.append(far_copy(far_keep))
    for copy in outgoing:
        copy.wait()


def project(where, streams, tokens, weights, passed, behind=()):
    rows, depth = tokens[0].shape
    width = weights.shape[2]
    total = 4 * len(streams) * rows
    groups = []
    for m in streams:
        if not any(passed[m][0] is group for group in groups):
            groups.append(passed[m][0])
    held = tuple((m, [passed[m][0] is group for group in groups].index(True), passed[m][1]) for m in streams)
    hbm = pl.BlockSpec(memory_space=pl.ANY)
    operands = [weights] + [block for group in groups for block in group] + list(behind)
    return pl.pallas_call(
        functools.partial(project_kernel, held, len(behind)),
        out_shape=tuple(jax.ShapeDtypeStruct((n, width), BF16) for n in (total // 2, total // 2, total, 2 * total)),
        in_specs=[pl.BlockSpec(memory_space=pltpu.SMEM)]
        + [pl.BlockSpec(memory_space=pltpu.VMEM)] * 4
        + [hbm] * len(operands),
        out_specs=(hbm,) * 4,
        scratch_shapes=[
            pltpu.VMEM((len(streams), 4, depth, width), BF16),
            pltpu.VMEM((4, total, width), BF16),
            pltpu.SemaphoreType.DMA((len(streams), 4)),
            pltpu.SemaphoreType.DMA((4 * len(streams), 3)),
            pltpu.SemaphoreType.DMA((4 * len(streams),)),
        ],
        compiler_params=pltpu.CompilerParams(vmem_limit_bytes=VMEM_LIMIT),
        cost_estimate=pl.CostEstimate(flops=COST, bytes_accessed=COST, transcendentals=0),
        name="project",
    )(where, *tokens, *operands)


def pick_kernel(first, source_ref, out_ref, sem):
    copies = [
        pltpu.make_async_copy(source_ref.at[first + k], out_ref.at[k], sem.at[k]) for k in range(out_ref.shape[0])
    ]
    for copy in copies:
        copy.start()
    for copy in copies:
        copy.wait()


def pick(value, first, count):
    hbm = pl.BlockSpec(memory_space=pl.ANY)
    return pl.pallas_call(
        functools.partial(pick_kernel, first),
        out_shape=jax.ShapeDtypeStruct((count,) + value.shape[1:], value.dtype),
        in_specs=[hbm],
        out_specs=hbm,
        scratch_shapes=[pltpu.SemaphoreType.DMA((count,))],
        cost_estimate=pl.CostEstimate(flops=COST, bytes_accessed=COST, transcendentals=0),
        name="pick",
    )(value)


def near_kernel(where_ref, keep_ref, got_ref, arrived_ref, *refs):
    out_ref = refs[-1]
    total = keep_ref.shape[0]
    half = total // 2
    step = 256
    core = where_ref[CORE]
    with_arrived = pl.multiple_of(core * half, half)
    without = pl.multiple_of((1 - core) * half, half)
    for start in range(0, half, step):
        here = pl.ds(with_arrived + start, step)
        out_ref[here, :] = (
            keep_ref[here, :].astype(F32)
            + got_ref[here, :].astype(F32)
            + arrived_ref[pl.ds(start, step), :].astype(F32)
        ).astype(BF16)
        here = pl.ds(without + start, step)
        out_ref[here, :] = (keep_ref[here, :].astype(F32) + got_ref[here, :].astype(F32)).astype(BF16)


def final_kernel(streams, where_ref, *refs):
    outs = refs[-5 - streams : -5]
    tail0_ref, tail1_ref, last_ref, buf, sem = refs[-5:]
    give, got, reached, crossed = refs[: -5 - streams]
    core = where_ref[CORE]
    rows = buf.shape[2]
    total = reached.shape[0]
    count = streams * TILES

    def copies(number):
        stream, tile = divmod(number, TILES)
        within = tile + core - 2 * tile * core
        row = pl.multiple_of(core * (total // 2) + stream * TILES * rows + within * rows, rows)
        beyond = pl.multiple_of(total + row, rows)
        parts = [give.at[pl.ds(beyond, rows)], got.at[pl.ds(beyond, rows)], reached.at[pl.ds(row, rows)], crossed.at[pl.ds(row, rows)]]
        return [pltpu.make_async_copy(part, buf.at[number, k], sem.at[number, k]) for k, part in enumerate(parts)]

    for number in range(count):
        for copy in copies(number):
            copy.start()
    for number in range(count):
        stream, tile = divmod(number, TILES)
        for copy in copies(number):
            copy.wait()
        value = (
            buf[number, 0].astype(F32)
            + buf[number, 1].astype(F32)
            + buf[number, 2].astype(F32)
            + buf[number, 3].astype(F32)
        ).astype(BF16)
        outs[stream][pl.ds(tile * rows, rows), :] = value
        tail = (tail0_ref, tail1_ref)[tile]
        tail[pl.ds(stream * HALO, HALO), :] = value[rows - 16 :].astype(F32)[16 - HALO :]
    last_ref[...] = jnp.where(where_ref[SPOT0] == N - 1, tail0_ref[...], tail1_ref[...])


def extend(ext, part_ref, where_ref, below_ref, beside_ref, tail_ref, stream):
    rows = part_ref.shape[0] // TILES
    here = pl.ds(stream * HALO, HALO)
    below = below_ref[here, :]
    ext[0, pl.ds(0, HALO), :] = jnp.where(where_ref[SPOT0] == 0, below, beside_ref[here, :])
    ext[1, pl.ds(0, HALO), :] = jnp.where(where_ref[SPOT1] == 0, below, tail_ref[here, :])
    for tile in range(TILES):
        ext[tile, pl.ds(HALO, rows), :] = part_ref[pl.ds(tile * rows, rows), :].astype(F32)


def smooth(ext, tile, taps, start, count):
    total = taps[0][None, :] * ext[tile, pl.ds(HALO + start, count), :]
    for k in range(1, SHORT):
        total = total + taps[k][None, :] * ext[tile, pl.ds(HALO + start - k, count), :]
    return total


def states_kernel(
    where_ref, first_ref, second_ref, below_ref, beside_ref, tail_ref, taps_ref, rate_ref,
    source_ref, init_ref, end_ref, ext1, ext2, ends,
):
    length, width = first_ref.shape
    modes = rate_ref.shape[0]
    rows = length // TILES
    seg = length // SEGMENTS
    extend(ext1, first_ref, where_ref, below_ref, beside_ref, tail_ref, 0)
    extend(ext2, second_ref, where_ref, below_ref, beside_ref, tail_ref, 1)
    taps1 = [taps_ref[k, 1] for k in range(SHORT)]
    taps2 = [taps_ref[k, 2] for k in range(SHORT)]
    step = 64
    for tile in range(TILES):
        for start in range(0, rows, step):
            product = smooth(ext1, tile, taps1, start, step) * smooth(ext2, tile, taps2, start, step)
            for lane in range(0, width, LANES):
                source_ref[lane // LANES, pl.ds(tile * rows + start, step), :] = product[:, lane : lane + LANES]
    for lane in range(0, width, LANES):
        column = source_ref.at[lane // LANES]
        lanes = pl.ds(lane, LANES)
        fade = [jnp.broadcast_to(jnp.exp(-rate_ref[r, lanes])[None, :], (SEGMENTS, LANES)) for r in range(modes)]

        def body(i, states):
            for j in range(4):
                x = column[pl.ds(4 * i + j, SEGMENTS, stride=seg), :]
                states = tuple(f * s + x for f, s in zip(fade, states))
            return states

        zero = jnp.zeros((SEGMENTS, LANES), F32)
        states = lax.fori_loop(0, seg // 4, body, (zero,) * modes)
        for r in range(modes):
            ends[r, :, lanes] = states[r]
    passing = jnp.exp(-rate_ref[...] * float(seg))
    for tile in range(TILES):
        state = jnp.zeros((modes, width), F32)
        for k in range(SEGMENTS // TILES):
            s = tile * (SEGMENTS // TILES) + k
            init_ref[:, s, :] = state
            state = passing * state + ends[:, s, :]
        end_ref[tile] = state


def tile_fade(rate, rows, tiles):
    return jnp.exp(-rate * (float(rows) * jnp.asarray(tiles).astype(F32)))


def convolve_kernel(
    where_ref, source_ref, init_ref, rate_ref, weight_ref, skip_ref,
    ends_ref, others_ref, beside_ref, crossed_ref, second_ref, out_ref, incoming_ref,
):
    modes = rate_ref.shape[0]
    width, length = rate_ref.shape[1], source_ref.shape[1]
    rows = length // TILES
    rate = rate_ref[...]
    row = where_ref[ROW]
    first_core = where_ref[CORE] == 0
    beside, crossed = beside_ref[...], crossed_ref[...]
    before = jnp.where(row >= 1, jnp.where(first_core, beside, crossed), 0.0)
    before = before + jnp.where(row >= 2, tile_fade(rate, rows, N) * second_ref[...], 0.0)
    before = before + jnp.where(row >= 3, tile_fade(rate, rows, 2 * N) * jnp.where(first_core, crossed, beside), 0.0)
    tile_ends = [ends_ref[0], ends_ref[1], others_ref[0], others_ref[1]]
    spots = [lax.rem(where_ref[SPOT0] + i, N) for i in range(N)]
    for i in range(TILES):
        total = tile_fade(rate, rows, spots[i]) * before
        for q, end in zip(spots, tile_ends):
            gap = spots[i] - 1 - q
            total = total + jnp.where(gap >= 0, tile_fade(rate, rows, jnp.maximum(gap, 0)) * end, 0.0)
        incoming_ref[i] = total
    seg = length // SEGMENTS
    per_tile = SEGMENTS // TILES
    number = lax.broadcasted_iota(jnp.int32, (SEGMENTS, LANES), 0)
    is_first = number < per_tile
    index = jnp.where(is_first, number, number - per_tile).astype(F32) * float(seg)
    for lane in range(0, width, LANES):
        lanes = pl.ds(lane, LANES)
        column, result = source_ref.at[lane // LANES], out_ref.at[lane // LANES]

        def spread(row):
            return jnp.broadcast_to(row[None, :], (SEGMENTS, LANES))

        rates = [spread(rate_ref[r, lanes]) for r in range(modes)]
        fade = [jnp.exp(-v) for v in rates]
        weight = [spread(weight_ref[r, lanes]) for r in range(modes)]
        skip = spread(skip_ref[0, lanes])
        states = tuple(
            init_ref[r, :, lanes]
            + jnp.exp(-rates[r] * index)
            * jnp.where(is_first, spread(incoming_ref[0, r, lanes]), spread(incoming_ref[1, r, lanes]))
            for r in range(modes)
        )

        def body(i, states):
            for j in range(4):
                at = pl.ds(4 * i + j, SEGMENTS, stride=seg)
                x = column[at, :]
                states = tuple(f * s + x for f, s in zip(fade, states))
                terms = [w * s for w, s in zip(weight, states)] + [skip * x]
                while len(terms) > 1:
                    terms = [a + b for a, b in zip(terms[::2], terms[1::2])] + ([terms[-1]] if len(terms) % 2 else [])
                result[at, :] = terms[0]
            return states

        lax.fori_loop(0, seg // 4, body, states)


def gate_kernel(where_ref, part_ref, below_ref, beside_ref, tail_ref, taps_ref, conv_ref, first_ref, second_ref, ext):
    length, width = part_ref.shape
    rows = length // TILES
    extend(ext, part_ref, where_ref, below_ref, beside_ref, tail_ref, 0)
    taps = [taps_ref[k, 0] for k in range(SHORT)]
    step = 64
    for tile, out_ref in enumerate((first_ref, second_ref)):
        for start in range(0, rows, step):
            gate = smooth(ext, tile, taps, start, step)
            for lane in range(0, width, LANES):
                lanes = slice(lane, lane + LANES)
                filtered = gate[:, lanes] * conv_ref[lane // LANES, pl.ds(tile * rows + start, step), :]
                out_ref[pl.ds(start, step), lanes] = filtered.astype(BF16)


def on_device(tokens, in_weight, short_taps, residues, decay_scale, skip_gain):
    y, x, z, c = (lax.axis_index(a) for a in ("y", "x", "z", "c"))
    rows, _ = tokens.shape
    width = in_weight.shape[2]
    channels = short_taps.shape[2]
    modes = residues.shape[0]
    seq_total = rows * N * N
    length = TILES * rows
    first_core = c == 0
    weights = jnp.transpose(in_weight, (1, 0, 2))

    def role(row):
        ahead = (row - z) % N
        near = jnp.where(ahead == 1 + 2 * c, KEEP, GIVE)
        return jnp.where(ahead == 0, SELF, jnp.where(ahead == 2, FAR, near))

    side = 1 - 2 * c
    spots = [(x + 2 * c + i) % N for i in range(N)]
    where = jnp.stack([role(y), role(y - side), role(y + side), role(y + 2), c, spots[0], spots[1], y]).astype(jnp.int32)

    packed = jnp.concatenate(
        [short_taps.reshape(SHORT * 3, channels), residues, decay_scale, skip_gain[None]], axis=0
    )
    packed = lax.dynamic_slice_in_dim(packed, (x % 2) * width, width, axis=1)
    packed = jnp.where(c == x // 2, packed, core_swap(packed))
    taps = packed[: SHORT * 3].reshape(SHORT, 3, width)
    rate = packed[SHORT * 3 + modes : SHORT * 3 + 2 * modes] / seq_total
    mode_weight = packed[SHORT * 3 : SHORT * 3 + modes] * jnp.sqrt(-jnp.expm1(-2.0 * rate))
    skip = packed[SHORT * 3 + 2 * modes :]

    def around(value, axis, *waits):
        heard = split_ring(value, axis)
        other = split_ring(value, axis, True)
        passed_on = after(heard, *waits) if waits else heard
        return heard, other, split_ring(passed_on, axis)

    held = (tokens,) + around(tokens, "x")
    pair = around(pick(weights, 1, 2), "y", taps, rate, mode_weight, skip)
    alone = around(pick(after(weights, pair[0], pair[1]), 0, 1), "y")
    passed = {0: (alone, 0), 1: (pair, 0), 2: (pair, 1)}

    def begin(streams, behind=()):
        far_keep, far_give, near, give = project(where, streams, held, weights, passed, behind)
        far = (far_keep.astype(F32) + core_swap(far_give).astype(F32)).astype(BF16)
        return far, near, give, core_swap(after(give, far))

    def middle(far, near, got, behind=()):
        arrived = split_ring(far, "z")
        total = near.shape[0]
        (summed,) = local_call(
            near_kernel,
            (jax.ShapeDtypeStruct(near.shape, BF16),),
            (where,),
            (near, got, arrived),
            behind,
            [],
            "near",
        )
        return summed

    def end(summed, give, got, *waits):
        reached = split_ring(summed, "z")
        return give, got, reached, core_swap(after(reached, *waits) if waits else reached)

    def finish(streams, piece):
        tail = jax.ShapeDtypeStruct((streams * HALO, width), F32)
        count = streams * TILES
        *parts, tail0, tail1, last = local_call(
            functools.partial(final_kernel, streams),
            (jax.ShapeDtypeStruct((length, width), BF16),) * streams + (tail,) * 3,
            (where,),
            (),
            piece,
            [pltpu.VMEM((count, 4, rows, width), BF16), pltpu.SemaphoreType.DMA((count, 4))],
            "final",
        )
        holders = {xs: ((N - 1 - xs) % N) // TILES for xs in range(N)}
        starts = {xs: ((-xs) % N) // TILES for xs in range(N)}
        moves = [
            ((yy * N + xs) * 2 + holders[xs], ((yy + 1) * N + xs) * 2 + starts[xs])
            for yy in range(N - 1)
            for xs in range(N)
        ]
        return parts, (lax.ppermute(last, ("y", "x", "c"), moves), core_swap(tail1), tail0)

    far_ab, near_ab, give_ab, got_ab = begin((1, 2))
    sum_ab = middle(far_ab, near_ab, got_ab, alone[:2])
    far_c, near_c, give_c, got_c = begin((0,), (sum_ab,))
    piece_ab = end(sum_ab, give_ab, got_ab)
    sum_c = middle(far_c, near_c, got_c, (piece_ab[2],))

    (first, second), halo12 = finish(2, piece_ab)
    state = jax.ShapeDtypeStruct((TILES, modes, width), F32)
    full = jax.ShapeDtypeStruct((width // LANES, length, LANES), F32)
    extended = pltpu.VMEM((TILES, HALO + rows, width), F32)
    source, init, ends = local_call(
        states_kernel,
        (full, jax.ShapeDtypeStruct((modes, SEGMENTS, width), F32), state),
        (where,),
        (first, second, *halo12, taps, rate),
        (),
        [extended, extended, pltpu.VMEM((modes, SEGMENTS, width), F32)],
        "states",
    )
    others = core_swap(ends)
    tile_ends = [ends[0], ends[1], others[0], others[1]]
    chip = sum(tile_fade(rate, rows, N - 1 - q) * e for q, e in zip(spots, tile_ends))
    beside = split_ring(chip, "y")
    crossed = core_swap(beside)
    beyond = split_ring(beside, "y")
    (convolved,) = local_call(
        convolve_kernel,
        (full,),
        (where,),
        (source, init, rate, mode_weight, skip, ends, others, beside, crossed, beyond),
        (),
        [pltpu.VMEM((TILES, modes, width), F32)],
        "convolve",
    )
    piece_c = end(sum_c, give_c, got_c, beyond)
    (gate,), halo0 = finish(1, piece_c)
    block = jax.ShapeDtypeStruct((rows, width), BF16)
    blocks = local_call(
        gate_kernel,
        (block, block),
        (where,),
        (gate, *halo0, taps, convolved),
        (),
        [extended],
        "gate",
    )
    steps = ((0, 2), (1, -1))
    placed = []
    for r in range(TILES):
        moves = [(2 * xs + cs, 2 * ((xs + steps[r][cs]) % N) + xs // 2) for xs in range(N) for cs in range(2)]
        placed.append(lax.ppermute(blocks[r], ("x", "c"), moves))
    even = x % 2 == 0
    return jnp.concatenate(
        [jnp.where(even, placed[0], placed[1]), jnp.where(even, placed[1], placed[0])], axis=1
    )


def solution(mesh):
    grid = Mesh(mesh.devices.reshape(N, N, N, 2), ("y", "x", "z", "c"))
    ctx, ch = ("y", "x"), ("z", "c")
    return jax.shard_map(
        on_device,
        mesh=grid,
        in_specs=(
            P(ctx, ch),
            P(ch, None, ctx),
            P(None, None, ch),
            P(None, ch),
            P(None, ch),
            P(ch),
        ),
        out_specs=P(ctx, ch),
        check_vma=False,
    )
```

time: 201 us -> 233 us (1.16)
  Pallas kernels: 49.9 us -> 103 us
  starting transfers between devices: 56.2 us -> 44.7 us
  waiting for transfers between devices: 84.8 us -> 75.7 us
    pallas_call x0 -> x4, Pallas kernels: none -> 84.3 us  [the longest x2 49.9 us: pick(): pl.pallas_call(functools.partial(pick_kernel, first), out_shape=jax.Shape...]
    pallas_call x12 -> x7, Pallas kernels: 49.9 us -> 18.5 us  [local_call(): pl.pallas_call(kernel, out_shape=shapes, in_specs=[pl.BlockSpec(memory_sp...]
    ppermute x13 -> x11, starting transfers between devices: 20.2 us -> 6.29 us  [core_swap(): return lax.ppermute(value, 'c', [(0, 1), (1, 0)])]
    ppermute x22 -> x17, waiting for transfers between devices: 73.2 us -> 60.5 us  [the longest x15 59.7 us: split_ring(): return lax.ppermute(value, (axis, 'c'), moves)]
    ppermute x22 -> x17, starting transfers between devices: 28.9 us -> 33.4 us  [the longest x15 29.7 us: split_ring(): return lax.ppermute(value, (axis, 'c'), moves)]
    unnamed x30 -> x25, local copies, waits for them, and re-layouts: 1.96 us -> 6.34 us
    squeeze x3 -> x0, local copies, waits for them, and re-layouts: 2.45 us -> none  [the longest x1 2.44 us: on_device(): passed[1] = around(weights[1], 'y')]
    ppermute x13 -> x11, waiting for transfers between devices: 5.46 us -> 7.78 us  [core_swap(): return lax.ppermute(value, 'c', [(0, 1), (1, 0)])]
  transfers between devices with their start and end apart: 37 -> 30, of which waited for: 21 -> 18; matrix products, arithmetic and copies ran while one was open for 3% -> 1% of each run, Pallas kernels for 19% -> 19%
where the time goes in v3:
time: 233 us
  Pallas kernels  103 us (44%)
  waiting for transfers between devices  75.7 us (32%)
  starting transfers between devices  44.7 us (19%)
  local copies, waits for them, and re-layouts  6.47 us (3%)
  other arithmetic  2.47 us (1%)
    ppermute x15, waiting for transfers between devices, split_ring(): return lax.ppermute(value, (axis, 'c'), moves)  59.7 us
    pallas_call x2, Pallas kernels, pick(): pl.pallas_call(functools.partial(pick_kernel, first), out_shape=jax.Shape...  49.9 us
    pallas_call x2, Pallas kernels, project(): pl.pallas_call(functools.partial(project_kernel, held, len(behind)), out_...  34.4 us
    ppermute x15, starting transfers between devices, split_ring(): return lax.ppermute(value, (axis, 'c'), moves)  29.7 us
    pallas_call x7, Pallas kernels, local_call(): pl.pallas_call(kernel, out_shape=shapes, in_specs=[pl.BlockSpec(memory_sp...  18.5 us
    ppermute x11, waiting for transfers between devices, core_swap(): return lax.ppermute(value, 'c', [(0, 1), (1, 0)])  7.78 us
    ppermute x2, waiting for transfers between devices, on_device(): placed.append(lax.ppermute(blocks[r], ('x', 'c'), moves))  7.46 us
    unnamed x25, local copies, waits for them, and re-layouts  6.34 us
  transfers between devices with their start and end apart: 30, of which 18 were waited for; matrix products, arithmetic and copies ran while one was open for 1% of the time, Pallas kernels for 19%

profile of v3, /device:TPU:1, one launch (start us, length us, event | category | flops | bytes accessed | tf_op | source)
XLA Modules:
  0.0 232.5 jit_solution(12522814888145749422)
XLA Ops:
  0.0 32.9 %pick.2 = bf16[2,1024,256]{2,1,0:T(8,128)(2,1)} custom-call(bf16[3,1024,256]{2,1,0:T(8,128)(2,1)} %bitcast.34), custom_call_target="tpu_custom_call" | custom-call | flops 1000 | bytes 1000 | tf_op jit(solution)/shard_map/pick/pallas_call | solution.py:165
  32.9 3.6 %collective-permute-start.3 = (bf16[2,1024,256]{2,1,0:T(8,128)(2,1)}, bf16[2,1024,256]{2,1,0:T(8,128)(2,1)}, u32[]{:S(2)}, u32[]{:S(2)}) collective-permute-start(bf16[2,1024,256]{2,1,0:T(8,128)(2,1)} %pick.2), channel_id=1, source_target_pairs={{0,32},{1,97},{32,64},{33,1},{64,96},{65,33},{96,0},{97,65},{2,34}... | collective-permute-start | bytes 3145736 | tf_op jit(solution)/shard_map/ppermute | solution.py:29
  36.6 2.5 %collective-permute-start = (bf16[512,1024]{1,0:T(8,128)(2,1)S(1)}, bf16[512,1024]{1,0:T(8,128)(2,1)}, u32[]{:S(2)}, u32[]{:S(2)}) collective-permute-start(bf16[512,1024]{1,0:T(8,128)(2,1)S(1)} %copy-done.2), channel_id=1, source_target_pairs={{0,8},{1,25},{8,16},{9,1},{16,24},{17,9},{24,0},{25,17},{2,10},{3,... | collective-permute-start | bytes 3145736 | tf_op jit(solution)/shard_map/ppermute | solution.py:29
  39.0 0.8 copy.8
  39.9 0.1 fusion.2
  40.0 0.1 collective-permute-start.8
  40.2 0.9 collective-permute-start.4
  41.1 0.2 collective-permute-done.8
  41.4 12.5 %collective-permute-done.3.refs_5_ = bf16[2,1024,256]{2,1,0:T(8,128)(2,1)} collective-permute-done((bf16[2,1024,256]{2,1,0:T(8,128)(2,1)}, bf16[2,1024,256]{2,1,0:T(8,128)(2,1)}, u32[]{:S(2)}, u32[]{:S(2)}) %collective-permute-start.3) | collective-permute-done | bytes 1048608 | tf_op jit(solution)/shard_map/ppermute | solution.py:29
  54.0 5.4 %collective-permute-done.refs_1_ = bf16[512,1024]{1,0:T(8,128)(2,1)} collective-permute-done((bf16[512,1024]{1,0:T(8,128)(2,1)S(1)}, bf16[512,1024]{1,0:T(8,128)(2,1)}, u32[]{:S(2)}, u32[]{:S(2)}) %collective-permute-start) | collective-permute-done | bytes 1048608 | tf_op jit(solution)/shard_map/ppermute | solution.py:29
  59.4 3.5 %collective-permute-start.2 = (bf16[512,1024]{1,0:T(8,128)(2,1)}, bf16[512,1024]{1,0:T(8,128)(2,1)}, u32[]{:S(2)}, u32[]{:S(2)}) collective-permute-start(bf16[512,1024]{1,0:T(8,128)(2,1)} %collective-permute-done.refs_1_), channel_id=1, source_target_pairs={{0,8},{1,25},{8,16},{9,1},{16,24},{17,9},{24,0},{25,17},{2,10},{3,... | collective-permute-start | bytes 3145736 | tf_op jit(solution)/shard_map/ppermute | solution.py:29
  62.9 0.5 collective-permute-start.9
  63.4 11.5 %collective-permute-done.2.refs_3_ = bf16[512,1024]{1,0:T(8,128)(2,1)} collective-permute-done((bf16[512,1024]{1,0:T(8,128)(2,1)}, bf16[512,1024]{1,0:T(8,128)(2,1)}, u32[]{:S(2)}, u32[]{:S(2)}) %collective-permute-start.2) | collective-permute-done | bytes 1048608 | tf_op jit(solution)/shard_map/ppermute | solution.py:29
  74.9 2.2 collective-permute-done.9.refs_7_
  77.1 20.6 %project.2 = (bf16[2048,256]{1,0:T(8,128)(2,1)S(1)}, bf16[2048,256]{1,0:T(8,128)(2,1)S(1)}, bf16[4096,256]{1,0:T(8,128)(2,1)S(1)}, bf16[8192,256]{1,0:T(8,128)(2,1)}) custom-call(s32[8]{0:T(128)S(1)} %stack.35.where_ref, bf16[512,1024]{1,0:T(8,128)(2,1)S(1)} %copy-done.2, bf16[512,1024]{1,0:T(8,128)(2,1)} %collective-permute-done.refs_1_, ...), custom_call_target="tpu_custom_call" | custom-call | flops 1000 | bytes 1000 | tf_op jit(solution)/shard_map/project/pallas_call | solution.py:133
  97.8 1.3 copy-done.5
  99.1 0.4 collective-permute-start.10
  99.5 2.3 collective-permute-done.10
  101.8 1.3 add_convert_fusion
  103.1 0.4 collective-permute-start.11
  103.4 3.8 %collective-permute-start.12 = (bf16[2048,256]{1,0:T(8,128)(2,1)}, bf16[2048,256]{1,0:T(8,128)(2,1)S(1)}, u32[]{:S(2)}, u32[]{:S(2)}) collective-permute-start(bf16[2048,256]{1,0:T(8,128)(2,1)} %add_convert_fusion), channel_id=1, source_target_pairs={{0,2},{1,7},{2,4},{3,1},{4,6},{5,3},{6,0},{7,5},{8,10},{9,15},{10,... | collective-permute-start | bytes 3145736 | tf_op jit(solution)/shard_map/ppermute | solution.py:29
  107.2 17.0 %pick.3 = bf16[1,1024,256]{2,1,0:T(8,128)(2,1)} custom-call(bf16[3,1024,256]{2,1,0:T(8,128)(2,1)} %bitcast.35), custom_call_target="tpu_custom_call" | custom-call | flops 1000 | bytes 1000 | tf_op jit(solution)/shard_map/pick/pallas_call | solution.py:165
  124.2 1.2 collective-permute-start.5
  125.4 0.3 collective-permute-start.6
  125.7 12.4 %collective-permute-done.5.refs_0_.refs_5_ = bf16[1,1024,256]{2,1,0:T(8,128)(2,1)S(1)} collective-permute-done((bf16[1,1024,256]{2,1,0:T(8,128)(2,1)}, bf16[1,1024,256]{2,1,0:T(8,128)(2,1)S(1)}, u32[]{:S(2)}, u32[]{:S(2)}) %collective-permute-start.5) | collective-permute-done | bytes 524320 | tf_op jit(solution)/shard_map/ppermute | solution.py:29
  138.1 1.6 copy-done.6
  139.7 2.9 %near.2.refs_8_ = bf16[4096,256]{1,0:T(8,128)(2,1)S(1)} custom-call(s32[8]{0:T(128)S(1)} %stack.35.where_ref, bf16[4096,256]{1,0:T(8,128)(2,1)S(1)} %copy-done.6, bf16[8192,256]{1,0:T(8,128)(2,1)} %collective-permute-done.11.got_ref.refs_1_, bf16[2048,256]{1,0:T(8,128)(2,1)S(1)} %collective-permute-done.12.arrived_ref, ...), custom_call_target="tpu_custom_call" | custom-call | flops 1000 | bytes 1000 | tf_op jit(solution)/shard_map/near/pallas_call | solution.py:42
  142.6 1.9 collective-permute-start.16
  144.5 0.5 collective-permute-start.7
  145.0 7.9 %collective-permute-done.7.refs_7_ = bf16[1,1024,256]{2,1,0:T(8,128)(2,1)S(1)} collective-permute-done((bf16[1,1024,256]{2,1,0:T(8,128)(2,1)S(1)}, bf16[1,1024,256]{2,1,0:T(8,128)(2,1)S(1)}, u32[]{:S(2)}, u32[]{:S(2)}) %collective-permute-start.7) | collective-permute-done | bytes 524320 | tf_op jit(solution)/shard_map/ppermute | solution.py:29
  152.9 13.8 %project.3 = (bf16[1024,256]{1,0:T(8,128)(2,1)S(1)}, bf16[1024,256]{1,0:T(8,128)(2,1)S(1)}, bf16[2048,256]{1,0:T(8,128)(2,1)S(1)}, bf16[4096,256]{1,0:T(8,128)(2,1)S(1)}) custom-call(s32[8]{0:T(128)S(1)} %stack.35.where_ref, bf16[512,1024]{1,0:T(8,128)(2,1)S(1)} %copy-done.2, bf16[512,1024]{1,0:T(8,128)(2,1)} %collective-permute-done.refs_1_, ...), custom_call_target="tpu_custom_call" | custom-call | flops 1000 | bytes 1000 | tf_op jit(solution)/shard_map/project/pallas_call | solution.py:133
  166.7 1.5 collective-permute-start.13
  168.2 1.5 collective-permute-done.13
  169.7 0.1 add_convert_fusion.1
  169.9 0.5 collective-permute-start.14
  170.3 0.3 collective-permute-start.18
  170.7 2.3 collective-permute-start.15
  172.9 6.1 %collective-permute-done.15.arrived_ref = bf16[1024,256]{1,0:T(8,128)(2,1)S(1)} collective-permute-done((bf16[1024,256]{1,0:T(8,128)(2,1)S(1)}, bf16[1024,256]{1,0:T(8,128)(2,1)S(1)}, u32[]{:S(2)}, u32[]{:S(2)}) %collective-permute-start.15) | collective-permute-done | bytes 524320 | tf_op jit(solution)/shard_map/ppermute | solution.py:29
  179.1 1.8 near.3
  180.9 3.1 %collective-permute-start.17 = (bf16[2048,256]{1,0:T(8,128)(2,1)}, bf16[2048,256]{1,0:T(8,128)(2,1)S(1)}, u32[]{:S(2)}, u32[]{:S(2)}) collective-permute-start(bf16[2048,256]{1,0:T(8,128)(2,1)} %near.3), channel_id=1, source_target_pairs={{0,2},{1,7},{2,4},{3,1},{4,6},{5,3},{6,0},{7,5},{8,10},{9,15},{10,... | collective-permute-start | bytes 3145736 | tf_op jit(solution)/shard_map/ppermute | solution.py:29
  184.0 2.5 %final.2 = (bf16[1024,256]{1,0:T(8,128)(2,1)S(1)}, bf16[1024,256]{1,0:T(8,128)(2,1)S(1)}, f32[16,256]{1,0:T(8,128)S(1)}, f32[16,256]{1,0:T(8,128)S(1)}, f32[16,256]{1,0:T(8,128)S(1)}) custom-call(s32[8]{0:T(128)S(1)} %stack.35.where_ref, bf16[8192,256]{1,0:T(8,128)(2,1)} %get-tuple-element.38.refs_0_, ...), custom_call_target="tpu_custom_call" | custom-call | flops 1000 | bytes 1000 | tf_op jit(solution)/shard_map/final/pallas_call | solution.py:42
  186.5 2.1 collective-permute-start.19
  188.6 0.1 collective-permute-start.20
  188.6 0.8 collective-permute-done.19.below_ref
  189.4 0.4 collective-permute-done.20.beside_ref
  189.8 4.4 %states.1 = (f32[2,1024,128]{2,1,0:T(8,128)S(1)}, f32[16,8,256]{2,1,0:T(8,128)S(1)}, f32[2,16,256]{2,1,0:T(8,128)S(1)}) custom-call(s32[8]{0:T(128)S(1)} %stack.35.where_ref, bf16[1024,256]{1,0:T(8,128)(2,1)S(1)} %get-tuple-element.44.first_ref, bf16[1024,256]{1,0:T(8,128)(2,1)S(1)} %get-tuple-element.45.second_ref, ...), custom_call_target="tpu_custom_call" | custom-call | flops 1000 | bytes 1000 | tf_op jit(solution)/shard_map/states/pallas_call | solution.py:42
  194.2 1.0 copy-done.7
  195.2 0.2 collective-permute-start.21
  195.4 1.0 collective-permute-done.21.others_ref
  196.4 2.7 %collective-permute-start.22 = (f32[16,256]{1,0:T(8,128)S(1)}, f32[16,256]{1,0:T(8,128)S(1)}, u32[]{:S(2)}, u32[]{:S(2)}) collective-permute-start(f32[16,256]{1,0:T(8,128)S(1)} %fusion.4), channel_id=1, source_target_pairs={{0,32},{1,97},{32,64},{33,1},{64,96},{65,33},{96,0},{97,65},{2,34}... | collective-permute-start | bytes 49160 | tf_op jit(solution)/shard_map/ppermute | solution.py:29
  199.1 0.9 collective-permute-done.22.beside_ref
  200.0 2.9 %collective-permute-start.23 = (f32[16,256]{1,0:T(8,128)S(1)}, f32[16,256]{1,0:T(8,128)S(1)}, u32[]{:S(2)}, u32[]{:S(2)}) collective-permute-start(f32[16,256]{1,0:T(8,128)S(1)} %collective-permute-done.22.beside_ref), channel_id=1, source_target_pairs={{0,32},{1,97},{32,64},{33,1},{64,96},{65,33},{96,0},{97,65},{2,34}... | collective-permute-start | bytes 49160 | tf_op jit(solution)/shard_map/ppermute | solution.py:29
  202.9 0.9 collective-permute-done.23.second_ref
  203.8 2.8 %collective-permute-start.24 = (bf16[2048,256]{1,0:T(8,128)(2,1)S(1)}, bf16[2048,256]{1,0:T(8,128)(2,1)S(1)}, u32[]{:S(2)}, u32[]{:S(2)}) collective-permute-start(bf16[2048,256]{1,0:T(8,128)(2,1)S(1)} %collective-permute-done.17.refs_2_), channel_id=1, source_target_pairs={{0,1},{1,0},{2,3},{3,2},{4,5},{5,4},{6,7},{7,6},{8,9},{9,8},{10,11... | collective-permute-start | bytes 3145736 | tf_op jit(solution)/shard_map/ppermute | solution.py:33
  206.6 2.3 collective-permute-done.24.refs_3_
  208.9 1.6 copy-done.4
  210.5 1.2 final.3
  211.6 1.6 collective-permute-start.25
  213.3 4.2 %convolve.1.conv_ref = f32[2,1024,128]{2,1,0:T(8,128)S(1)} custom-call(s32[8]{0:T(128)S(1)} %stack.35.where_ref, f32[2,1024,128]{2,1,0:T(8,128)S(1)} %copy-done.8, f32[16,8,256]{2,1,0:T(8,128)S(1)} %get-tuple-element.56.init_ref, f32[16,256]{1,0:T(8,128)S(1)} %get-tuple-element.62.rate_ref, f32[16,256]{1,0:T(8,128)S(1)} %get-tuple-element.61.weight_ref, ...), custom_call_target="tpu_custom_call" | custom-call | flops 1000 | bytes 1000 | tf_op jit(solution)/shard_map/convolve/pallas_call | solution.py:42
  217.5 1.6 gate.1
  219.1 5.0 %collective-permute-start.28 = (bf16[512,256]{1,0:T(8,128)(2,1)S(1)}, bf16[512,256]{1,0:T(8,128)(2,1)S(1)}, u32[]{:S(2)}, u32[]{:S(2)}) collective-permute-start(bf16[512,256]{1,0:T(8,128)(2,1)S(1)} %get-tuple-element.57), channel_id=1, source_target_pairs={{0,0},{1,16},{8,8},{9,24},{16,17},{17,1},{24,25},{25,9},{2,2},{3,1... | collective-permute-start | bytes 786440 | tf_op jit(solution)/shard_map/ppermute | solution.py:504
  224.2 5.1 %collective-permute-done.28 = bf16[512,256]{1,0:T(8,128)(2,1)S(1)} collective-permute-done((bf16[512,256]{1,0:T(8,128)(2,1)S(1)}, bf16[512,256]{1,0:T(8,128)(2,1)S(1)}, u32[]{:S(2)}, u32[]{:S(2)}) %collective-permute-start.28) | collective-permute-done | bytes 262176 | tf_op jit(solution)/shard_map/ppermute | solution.py:504
  229.3 2.3 %collective-permute-done.29 = bf16[512,256]{1,0:T(8,128)(2,1)S(1)} collective-permute-done((bf16[512,256]{1,0:T(8,128)(2,1)S(1)}, bf16[512,256]{1,0:T(8,128)(2,1)S(1)}, u32[]{:S(2)}, u32[]{:S(2)}) %collective-permute-start.29) | collective-permute-done | bytes 262176 | tf_op jit(solution)/shard_map/ppermute | solution.py:504
  231.7 0.8 pad_maximum_fusion
  (45 shorter events, 0.5 us)
Async XLA Ops:
  0.0 77.1 %copy-start = (bf16[1024,3,256]{2,0,1:T(8,128)(2,1)S(1)}, bf16[1024,3,256]{2,0,1:T(8,128)(2,1)}, u32[]{:S(2)}) copy-start(bf16[1024,3,256]{2,0,1:T(8,128)(2,1)} %param.7) | copy-start | bytes 4718596
  0.0 36.6 %copy-start.2 = (bf16[512,1024]{1,0:T(8,128)(2,1)S(1)}, bf16[512,1024]{1,0:T(8,128)(2,1)}, u32[]{:S(2)}) copy-start(bf16[512,1024]{1,0:T(8,128)(2,1)} %refs_0_.3) | copy-start | bytes 3145732
  0.0 39.9 %copy-start.9 = (f32[16,512]{1,0:T(8,128)S(1)}, f32[16,512]{1,0:T(8,128)}, u32[]{:S(2)}) copy-start(f32[16,512]{1,0:T(8,128)} %param.9) | copy-start | bytes 98308
  0.0 39.9 %copy-start.10 = (f32[16,512]{1,0:T(8,128)S(1)}, f32[16,512]{1,0:T(8,128)}, u32[]{:S(2)}) copy-start(f32[16,512]{1,0:T(8,128)} %param.10) | copy-start | bytes 98308
  0.0 39.9 %copy-start.11 = (f32[512]{0:T(512)S(1)}, f32[512]{0:T(512)}, u32[]{:S(2)}) copy-start(f32[512]{0:T(512)} %param.11) | copy-start | bytes 6148
  32.9 21.0 %collective-permute-start.3 = (bf16[2,1024,256]{2,1,0:T(8,128)(2,1)}, bf16[2,1024,256]{2,1,0:T(8,128)(2,1)}, u32[]{:S(2)}, u32[]{:S(2)}) collective-permute-start(bf16[2,1024,256]{2,1,0:T(8,128)(2,1)} %pick.2), channel_id=1, source_target_pairs={{0,32},{1,97},{32,64},{33,1},{64,96},{65,33},{96,0},{97,65},{2,34}... | collective-permute-start | bytes 3145736 | tf_op jit(solution)/shard_map/ppermute | solution.py:29
  36.6 22.8 %collective-permute-start = (bf16[512,1024]{1,0:T(8,128)(2,1)S(1)}, bf16[512,1024]{1,0:T(8,128)(2,1)}, u32[]{:S(2)}, u32[]{:S(2)}) collective-permute-start(bf16[512,1024]{1,0:T(8,128)(2,1)S(1)} %copy-done.2), channel_id=1, source_target_pairs={{0,8},{1,25},{8,16},{9,1},{16,24},{17,9},{24,0},{25,17},{2,10},{3,... | collective-permute-start | bytes 3145736 | tf_op jit(solution)/shard_map/ppermute | solution.py:29
  40.0 1.3 collective-permute-start.8
  40.1 23.3 %collective-permute-start.1 = (bf16[512,1024]{1,0:T(8,128)(2,1)S(1)}, bf16[512,1024]{1,0:T(8,128)(2,1)}, u32[]{:S(2)}, u32[]{:S(2)}) collective-permute-start(bf16[512,1024]{1,0:T(8,128)(2,1)S(1)} %copy-done.2), channel_id=1, source_target_pairs={{0,24},{1,9},{8,0},{9,17},{16,8},{17,25},{24,16},{25,1},{2,26},{3,... | collective-permute-start | bytes 3145736 | tf_op jit(solution)/shard_map/ppermute | solution.py:29
  40.2 23.2 %collective-permute-start.4 = (bf16[2,1024,256]{2,1,0:T(8,128)(2,1)}, bf16[2,1024,256]{2,1,0:T(8,128)(2,1)}, u32[]{:S(2)}, u32[]{:S(2)}) collective-permute-start(bf16[2,1024,256]{2,1,0:T(8,128)(2,1)} %pick.2), channel_id=1, source_target_pairs={{0,96},{1,33},{32,0},{33,65},{64,32},{65,97},{96,64},{97,1},{2,98}... | collective-permute-start | bytes 3145736 | tf_op jit(solution)/shard_map/ppermute | solution.py:29
  59.4 15.6 %collective-permute-start.2 = (bf16[512,1024]{1,0:T(8,128)(2,1)}, bf16[512,1024]{1,0:T(8,128)(2,1)}, u32[]{:S(2)}, u32[]{:S(2)}) collective-permute-start(bf16[512,1024]{1,0:T(8,128)(2,1)} %collective-permute-done.refs_1_), channel_id=1, source_target_pairs={{0,8},{1,25},{8,16},{9,1},{16,24},{17,9},{24,0},{25,17},{2,10},{3,... | collective-permute-start | bytes 3145736 | tf_op jit(solution)/shard_map/ppermute | solution.py:29
  62.9 14.2 %collective-permute-start.9 = (bf16[2,1024,256]{2,1,0:T(8,128)(2,1)}, bf16[2,1024,256]{2,1,0:T(8,128)(2,1)}, u32[]{:S(2)}, u32[]{:S(2)}) collective-permute-start(bf16[2,1024,256]{2,1,0:T(8,128)(2,1)} %collective-permute-done.3.refs_5_), channel_id=1, source_target_pairs={{0,32},{1,97},{32,64},{33,1},{64,96},{65,33},{96,0},{97,65},{2,34}... | collective-permute-start | bytes 3145736 | tf_op jit(solution)/shard_map/ppermute | solution.py:29
  97.7 1.3 copy-start.5
  99.1 2.7 %collective-permute-start.10 = (bf16[2048,256]{1,0:T(8,128)(2,1)S(1)}, bf16[2048,256]{1,0:T(8,128)(2,1)S(1)}, u32[]{:S(2)}, u32[]{:S(2)}) collective-permute-start(bf16[2048,256]{1,0:T(8,128)(2,1)S(1)} %get-tuple-element.37), channel_id=1, source_target_pairs={{0,1},{1,0},{2,3},{3,2},{4,5},{5,4},{6,7},{7,6},{8,9},{9,8},{10,11... | collective-permute-start | bytes 3145736 | tf_op jit(solution)/shard_map/ppermute | solution.py:33
  103.1 35.0 %collective-permute-start.11 = (bf16[8192,256]{1,0:T(8,128)(2,1)}, bf16[8192,256]{1,0:T(8,128)(2,1)}, u32[]{:S(2)}, u32[]{:S(2)}) collective-permute-start(bf16[8192,256]{1,0:T(8,128)(2,1)} %get-tuple-element.38.refs_0_), channel_id=1, source_target_pairs={{0,1},{1,0},{2,3},{3,2},{4,5},{5,4},{6,7},{7,6},{8,9},{9,8},{10,11... | collective-permute-start | bytes 12582920 | tf_op jit(solution)/shard_map/ppermute | solution.py:33
  103.4 34.7 %collective-permute-start.12 = (bf16[2048,256]{1,0:T(8,128)(2,1)}, bf16[2048,256]{1,0:T(8,128)(2,1)S(1)}, u32[]{:S(2)}, u32[]{:S(2)}) collective-permute-start(bf16[2048,256]{1,0:T(8,128)(2,1)} %add_convert_fusion), channel_id=1, source_target_pairs={{0,2},{1,7},{2,4},{3,1},{4,6},{5,3},{6,0},{7,5},{8,10},{9,15},{10,... | collective-permute-start | bytes 3145736 | tf_op jit(solution)/shard_map/ppermute | solution.py:29
  124.2 13.9 %collective-permute-start.5 = (bf16[1,1024,256]{2,1,0:T(8,128)(2,1)}, bf16[1,1024,256]{2,1,0:T(8,128)(2,1)S(1)}, u32[]{:S(2)}, u32[]{:S(2)}) collective-permute-start(bf16[1,1024,256]{2,1,0:T(8,128)(2,1)} %pick.3), channel_id=1, source_target_pairs={{0,32},{1,97},{32,64},{33,1},{64,96},{65,33},{96,0},{97,65},{2,34}... | collective-permute-start | bytes 1572872 | tf_op jit(solution)/shard_map/ppermute | solution.py:29
  125.4 12.7 %collective-permute-start.6 = (bf16[1,1024,256]{2,1,0:T(8,128)(2,1)}, bf16[1,1024,256]{2,1,0:T(8,128)(2,1)S(1)}, u32[]{:S(2)}, u32[]{:S(2)}) collective-permute-start(bf16[1,1024,256]{2,1,0:T(8,128)(2,1)} %pick.3), channel_id=1, source_target_pairs={{0,96},{1,33},{32,0},{33,65},{64,32},{65,97},{96,64},{97,1},{2,98}... | collective-permute-start | bytes 1572872 | tf_op jit(solution)/shard_map/ppermute | solution.py:29
  138.1 1.6 copy-start.6
  139.7 13.2 %copy-start.1 = (bf16[1024,3,256]{2,0,1:T(8,128)(2,1)S(1)}, bf16[1024,3,256]{2,0,1:T(8,128)(2,1)}, u32[]{:S(2)}) copy-start(bf16[1024,3,256]{2,0,1:T(8,128)(2,1)} %param.7) | copy-start | bytes 4718596
  142.6 27.7 %collective-permute-start.16 = (bf16[4096,256]{1,0:T(8,128)(2,1)S(1)}, bf16[4096,256]{1,0:T(8,128)(2,1)S(1)}, u32[]{:S(2)}, u32[]{:S(2)}) collective-permute-start(bf16[4096,256]{1,0:T(8,128)(2,1)S(1)} %near.2.refs_8_), channel_id=1, source_target_pairs={{0,2},{1,7},{2,4},{3,1},{4,6},{5,3},{6,0},{7,5},{8,10},{9,15},{10,... | collective-permute-start | bytes 6291464 | tf_op jit(solution)/shard_map/ppermute | solution.py:29
  144.5 8.3 %collective-permute-start.7 = (bf16[1,1024,256]{2,1,0:T(8,128)(2,1)S(1)}, bf16[1,1024,256]{2,1,0:T(8,128)(2,1)S(1)}, u32[]{:S(2)}, u32[]{:S(2)}) collective-permute-start(bf16[1,1024,256]{2,1,0:T(8,128)(2,1)S(1)} %collective-permute-done.5.refs_0_.refs_5_), channel_id=1, source_target_pairs={{0,32},{1,97},{32,64},{33,1},{64,96},{65,33},{96,0},{97,65},{2,34}... | collective-permute-start | bytes 1572872 | tf_op jit(solution)/shard_map/ppermute | solution.py:29
  166.7 14.2 %copy-start.3 = (bf16[4096,256]{1,0:T(8,128)(2,1)}, bf16[4096,256]{1,0:T(8,128)(2,1)S(1)}, u32[]{:S(2)}) copy-start(bf16[4096,256]{1,0:T(8,128)(2,1)S(1)} %get-tuple-element.42.refs_0_) | copy-start | bytes 6291460
  166.7 3.1 %collective-permute-start.13 = (bf16[1024,256]{1,0:T(8,128)(2,1)S(1)}, bf16[1024,256]{1,0:T(8,128)(2,1)S(1)}, u32[]{:S(2)}, u32[]{:S(2)}) collective-permute-start(bf16[1024,256]{1,0:T(8,128)(2,1)S(1)} %get-tuple-element.41), channel_id=1, source_target_pairs={{0,1},{1,0},{2,3},{3,2},{4,5},{5,4},{6,7},{7,6},{8,9},{9,8},{10,11... | collective-permute-start | bytes 1572872 | tf_op jit(solution)/shard_map/ppermute | solution.py:33
  169.9 9.2 %collective-permute-start.14 = (bf16[4096,256]{1,0:T(8,128)(2,1)S(1)}, bf16[4096,256]{1,0:T(8,128)(2,1)S(1)}, u32[]{:S(2)}, u32[]{:S(2)}) collective-permute-start(bf16[4096,256]{1,0:T(8,128)(2,1)S(1)} %get-tuple-element.42.refs_0_), channel_id=1, source_target_pairs={{0,1},{1,0},{2,3},{3,2},{4,5},{5,4},{6,7},{7,6},{8,9},{9,8},{10,11... | collective-permute-start | bytes 6291464 | tf_op jit(solution)/shard_map/ppermute | solution.py:33
  170.3 13.7 %collective-permute-start.18 = (bf16[4096,256]{1,0:T(8,128)(2,1)S(1)}, bf16[4096,256]{1,0:T(8,128)(2,1)S(1)}, u32[]{:S(2)}, u32[]{:S(2)}) collective-permute-start(bf16[4096,256]{1,0:T(8,128)(2,1)S(1)} %collective-permute-done.16.refs_0_.refs_2_), channel_id=1, source_target_pairs={{0,1},{1,0},{2,3},{3,2},{4,5},{5,4},{6,7},{7,6},{8,9},{9,8},{10,11... | collective-permute-start | bytes 6291464 | tf_op jit(solution)/shard_map/ppermute | solution.py:33
  170.7 8.4 %collective-permute-start.15 = (bf16[1024,256]{1,0:T(8,128)(2,1)S(1)}, bf16[1024,256]{1,0:T(8,128)(2,1)S(1)}, u32[]{:S(2)}, u32[]{:S(2)}) collective-permute-start(bf16[1024,256]{1,0:T(8,128)(2,1)S(1)} %add_convert_fusion.1), channel_id=1, source_target_pairs={{0,2},{1,7},{2,4},{3,1},{4,6},{5,3},{6,0},{7,5},{8,10},{9,15},{10,... | collective-permute-start | bytes 1572872 | tf_op jit(solution)/shard_map/ppermute | solution.py:29
  180.9 22.1 %collective-permute-start.17 = (bf16[2048,256]{1,0:T(8,128)(2,1)}, bf16[2048,256]{1,0:T(8,128)(2,1)S(1)}, u32[]{:S(2)}, u32[]{:S(2)}) collective-permute-start(bf16[2048,256]{1,0:T(8,128)(2,1)} %near.3), channel_id=1, source_target_pairs={{0,2},{1,7},{2,4},{3,1},{4,6},{5,3},{6,0},{7,5},{8,10},{9,15},{10,... | collective-permute-start | bytes 3145736 | tf_op jit(solution)/shard_map/ppermute | solution.py:29
  186.5 2.9 %collective-permute-start.19 = (f32[16,256]{1,0:T(8,128)S(1)}, f32[16,256]{1,0:T(8,128)S(1)}, u32[]{:S(2)}, u32[]{:S(2)}) collective-permute-start(f32[16,256]{1,0:T(8,128)S(1)} %get-tuple-element.46), channel_id=1, source_target_pairs={{1,32},{9,41},{16,49},{24,56},{33,64},{41,73},{48,81},{56,88},{65,... | collective-permute-start | bytes 49160 | tf_op jit(solution)/shard_map/ppermute | solution.py:452
  188.6 1.3 collective-permute-start.20
  194.2 1.0 copy-start.7
  195.2 1.2 collective-permute-start.21
  196.4 3.6 %collective-permute-start.22 = (f32[16,256]{1,0:T(8,128)S(1)}, f32[16,256]{1,0:T(8,128)S(1)}, u32[]{:S(2)}, u32[]{:S(2)}) collective-permute-start(f32[16,256]{1,0:T(8,128)S(1)} %fusion.4), channel_id=1, source_target_pairs={{0,32},{1,97},{32,64},{33,1},{64,96},{65,33},{96,0},{97,65},{2,34}... | collective-permute-start | bytes 49160 | tf_op jit(solution)/shard_map/ppermute | solution.py:29
  200.0 3.8 %collective-permute-start.23 = (f32[16,256]{1,0:T(8,128)S(1)}, f32[16,256]{1,0:T(8,128)S(1)}, u32[]{:S(2)}, u32[]{:S(2)}) collective-permute-start(f32[16,256]{1,0:T(8,128)S(1)} %collective-permute-done.22.beside_ref), channel_id=1, source_target_pairs={{0,32},{1,97},{32,64},{33,1},{64,96},{65,33},{96,0},{97,65},{2,34}... | collective-permute-start | bytes 49160 | tf_op jit(solution)/shard_map/ppermute | solution.py:29
  203.8 5.1 %collective-permute-start.24 = (bf16[2048,256]{1,0:T(8,128)(2,1)S(1)}, bf16[2048,256]{1,0:T(8,128)(2,1)S(1)}, u32[]{:S(2)}, u32[]{:S(2)}) collective-permute-start(bf16[2048,256]{1,0:T(8,128)(2,1)S(1)} %collective-permute-done.17.refs_2_), channel_id=1, source_target_pairs={{0,1},{1,0},{2,3},{3,2},{4,5},{5,4},{6,7},{7,6},{8,9},{9,8},{10,11... | collective-permute-start | bytes 3145736 | tf_op jit(solution)/shard_map/ppermute | solution.py:33
  206.6 6.7 %collective-permute-start.27 = (f32[16,256]{1,0:T(8,128)S(1)}, f32[16,256]{1,0:T(8,128)S(1)}, u32[]{:S(2)}, u32[]{:S(2)}) collective-permute-start(f32[16,256]{1,0:T(8,128)S(1)} %collective-permute-done.22.beside_ref), channel_id=1, source_target_pairs={{0,1},{1,0},{2,3},{3,2},{4,5},{5,4},{6,7},{7,6},{8,9},{9,8},{10,11... | collective-permute-start | bytes 49160 | tf_op jit(solution)/shard_map/ppermute | solution.py:33
  208.9 1.6 copy-start.4
  210.4 2.9 %copy-start.8 = (f32[2,1024,128]{2,1,0:T(8,128)S(1)}, f32[2,1024,128]{2,1,0:T(8,128)}, u32[]{:S(2)}) copy-start(f32[2,1024,128]{2,1,0:T(8,128)} %copy-done.7) | copy-start | bytes 3145732
  211.6 5.9 %collective-permute-start.25 = (f32[8,256]{1,0:T(8,128)S(1)}, f32[8,256]{1,0:T(8,128)S(1)}, u32[]{:S(2)}, u32[]{:S(2)}) collective-permute-start(f32[8,256]{1,0:T(8,128)S(1)} %get-tuple-element.52), channel_id=1, source_target_pairs={{1,32},{9,41},{16,49},{24,56},{33,64},{41,73},{48,81},{56,88},{65,... | collective-permute-start | bytes 24584 | tf_op jit(solution)/shard_map/ppermute | solution.py:452
  213.2 4.3 %collective-permute-start.26 = (f32[8,256]{1,0:T(8,128)S(1)}, f32[8,256]{1,0:T(8,128)S(1)}, u32[]{:S(2)}, u32[]{:S(2)}) collective-permute-start(f32[8,256]{1,0:T(8,128)S(1)} %get-tuple-element.53), channel_id=1, source_target_pairs={{0,1},{1,0},{2,3},{3,2},{4,5},{5,4},{6,7},{7,6},{8,9},{9,8},{10,11... | collective-permute-start | bytes 24584 | tf_op jit(solution)/shard_map/ppermute | solution.py:33
  219.1 10.2 %collective-permute-start.28 = (bf16[512,256]{1,0:T(8,128)(2,1)S(1)}, bf16[512,256]{1,0:T(8,128)(2,1)S(1)}, u32[]{:S(2)}, u32[]{:S(2)}) collective-permute-start(bf16[512,256]{1,0:T(8,128)(2,1)S(1)} %get-tuple-element.57), channel_id=1, source_target_pairs={{0,0},{1,16},{8,8},{9,24},{16,17},{17,1},{24,25},{25,9},{2,2},{3,1... | collective-permute-start | bytes 786440 | tf_op jit(solution)/shard_map/ppermute | solution.py:504
  224.1 7.6 %collective-permute-start.29 = (bf16[512,256]{1,0:T(8,128)(2,1)S(1)}, bf16[512,256]{1,0:T(8,128)(2,1)S(1)}, u32[]{:S(2)}, u32[]{:S(2)}) collective-permute-start(bf16[512,256]{1,0:T(8,128)(2,1)S(1)} %get-tuple-element.58), channel_id=1, source_target_pairs={{0,8},{1,24},{8,16},{9,0},{16,25},{17,9},{24,1},{25,17},{2,10},{3,... | collective-permute-start | bytes 786440 | tf_op jit(solution)/shard_map/ppermute | solution.py:504

commit v4 on v3

--- a/solution.py
+++ b/solution.py
@@ -16,7 +16,6 @@
 N = 4
 F32 = jnp.float32
 BF16 = jnp.bfloat16
-VMEM_LIMIT = 32 * 1024 * 1024
 KEEP, GIVE, SELF, FAR = range(4)
 CORE, SPOT0, SPOT1, ROW = range(4, 8)
 COST = 1_000
@@ -37,7 +36,7 @@
     return lax.optimization_barrier((value,) + others)[0]
 
 
-def local_call(kernel, shapes, scalars, arrays, kept, scratch, name):
+def local_call(kernel, shapes, scalars, arrays, kept, scratch, name, mebibytes=20):
     vmem = pl.BlockSpec(memory_space=pltpu.VMEM)
     return pl.pallas_call(
         kernel,
@@ -47,7 +46,7 @@
         + [pl.BlockSpec(memory_space=pl.ANY)] * len(kept),
         out_specs=tuple(vmem for _ in shapes),
         scratch_shapes=scratch,
-        compiler_params=pltpu.CompilerParams(vmem_limit_bytes=VMEM_LIMIT),
+        compiler_params=pltpu.CompilerParams(vmem_limit_bytes=mebibytes * 1024 * 1024),
         cost_estimate=pl.CostEstimate(flops=COST, bytes_accessed=COST, transcendentals=0),
         name=name,
     )(*scalars, *arrays, *kept)
@@ -56,121 +55,57 @@
 def project_kernel(streams, n_after, where_ref, *refs):
     core = where_ref[CORE]
     tokens = refs[:4]
-    all_weights = refs[4]
-    blocks = refs[5 : -9 - n_after]
-    far_keep, far_give, near_ref, give_ref, w_buf, o_buf, w_sem, o_sem, f_sem = refs[-9:]
+    blocks = refs[4 : -5 - n_after]
+    far_keep, far_give, near_ref, give_ref, w_buf = refs[-5:]
     rows = tokens[0].shape[0]
     middle = TILES * len(streams) * rows
     sides = (0, 1 - core, core, 1)
     withins = (0, core, 1 - core, 1)
 
-    def weight_copies(s):
-        stream, group, place = streams[s]
-        sources = [all_weights.at[stream]] + [block.at[place] for block in blocks[3 * group : 3 * group + 3]]
-        return [
-            pltpu.make_async_copy(source, w_buf.at[s, where_ref[slot]], w_sem.at[s, slot])
-            for slot, source in enumerate(sources)
-        ]
-
+    for s, (group, places) in enumerate(streams):
+        for slot in range(4):
+            w_buf[s, where_ref[slot]] = blocks[4 * group + slot][places[slot]]
     for s in range(len(streams)):
-        for copy in weight_copies(s):
-            copy.start()
-    outgoing = []
-    for s in range(len(streams)):
-        for copy in weight_copies(s):
-            copy.wait()
         for slot in range(4):
             place = pl.multiple_of(s * TILES * rows + withins[slot] * rows, rows)
             at = pl.multiple_of(sides[slot] * middle + place, rows)
-            staged = (4 * s + slot) * rows
-            for role, target, start in (
-                (FAR, None, place),
-                (KEEP, near_ref, at),
-                (GIVE, give_ref, at),
-                (SELF, give_ref, pl.multiple_of(2 * middle + at, rows)),
-            ):
-                here = o_buf.at[role, pl.ds(staged, rows)]
-                here[...] = jnp.dot(tokens[slot][...], w_buf[s, role], preferred_element_type=F32).astype(BF16)
-                if target is not None:
-                    copy = pltpu.make_async_copy(here, target.at[pl.ds(start, rows)], o_sem.at[4 * s + slot, role])
-                    copy.start()
-                    outgoing.append(copy)
-                    continue
-
-                def far_copy(ref):
-                    return pltpu.make_async_copy(here, ref.at[pl.ds(start, rows)], f_sem.at[4 * s + slot])
-
-                if slot == 1:
-                    far_copy(far_give).start()
-                elif slot == 2:
-                    far_copy(far_keep).start()
-                else:
-
-                    @pl.when(core == sides[slot])
-                    def _():
-                        far_copy(far_keep).start()
-
-                    @pl.when(core != sides[slot])
-                    def _():
-                        far_copy(far_give).start()
-
-                outgoing.append(far_copy(far_keep))
-    for copy in outgoing:
-        copy.wait()
-
-
-def project(where, streams, tokens, weights, passed, behind=()):
-    rows, depth = tokens[0].shape
-    width = weights.shape[2]
+
+            def product(role):
+                return jnp.dot(tokens[slot][...], w_buf[s, role], preferred_element_type=F32).astype(BF16)
+
+            near_ref[pl.ds(at, rows), :] = product(KEEP)
+            give_ref[pl.ds(at, rows), :] = product(GIVE)
+            give_ref[pl.ds(pl.multiple_of(2 * middle + at, rows), rows), :] = product(SELF)
+            if slot == 1:
+                far_give[pl.ds(place, rows), :] = product(FAR)
+            elif slot == 2:
+                far_keep[pl.ds(place, rows), :] = product(FAR)
+            else:
+
+                @pl.when(core == sides[slot])
+                def _():
+                    far_keep[pl.ds(place, rows), :] = product(FAR)
+
+                @pl.when(core != sides[slot])
+                def _():
+                    far_give[pl.ds(place, rows), :] = product(FAR)
+
+
+def project(where, tokens, groups, streams, behind=()):
+    rows = tokens[0].shape[0]
+    depth, width = groups[0][0].shape[1:]
     total = 4 * len(streams) * rows
-    groups = []
-    for m in streams:
-        if not any(passed[m][0] is group for group in groups):
-            groups.append(passed[m][0])
-    held = tuple((m, [passed[m][0] is group for group in groups].index(True), passed[m][1]) for m in streams)
-    hbm = pl.BlockSpec(memory_space=pl.ANY)
-    operands = [weights] + [block for group in groups for block in group] + list(behind)
-    return pl.pallas_call(
-        functools.partial(project_kernel, held, len(behind)),
-        out_shape=tuple(jax.ShapeDtypeStruct((n, width), BF16) for n in (total // 2, total // 2, total, 2 * total)),
-        in_specs=[pl.BlockSpec(memory_space=pltpu.SMEM)]
-        + [pl.BlockSpec(memory_space=pltpu.VMEM)] * 4
-        + [hbm] * len(operands),
-        out_specs=(hbm,) * 4,
-        scratch_shapes=[
-            pltpu.VMEM((len(streams), 4, depth, width), BF16),
-            pltpu.VMEM((4, total, width), BF16),
-            pltpu.SemaphoreType.DMA((len(streams), 4)),
-            pltpu.SemaphoreType.DMA((4 * len(streams), 3)),
-            pltpu.SemaphoreType.DMA((4 * len(streams),)),
-        ],
-        compiler_params=pltpu.CompilerParams(vmem_limit_bytes=VMEM_LIMIT),
-        cost_estimate=pl.CostEstimate(flops=COST, bytes_accessed=COST, transcendentals=0),
-        name="project",
-    )(where, *tokens, *operands)
-
-
-def pick_kernel(first, source_ref, out_ref, sem):
-    copies = [
-        pltpu.make_async_copy(source_ref.at[first + k], out_ref.at[k], sem.at[k]) for k in range(out_ref.shape[0])
-    ]
-    for copy in copies:
-        copy.start()
-    for copy in copies:
-        copy.wait()
-
-
-def pick(value, first, count):
-    hbm = pl.BlockSpec(memory_space=pl.ANY)
-    return pl.pallas_call(
-        functools.partial(pick_kernel, first),
-        out_shape=jax.ShapeDtypeStruct((count,) + value.shape[1:], value.dtype),
-        in_specs=[hbm],
-        out_specs=hbm,
-        scratch_shapes=[pltpu.SemaphoreType.DMA((count,))],
-        cost_estimate=pl.CostEstimate(flops=COST, bytes_accessed=COST, transcendentals=0),
-        name="pick",
-    )(value)
+    shapes = tuple(jax.ShapeDtypeStruct((n, width), BF16) for n in (total // 2, total // 2, total, 2 * total))
+    return local_call(
+        functools.partial(project_kernel, tuple(streams), len(behind)),
+        shapes,
+        (where,),
+        list(tokens) + [block for group in groups for block in group],
+        list(behind),
+        [pltpu.VMEM((len(streams), 4, depth, width), BF16)],
+        "project",
+        32,
+    )
 
 
 def near_kernel(where_ref, keep_ref, got_ref, arrived_ref, *refs):
@@ -204,9 +139,10 @@
     def copies(number):
         stream, tile = divmod(number, TILES)
         within = tile + core - 2 * tile * core
-        row = pl.multiple_of(core * (total // 2) + stream * TILES * rows + within * rows, rows)
+        place = pl.multiple_of(stream * TILES * rows + within * rows, rows)
+        row = pl.multiple_of(core * (total // 2) + place, rows)
         beyond = pl.multiple_of(total + row, rows)
-        parts = [give.at[pl.ds(beyond, rows)], got.at[pl.ds(beyond, rows)], reached.at[pl.ds(row, rows)], crossed.at[pl.ds(row, rows)]]
+        parts = [give.at[pl.ds(beyond, rows)], got.at[pl.ds(beyond, rows)], reached.at[pl.ds(row, rows)], crossed.at[pl.ds(place, rows)]]
         return [pltpu.make_async_copy(part, buf.at[number, k], sem.at[number, k]) for k, part in enumerate(parts)]
 
     for number in range(count):
@@ -294,18 +230,16 @@
 
 def convolve_kernel(
     where_ref, source_ref, init_ref, rate_ref, weight_ref, skip_ref,
-    ends_ref, others_ref, beside_ref, crossed_ref, second_ref, out_ref, incoming_ref,
+    ends_ref, others_ref, one_ref, two_ref, three_ref, out_ref, incoming_ref,
 ):
     modes = rate_ref.shape[0]
     width, length = rate_ref.shape[1], source_ref.shape[1]
     rows = length // TILES
     rate = rate_ref[...]
     row = where_ref[ROW]
-    first_core = where_ref[CORE] == 0
-    beside, crossed = beside_ref[...], crossed_ref[...]
-    before = jnp.where(row >= 1, jnp.where(first_core, beside, crossed), 0.0)
-    before = before + jnp.where(row >= 2, tile_fade(rate, rows, N) * second_ref[...], 0.0)
-    before = before + jnp.where(row >= 3, tile_fade(rate, rows, 2 * N) * jnp.where(first_core, crossed, beside), 0.0)
+    before = jnp.where(row >= 1, one_ref[...], 0.0)
+    before = before + jnp.where(row >= 2, tile_fade(rate, rows, N) * two_ref[...], 0.0)
+    before = before + jnp.where(row >= 3, tile_fade(rate, rows, 2 * N) * three_ref[...], 0.0)
     tile_ends = [ends_ref[0], ends_ref[1], others_ref[0], others_ref[1]]
     spots = [lax.rem(where_ref[SPOT0] + i, N) for i in range(N)]
     for i in range(TILES):
@@ -386,8 +320,18 @@
     spots = [(x + 2 * c + i) % N for i in range(N)]
     where = jnp.stack([role(y), role(y - side), role(y + side), role(y + 2), c, spots[0], spots[1], y]).astype(jnp.int32)
 
+    def around(value, axis, *waits):
+        heard = split_ring(value, axis)
+        other = split_ring(value, axis, True)
+        passed_on = after(heard, *waits) if waits else heard
+        return heard, other, split_ring(passed_on, axis)
+
+    held = (tokens,) + around(tokens, "x")
+    pair = around(weights[1:], "y")
+    alone = around(after(weights, pair[0], pair[1])[:1], "y")
+
     packed = jnp.concatenate(
-        [short_taps.reshape(SHORT * 3, channels), residues, decay_scale, skip_gain[None]], axis=0
+        [after(short_taps, held[1]).reshape(SHORT * 3, channels), residues, decay_scale, skip_gain[None]], axis=0
     )
     packed = lax.dynamic_slice_in_dim(packed, (x % 2) * width, width, axis=1)
     packed = jnp.where(c == x // 2, packed, core_swap(packed))
@@ -396,19 +340,8 @@
     mode_weight = packed[SHORT * 3 : SHORT * 3 + modes] * jnp.sqrt(-jnp.expm1(-2.0 * rate))
     skip = packed[SHORT * 3 + 2 * modes :]
 
-    def around(value, axis, *waits):
-        heard = split_ring(value, axis)
-        other = split_ring(value, axis, True)
-        passed_on = after(heard, *waits) if waits else heard
-        return heard, other, split_ring(passed_on, axis)
-
-    held = (tokens,) + around(tokens, "x")
-    pair = around(pick(weights, 1, 2), "y", taps, rate, mode_weight, skip)
-    alone = around(pick(after(weights, pair[0], pair[1]), 0, 1), "y")
-    passed = {0: (alone, 0), 1: (pair, 0), 2: (pair, 1)}
-
-    def begin(streams, behind=()):
-        far_keep, far_give, near, give = project(where, streams, held, weights, passed, behind)
+    def begin(group, streams, behind=()):
+        far_keep, far_give, near, give = project(where, held, [(weights,) + group], streams, behind)
         far = (far_keep.astype(F32) + core_swap(far_give).astype(F32)).astype(BF16)
         return far, near, give, core_swap(after(give, far))
 
@@ -426,9 +359,10 @@
         )
         return summed
 
-    def end(summed, give, got, *waits):
+    def end(summed, give, got):
         reached = split_ring(summed, "z")
-        return give, got, reached, core_swap(after(reached, *waits) if waits else reached)
+        half = summed.shape[0] // 2
+        return give, got, reached, core_swap(lax.dynamic_slice_in_dim(reached, (1 - c) * half, half, axis=0))
 
     def finish(streams, piece):
         tail = jax.ShapeDtypeStruct((streams * HALO, width), F32)
@@ -451,13 +385,14 @@
         ]
         return parts, (lax.ppermute(last, ("y", "x", "c"), moves), core_swap(tail1), tail0)
 
-    far_ab, near_ab, give_ab, got_ab = begin((1, 2))
-    sum_ab = middle(far_ab, near_ab, got_ab, alone[:2])
-    far_c, near_c, give_c, got_c = begin((0,), (sum_ab,))
+    far_ab, near_ab, give_ab, got_ab = begin(pair, [(0, (1, 0, 0, 0)), (0, (2, 1, 1, 1))], (taps, rate, mode_weight, skip))
+    sum_ab = middle(far_ab, near_ab, got_ab, alone[:1])
+    far_c, near_c, give_c, got_c = begin(alone, [(0, (0, 0, 0, 0))], (sum_ab,))
     piece_ab = end(sum_ab, give_ab, got_ab)
-    sum_c = middle(far_c, near_c, got_c, (piece_ab[2],))
 
     (first, second), halo12 = finish(2, piece_ab)
+    sum_c = middle(far_c, near_c, got_c, (halo12[0],))
+    piece_c = end(sum_c, give_c, got_c)
     state = jax.ShapeDtypeStruct((TILES, modes, width), F32)
     full = jax.ShapeDtypeStruct((width // LANES, length, LANES), F32)
     extended = pltpu.VMEM((TILES, HALO + rows, width), F32)
@@ -473,19 +408,16 @@
     others = core_swap(ends)
     tile_ends = [ends[0], ends[1], others[0], others[1]]
     chip = sum(tile_fade(rate, rows, N - 1 - q) * e for q, e in zip(spots, tile_ends))
-    beside = split_ring(chip, "y")
-    crossed = core_swap(beside)
-    beyond = split_ring(beside, "y")
+    one, two, three = (lax.ppermute(chip, "y", [(i, (i + k) % N) for i in range(N)]) for k in (1, 2, 3))
     (convolved,) = local_call(
         convolve_kernel,
         (full,),
         (where,),
-        (source, init, rate, mode_weight, skip, ends, others, beside, crossed, beyond),
+        (source, init, rate, mode_weight, skip, ends, others, one, two, three),
         (),
         [pltpu.VMEM((TILES, modes, width), F32)],
         "convolve",
     )
-    piece_c = end(sum_c, give_c, got_c, beyond)
     (gate,), halo0 = finish(1, piece_c)
     block = jax.ShapeDtypeStruct((rows, width), BF16)
     blocks = local_call(

time: 233 us -> 185 us (0.79)
  Pallas kernels: 103 us -> 40.7 us
  local copies, waits for them, and re-layouts: 6.47 us -> 13.2 us
  starting transfers between devices: 44.7 us -> 49.4 us
  waiting for transfers between devices: 75.7 us -> 78.2 us
    pallas_call x4 -> x0, Pallas kernels: 84.3 us -> none  [the longest x2 49.9 us: pick(): pl.pallas_call(functools.partial(pick_kernel, first), out_shape=jax.Shape...]
    pallas_call x7 -> x9, Pallas kernels: 18.5 us -> 40.7 us  [local_call(): pl.pallas_call(kernel, out_shape=shapes, in_specs=[pl.BlockSpec(memory_sp...]
    ppermute x0 -> x3, starting transfers between devices: none -> 8.1 us  [on_device(): lax.ppermute(chip, 'y', [(i, (i + k) % N) for i in range(N)])]
    ppermute x15 -> x13, starting transfers between devices: 29.7 us -> 27.2 us  [split_ring(): return lax.ppermute(value, (axis, 'c'), moves)]
    slice x0 -> x2, local copies, waits for them, and re-layouts: none -> 2.48 us  [the longest x1 2.44 us: on_device(): pair = around(weights[1:], 'y')]
    ppermute x11 -> x10, waiting for transfers between devices: 7.78 us -> 9.67 us  [core_swap(): return lax.ppermute(value, 'c', [(0, 1), (1, 0)])]
    ppermute x11 -> x10, starting transfers between devices: 6.29 us -> 4.81 us  [core_swap(): return lax.ppermute(value, 'c', [(0, 1), (1, 0)])]
    ppermute x15 -> x13, waiting for transfers between devices: 59.7 us -> 61.1 us  [split_ring(): return lax.ppermute(value, (axis, 'c'), moves)]
  transfers between devices with their start and end apart: 30 -> 30, of which waited for: 18 -> 16; matrix products, arithmetic and copies ran while one was open for 1% -> 2% of each run, Pallas kernels for 19% -> 12%
where the time goes in v4:
time: 185 us
  waiting for transfers between devices  78.2 us (42%)
  starting transfers between devices  49.4 us (27%)
  Pallas kernels  40.7 us (22%)
  local copies, waits for them, and re-layouts  13.2 us (7%)
  other arithmetic  2.97 us (2%)
    ppermute x13, waiting for transfers between devices, split_ring(): return lax.ppermute(value, (axis, 'c'), moves)  61.1 us
    pallas_call x9, Pallas kernels, local_call(): pl.pallas_call(kernel, out_shape=shapes, in_specs=[pl.BlockSpec(memory_sp...  40.7 us
    ppermute x13, starting transfers between devices, split_ring(): return lax.ppermute(value, (axis, 'c'), moves)  27.2 us
    ppermute x10, waiting for transfers between devices, core_swap(): return lax.ppermute(value, 'c', [(0, 1), (1, 0)])  9.67 us
    ppermute x3, starting transfers between devices, on_device(): lax.ppermute(chip, 'y', [(i, (i + k) % N) for i in range(N)])  8.1 us
    unnamed x30, local copies, waits for them, and re-layouts  7.49 us
    ppermute x2, waiting for transfers between devices, on_device(): placed.append(lax.ppermute(blocks[r], ('x', 'c'), moves))  6.57 us
    ppermute x2, starting transfers between devices, on_device(): placed.append(lax.ppermute(blocks[r], ('x', 'c'), moves))  4.85 us
  transfers between devices with their start and end apart: 30, of which 16 were waited for; matrix products, arithmetic and copies ran while one was open for 2% of the time, Pallas kernels for 12%

profile of v4, /device:TPU:1, one launch (start us, length us, event | category | flops | bytes accessed | tf_op | source)
XLA Modules:
  0.0 184.9 jit_solution(12764620947664550277)
XLA Ops:
  0.0 2.4 %slice.40 = bf16[2,1024,256]{2,1,0:T(8,128)(2,1)} slice(bf16[3,1024,256]{2,1,0:T(8,128)(2,1)} %bitcast.34), slice={[1:3], [0:1024], [0:256]} | slice | bytes 2097152 | tf_op jit(solution)/shard_map/slice | solution.py:330
  2.4 3.6 %collective-permute-start.3 = (bf16[2,1024,256]{2,1,0:T(8,128)(2,1)}, bf16[2,1024,256]{2,1,0:T(8,128)(2,1)}, u32[]{:S(2)}, u32[]{:S(2)}) collective-permute-start(bf16[2,1024,256]{2,1,0:T(8,128)(2,1)} %slice.40), channel_id=1, source_target_pairs={{0,32},{1,97},{32,64},{33,1},{64,96},{65,33},{96,0},{97,65},{2,34}... | collective-permute-start | bytes 3145736 | tf_op jit(solution)/shard_map/ppermute | solution.py:28
  6.0 2.5 %collective-permute-start = (bf16[512,1024]{1,0:T(8,128)(2,1)}, bf16[512,1024]{1,0:T(8,128)(2,1)}, u32[]{:S(2)}, u32[]{:S(2)}) collective-permute-start(bf16[512,1024]{1,0:T(8,128)(2,1)} %refs_0_.3), channel_id=1, source_target_pairs={{0,8},{1,25},{8,16},{9,1},{16,24},{17,9},{24,0},{25,17},{2,10},{3,... | collective-permute-start | bytes 3145736 | tf_op jit(solution)/shard_map/ppermute | solution.py:28
  8.5 17.9 %collective-permute-done.3.refs_5_ = bf16[2,1024,256]{2,1,0:T(8,128)(2,1)} collective-permute-done((bf16[2,1024,256]{2,1,0:T(8,128)(2,1)}, bf16[2,1024,256]{2,1,0:T(8,128)(2,1)}, u32[]{:S(2)}, u32[]{:S(2)}) %collective-permute-start.3) | collective-permute-done | bytes 1048608 | tf_op jit(solution)/shard_map/ppermute | solution.py:28
  26.4 3.4 %collective-permute-start.8 = (bf16[2,1024,256]{2,1,0:T(8,128)(2,1)}, bf16[2,1024,256]{2,1,0:T(8,128)(2,1)}, u32[]{:S(2)}, u32[]{:S(2)}) collective-permute-start(bf16[2,1024,256]{2,1,0:T(8,128)(2,1)} %collective-permute-done.3.refs_5_), channel_id=1, source_target_pairs={{0,32},{1,97},{32,64},{33,1},{64,96},{65,33},{96,0},{97,65},{2,34}... | collective-permute-start | bytes 3145736 | tf_op jit(solution)/shard_map/ppermute | solution.py:28
  29.8 3.6 %collective-permute-start.2 = (bf16[512,1024]{1,0:T(8,128)(2,1)}, bf16[512,1024]{1,0:T(8,128)(2,1)}, u32[]{:S(2)}, u32[]{:S(2)}) collective-permute-start(bf16[512,1024]{1,0:T(8,128)(2,1)} %collective-permute-done.refs_1_), channel_id=1, source_target_pairs={{0,8},{1,25},{8,16},{9,1},{16,24},{17,9},{24,0},{25,17},{2,10},{3,... | collective-permute-start | bytes 3145736 | tf_op jit(solution)/shard_map/ppermute | solution.py:28
  33.4 0.8 copy.8
  34.2 0.8 fusion.2
  35.4 1.0 collective-permute-done.9
  36.5 5.4 %collective-permute-done.8.refs_7_ = bf16[2,1024,256]{2,1,0:T(8,128)(2,1)} collective-permute-done((bf16[2,1024,256]{2,1,0:T(8,128)(2,1)}, bf16[2,1024,256]{2,1,0:T(8,128)(2,1)}, u32[]{:S(2)}, u32[]{:S(2)}) %collective-permute-start.8) | collective-permute-done | bytes 1048608 | tf_op jit(solution)/shard_map/ppermute | solution.py:28
  41.9 3.6 %collective-permute-done.2.refs_3_ = bf16[512,1024]{1,0:T(8,128)(2,1)} collective-permute-done((bf16[512,1024]{1,0:T(8,128)(2,1)}, bf16[512,1024]{1,0:T(8,128)(2,1)}, u32[]{:S(2)}, u32[]{:S(2)}) %collective-permute-start.2) | collective-permute-done | bytes 1048608 | tf_op jit(solution)/shard_map/ppermute | solution.py:28
  45.4 13.3 %project.2 = (bf16[2048,256]{1,0:T(8,128)(2,1)S(1)}, bf16[2048,256]{1,0:T(8,128)(2,1)S(1)}, bf16[4096,256]{1,0:T(8,128)(2,1)S(1)}, bf16[8192,256]{1,0:T(8,128)(2,1)S(1)}) custom-call(s32[8]{0:T(128)S(1)} %stack.35.where_ref, bf16[512,1024]{1,0:T(8,128)(2,1)S(1)} %copy-done.3, bf16[512,1024]{1,0:T(8,128)(2,1)} %collective-permute-done.refs_1_, ...), custom_call_target="tpu_custom_call" | custom-call | flops 1000 | bytes 1000 | tf_op jit(solution)/shard_map/project/pallas_call | solution.py:41
  58.8 1.8 collective-permute-start.10
  60.6 2.3 %collective-permute-done.10 = bf16[2048,256]{1,0:T(8,128)(2,1)S(1)} collective-permute-done((bf16[2048,256]{1,0:T(8,128)(2,1)S(1)}, bf16[2048,256]{1,0:T(8,128)(2,1)S(1)}, u32[]{:S(2)}, u32[]{:S(2)}) %collective-permute-start.10) | collective-permute-done | bytes 1048608 | tf_op jit(solution)/shard_map/ppermute | solution.py:32
  62.9 0.3 add_convert_fusion
  63.2 0.5 collective-permute-start.11
  63.7 3.7 %collective-permute-start.12 = (bf16[2048,256]{1,0:T(8,128)(2,1)S(1)}, bf16[2048,256]{1,0:T(8,128)(2,1)S(1)}, u32[]{:S(2)}, u32[]{:S(2)}) collective-permute-start(bf16[2048,256]{1,0:T(8,128)(2,1)S(1)} %add_convert_fusion), channel_id=1, source_target_pairs={{0,2},{1,7},{2,4},{3,1},{4,6},{5,3},{6,0},{7,5},{8,10},{9,15},{10,... | collective-permute-start | bytes 3145736 | tf_op jit(solution)/shard_map/ppermute | solution.py:28
  67.5 1.6 collective-permute-start.5
  69.1 7.5 %collective-permute-done.5.refs_0_.refs_5_ = bf16[1,1024,256]{2,1,0:T(8,128)(2,1)S(1)} collective-permute-done((bf16[1,1024,256]{2,1,0:T(8,128)(2,1)S(1)}, bf16[1,1024,256]{2,1,0:T(8,128)(2,1)S(1)}, u32[]{:S(2)}, u32[]{:S(2)}) %collective-permute-start.5) | collective-permute-done | bytes 524320 | tf_op jit(solution)/shard_map/ppermute | solution.py:28
  76.6 2.5 %collective-permute-done.12.arrived_ref = bf16[2048,256]{1,0:T(8,128)(2,1)S(1)} collective-permute-done((bf16[2048,256]{1,0:T(8,128)(2,1)S(1)}, bf16[2048,256]{1,0:T(8,128)(2,1)S(1)}, u32[]{:S(2)}, u32[]{:S(2)}) %collective-permute-start.12) | collective-permute-done | bytes 1048608 | tf_op jit(solution)/shard_map/ppermute | solution.py:28
  79.2 2.6 %near.2.refs_8_ = bf16[4096,256]{1,0:T(8,128)(2,1)} custom-call(s32[8]{0:T(128)S(1)} %stack.35.where_ref, bf16[4096,256]{1,0:T(8,128)(2,1)S(1)} %get-tuple-element.33.keep_ref, bf16[8192,256]{1,0:T(8,128)(2,1)S(1)} %collective-permute-done.11.got_ref.refs_1_, bf16[2048,256]{1,0:T(8,128)(2,1)S(1)} %collective-permute-done.12.arrived_ref, ...), custom_call_target="tpu_custom_call" | custom-call | flops 1000 | bytes 1000 | tf_op jit(solution)/shard_map/near/pallas_call | solution.py:41
  81.8 3.1 %collective-permute-start.16 = (bf16[4096,256]{1,0:T(8,128)(2,1)}, bf16[4096,256]{1,0:T(8,128)(2,1)}, u32[]{:S(2)}, u32[]{:S(2)}) collective-permute-start(bf16[4096,256]{1,0:T(8,128)(2,1)} %near.2.refs_8_), channel_id=1, source_target_pairs={{0,2},{1,7},{2,4},{3,1},{4,6},{5,3},{6,0},{7,5},{8,10},{9,15},{10,... | collective-permute-start | bytes 6291464 | tf_op jit(solution)/shard_map/ppermute | solution.py:28
  84.9 2.2 %collective-permute-start.6 = (bf16[1,1024,256]{2,1,0:T(8,128)(2,1)S(1)}, bf16[1,1024,256]{2,1,0:T(8,128)(2,1)S(1)}, u32[]{:S(2)}, u32[]{:S(2)}) collective-permute-start(bf16[1,1024,256]{2,1,0:T(8,128)(2,1)S(1)} %slice.31), channel_id=1, source_target_pairs={{0,96},{1,33},{32,0},{33,65},{64,32},{65,97},{96,64},{97,1},{2,98}... | collective-permute-start | bytes 1572872 | tf_op jit(solution)/shard_map/ppermute | solution.py:28
  87.2 0.4 collective-permute-start.7
  87.6 12.0 %collective-permute-done.6.refs_6_ = bf16[1,1024,256]{2,1,0:T(8,128)(2,1)S(1)} collective-permute-done((bf16[1,1024,256]{2,1,0:T(8,128)(2,1)S(1)}, bf16[1,1024,256]{2,1,0:T(8,128)(2,1)S(1)}, u32[]{:S(2)}, u32[]{:S(2)}) %collective-permute-start.6) | collective-permute-done | bytes 524320 | tf_op jit(solution)/shard_map/ppermute | solution.py:28
  99.6 8.3 %project.3 = (bf16[1024,256]{1,0:T(8,128)(2,1)S(1)}, bf16[1024,256]{1,0:T(8,128)(2,1)S(1)}, bf16[2048,256]{1,0:T(8,128)(2,1)S(1)}, bf16[4096,256]{1,0:T(8,128)(2,1)}) custom-call(s32[8]{0:T(128)S(1)} %stack.35.where_ref, bf16[512,1024]{1,0:T(8,128)(2,1)S(1)} %copy-done.3, bf16[512,1024]{1,0:T(8,128)(2,1)} %collective-permute-done.refs_1_, ...), custom_call_target="tpu_custom_call" | custom-call | flops 1000 | bytes 1000 | tf_op jit(solution)/shard_map/project/pallas_call | solution.py:41
  108.0 0.9 collective-permute-start.13
  108.8 1.5 collective-permute-done.13
  110.4 0.9 add_convert_fusion.1
  111.3 0.4 collective-permute-start.14
  111.7 1.4 constant_dynamic-slice_fusion.1
  113.1 0.2 collective-permute-start.17
  113.3 1.1 collective-permute-start.15
  114.4 2.5 %collective-permute-done.17.refs_3_ = bf16[2048,256]{1,0:T(8,128)(2,1)S(1)} collective-permute-done((bf16[2048,256]{1,0:T(8,128)(2,1)S(1)}, bf16[2048,256]{1,0:T(8,128)(2,1)S(1)}, u32[]{:S(2)}, u32[]{:S(2)}) %collective-permute-start.17) | collective-permute-done | bytes 1048608 | tf_op jit(solution)/shard_map/ppermute | solution.py:32
  117.0 2.2 %copy-done.1 = bf16[8192,256]{1,0:T(8,128)(2,1)S(1)} copy-done((bf16[8192,256]{1,0:T(8,128)(2,1)S(1)}, bf16[8192,256]{1,0:T(8,128)(2,1)}, u32[]{:S(2)}) %copy-start.1) | copy-done | bytes 4194328
  119.2 2.2 %copy-done.5 = bf16[8192,256]{1,0:T(8,128)(2,1)S(1)} copy-done((bf16[8192,256]{1,0:T(8,128)(2,1)S(1)}, bf16[8192,256]{1,0:T(8,128)(2,1)}, u32[]{:S(2)}) %copy-start.5) | copy-done | bytes 4194328
  121.3 2.3 %final.2 = (bf16[1024,256]{1,0:T(8,128)(2,1)S(1)}, bf16[1024,256]{1,0:T(8,128)(2,1)S(1)}, f32[16,256]{1,0:T(8,128)S(1)}, f32[16,256]{1,0:T(8,128)S(1)}, f32[16,256]{1,0:T(8,128)S(1)}) custom-call(s32[8]{0:T(128)S(1)} %stack.35.where_ref, bf16[8192,256]{1,0:T(8,128)(2,1)S(1)} %copy-done.5, bf16[8192,256]{1,0:T(8,128)(2,1)S(1)} %copy-done.1, ...), custom_call_target="tpu_custom_call" | custom-call | flops 1000 | bytes 1000 | tf_op jit(solution)/shard_map/final/pallas_call | solution.py:41
  123.7 2.0 %collective-permute-start.18 = (f32[16,256]{1,0:T(8,128)S(1)}, f32[16,256]{1,0:T(8,128)S(1)}, u32[]{:S(2)}, u32[]{:S(2)}) collective-permute-start(f32[16,256]{1,0:T(8,128)S(1)} %get-tuple-element.43), channel_id=1, source_target_pairs={{1,32},{9,41},{16,49},{24,56},{33,64},{41,73},{48,81},{56,88},{65,... | collective-permute-start | bytes 49160 | tf_op jit(solution)/shard_map/ppermute | solution.py:386
  125.8 0.8 collective-permute-done.18.refs_0_.below_ref
  126.6 1.9 %near.3 = bf16[2048,256]{1,0:T(8,128)(2,1)} custom-call(s32[8]{0:T(128)S(1)} %stack.35.where_ref, bf16[2048,256]{1,0:T(8,128)(2,1)S(1)} %copy-done.7, bf16[4096,256]{1,0:T(8,128)(2,1)S(1)} %collective-permute-done.14.got_ref.refs_1_, bf16[1024,256]{1,0:T(8,128)(2,1)S(1)} %collective-permute-done.15.arrived_ref, ...), custom_call_target="tpu_custom_call" | custom-call | flops 1000 | bytes 1000 | tf_op jit(solution)/shard_map/near/pallas_call | solution.py:41
  128.4 1.8 collective-permute-start.19
  130.3 12.2 %collective-permute-done.19.refs_2_ = bf16[2048,256]{1,0:T(8,128)(2,1)S(1)} collective-permute-done((bf16[2048,256]{1,0:T(8,128)(2,1)}, bf16[2048,256]{1,0:T(8,128)(2,1)S(1)}, u32[]{:S(2)}, u32[]{:S(2)}) %collective-permute-start.19) | collective-permute-done | bytes 1048608 | tf_op jit(solution)/shard_map/ppermute | solution.py:28
  142.5 0.8 constant_dynamic-slice_fusion
  143.3 0.4 collective-permute-start.20
  143.7 0.1 collective-permute-start.23
  143.8 1.4 collective-permute-done.23.beside_ref
  145.3 1.0 copy-done.11
  146.3 1.0 copy-done.13
  147.3 4.4 %states.1 = (f32[2,1024,128]{2,1,0:T(8,128)S(1)}, f32[16,8,256]{2,1,0:T(8,128)S(1)}, f32[2,16,256]{2,1,0:T(8,128)S(1)}) custom-call(s32[8]{0:T(128)S(1)} %stack.35.where_ref, bf16[1024,256]{1,0:T(8,128)(2,1)S(1)} %copy-done.11, bf16[1024,256]{1,0:T(8,128)(2,1)S(1)} %copy-done.13, f32[16,256]{1,0:T(8,128)S(1)} %collective-permute-done.18.refs_0_.below_ref, ...), custom_call_target="tpu_custom_call" | custom-call | flops 1000 | bytes 1000 | tf_op jit(solution)/shard_map/states/pallas_call | solution.py:41
  151.7 1.0 copy-done.8
  152.7 0.4 collective-permute-start.24
  153.1 0.9 collective-permute-done.24.others_ref
  154.0 4.1 %collective-permute-start.25 = (f32[16,256]{1,0:T(8,128)S(1)}, f32[16,256]{1,0:T(8,128)S(1)}, u32[]{:S(2)}, u32[]{:S(2)}) collective-permute-start(f32[16,256]{1,0:T(8,128)S(1)} %fusion.4), channel_id=1, source_target_pairs={{0,32},{32,64},{64,96},{96,0},{1,33},{33,65},{65,97},{97,1},{2,34}... | collective-permute-start | bytes 49160 | tf_op jit(solution)/shard_map/ppermute | solution.py:411
  158.1 2.2 %collective-permute-start.26 = (f32[16,256]{1,0:T(8,128)S(1)}, f32[16,256]{1,0:T(8,128)S(1)}, u32[]{:S(2)}, u32[]{:S(2)}) collective-permute-start(f32[16,256]{1,0:T(8,128)S(1)} %fusion.4), channel_id=1, source_target_pairs={{0,64},{32,96},{64,0},{96,32},{1,65},{33,97},{65,1},{97,33},{2,66}... | collective-permute-start | bytes 49160 | tf_op jit(solution)/shard_map/ppermute | solution.py:411
  160.3 1.8 collective-permute-start.27
  162.1 2.1 %final.3 = (bf16[1024,256]{1,0:T(8,128)(2,1)S(1)}, f32[8,256]{1,0:T(8,128)S(1)}, f32[8,256]{1,0:T(8,128)S(1)}, f32[8,256]{1,0:T(8,128)S(1)}) custom-call(s32[8]{0:T(128)S(1)} %stack.35.where_ref, bf16[4096,256]{1,0:T(8,128)(2,1)} %get-tuple-element.41.refs_0_, bf16[4096,256]{1,0:T(8,128)(2,1)S(1)} %collective-permute-done.14.got_ref.refs_1_, ...), custom_call_target="tpu_custom_call" | custom-call | flops 1000 | bytes 1000 | tf_op jit(solution)/shard_map/final/pallas_call | solution.py:41
  164.2 2.4 %collective-permute-start.21 = (f32[8,256]{1,0:T(8,128)S(1)}, f32[8,256]{1,0:T(8,128)S(1)}, u32[]{:S(2)}, u32[]{:S(2)}) collective-permute-start(f32[8,256]{1,0:T(8,128)S(1)} %get-tuple-element.45), channel_id=1, source_target_pairs={{1,32},{9,41},{16,49},{24,56},{33,64},{41,73},{48,81},{56,88},{65,... | collective-permute-start | bytes 24584 | tf_op jit(solution)/shard_map/ppermute | solution.py:386
  166.8 4.2 %convolve.1.conv_ref = f32[2,1024,128]{2,1,0:T(8,128)S(1)} custom-call(s32[8]{0:T(128)S(1)} %stack.35.where_ref, f32[2,1024,128]{2,1,0:T(8,128)S(1)} %copy-done.9, f32[16,8,256]{2,1,0:T(8,128)S(1)} %get-tuple-element.53.init_ref, f32[16,256]{1,0:T(8,128)S(1)} %get-tuple-element.60.refs_9_.rate_ref, f32[16,256]{1,0:T(8,128)S(1)} %get-tuple-element.59.refs_10_.weight_ref, ...), custom_call_target="tpu_custom_call" | custom-call | flops 1000 | bytes 1000 | tf_op jit(solution)/shard_map/convolve/pallas_call | solution.py:41
  171.0 1.6 gate.1
  172.6 1.9 %collective-permute-start.28 = (bf16[512,256]{1,0:T(8,128)(2,1)S(1)}, bf16[512,256]{1,0:T(8,128)(2,1)S(1)}, u32[]{:S(2)}, u32[]{:S(2)}) collective-permute-start(bf16[512,256]{1,0:T(8,128)(2,1)S(1)} %get-tuple-element.55), channel_id=1, source_target_pairs={{0,0},{1,16},{8,8},{9,24},{16,17},{17,1},{24,25},{25,9},{2,2},{3,1... | collective-permute-start | bytes 786440 | tf_op jit(solution)/shard_map/ppermute | solution.py:436
  174.5 2.9 %collective-permute-start.29 = (bf16[512,256]{1,0:T(8,128)(2,1)S(1)}, bf16[512,256]{1,0:T(8,128)(2,1)S(1)}, u32[]{:S(2)}, u32[]{:S(2)}) collective-permute-start(bf16[512,256]{1,0:T(8,128)(2,1)S(1)} %get-tuple-element.56), channel_id=1, source_target_pairs={{0,8},{1,24},{8,16},{9,0},{16,25},{17,9},{24,1},{25,17},{2,10},{3,... | collective-permute-start | bytes 786440 | tf_op jit(solution)/shard_map/ppermute | solution.py:436
  177.4 5.1 %collective-permute-done.28 = bf16[512,256]{1,0:T(8,128)(2,1)S(1)} collective-permute-done((bf16[512,256]{1,0:T(8,128)(2,1)S(1)}, bf16[512,256]{1,0:T(8,128)(2,1)S(1)}, u32[]{:S(2)}, u32[]{:S(2)}) %collective-permute-start.28) | collective-permute-done | bytes 262176 | tf_op jit(solution)/shard_map/ppermute | solution.py:436
  182.6 1.4 collective-permute-done.29
  184.0 0.8 pad_maximum_fusion
  (53 shorter events, 0.5 us)
Async XLA Ops:
  0.0 45.4 %copy-start.2 = (bf16[1024,3,256]{2,0,1:T(8,128)(2,1)S(1)}, bf16[1024,3,256]{2,0,1:T(8,128)(2,1)}, u32[]{:S(2)}) copy-start(bf16[1024,3,256]{2,0,1:T(8,128)(2,1)} %param.7) | copy-start | bytes 4718596
  0.0 45.4 %copy-start.3 = (bf16[512,1024]{1,0:T(8,128)(2,1)S(1)}, bf16[512,1024]{1,0:T(8,128)(2,1)}, u32[]{:S(2)}) copy-start(bf16[512,1024]{1,0:T(8,128)(2,1)} %refs_0_.3) | copy-start | bytes 3145732
  2.4 23.9 %collective-permute-start.3 = (bf16[2,1024,256]{2,1,0:T(8,128)(2,1)}, bf16[2,1024,256]{2,1,0:T(8,128)(2,1)}, u32[]{:S(2)}, u32[]{:S(2)}) collective-permute-start(bf16[2,1024,256]{2,1,0:T(8,128)(2,1)} %slice.40), channel_id=1, source_target_pairs={{0,32},{1,97},{32,64},{33,1},{64,96},{65,33},{96,0},{97,65},{2,34}... | collective-permute-start | bytes 3145736 | tf_op jit(solution)/shard_map/ppermute | solution.py:28
  6.0 23.8 %collective-permute-start = (bf16[512,1024]{1,0:T(8,128)(2,1)}, bf16[512,1024]{1,0:T(8,128)(2,1)}, u32[]{:S(2)}, u32[]{:S(2)}) collective-permute-start(bf16[512,1024]{1,0:T(8,128)(2,1)} %refs_0_.3), channel_id=1, source_target_pairs={{0,8},{1,25},{8,16},{9,1},{16,24},{17,9},{24,0},{25,17},{2,10},{3,... | collective-permute-start | bytes 3145736 | tf_op jit(solution)/shard_map/ppermute | solution.py:28
  8.5 28.0 %collective-permute-start.4 = (bf16[2,1024,256]{2,1,0:T(8,128)(2,1)}, bf16[2,1024,256]{2,1,0:T(8,128)(2,1)}, u32[]{:S(2)}, u32[]{:S(2)}) collective-permute-start(bf16[2,1024,256]{2,1,0:T(8,128)(2,1)} %slice.40), channel_id=1, source_target_pairs={{0,96},{1,33},{32,0},{33,65},{64,32},{65,97},{96,64},{97,1},{2,98}... | collective-permute-start | bytes 3145736 | tf_op jit(solution)/shard_map/ppermute | solution.py:28
  8.5 28.0 %collective-permute-start.1 = (bf16[512,1024]{1,0:T(8,128)(2,1)}, bf16[512,1024]{1,0:T(8,128)(2,1)}, u32[]{:S(2)}, u32[]{:S(2)}) collective-permute-start(bf16[512,1024]{1,0:T(8,128)(2,1)} %refs_0_.3), channel_id=1, source_target_pairs={{0,24},{1,9},{8,0},{9,17},{16,8},{17,25},{24,16},{25,1},{2,26},{3,... | collective-permute-start | bytes 3145736 | tf_op jit(solution)/shard_map/ppermute | solution.py:28
  26.4 15.5 %collective-permute-start.8 = (bf16[2,1024,256]{2,1,0:T(8,128)(2,1)}, bf16[2,1024,256]{2,1,0:T(8,128)(2,1)}, u32[]{:S(2)}, u32[]{:S(2)}) collective-permute-start(bf16[2,1024,256]{2,1,0:T(8,128)(2,1)} %collective-permute-done.3.refs_5_), channel_id=1, source_target_pairs={{0,32},{1,97},{32,64},{33,1},{64,96},{65,33},{96,0},{97,65},{2,34}... | collective-permute-start | bytes 3145736 | tf_op jit(solution)/shard_map/ppermute | solution.py:28
  29.8 15.6 %collective-permute-start.2 = (bf16[512,1024]{1,0:T(8,128)(2,1)}, bf16[512,1024]{1,0:T(8,128)(2,1)}, u32[]{:S(2)}, u32[]{:S(2)}) collective-permute-start(bf16[512,1024]{1,0:T(8,128)(2,1)} %collective-permute-done.refs_1_), channel_id=1, source_target_pairs={{0,8},{1,25},{8,16},{9,1},{16,24},{17,9},{24,0},{25,17},{2,10},{3,... | collective-permute-start | bytes 3145736 | tf_op jit(solution)/shard_map/ppermute | solution.py:28
  35.1 1.3 collective-permute-start.9
  58.8 8.7 %copy-start.4 = (bf16[8192,256]{1,0:T(8,128)(2,1)}, bf16[8192,256]{1,0:T(8,128)(2,1)S(1)}, u32[]{:S(2)}) copy-start(bf16[8192,256]{1,0:T(8,128)(2,1)S(1)} %get-tuple-element.37.refs_0_) | copy-start | bytes 12582916
  58.8 4.1 %collective-permute-start.10 = (bf16[2048,256]{1,0:T(8,128)(2,1)S(1)}, bf16[2048,256]{1,0:T(8,128)(2,1)S(1)}, u32[]{:S(2)}, u32[]{:S(2)}) collective-permute-start(bf16[2048,256]{1,0:T(8,128)(2,1)S(1)} %get-tuple-element.36), channel_id=1, source_target_pairs={{0,1},{1,0},{2,3},{3,2},{4,5},{5,4},{6,7},{7,6},{8,9},{9,8},{10,11... | collective-permute-start | bytes 3145736 | tf_op jit(solution)/shard_map/ppermute | solution.py:32
  63.2 15.9 %collective-permute-start.11 = (bf16[8192,256]{1,0:T(8,128)(2,1)S(1)}, bf16[8192,256]{1,0:T(8,128)(2,1)S(1)}, u32[]{:S(2)}, u32[]{:S(2)}) collective-permute-start(bf16[8192,256]{1,0:T(8,128)(2,1)S(1)} %get-tuple-element.37.refs_0_), channel_id=1, source_target_pairs={{0,1},{1,0},{2,3},{3,2},{4,5},{5,4},{6,7},{7,6},{8,9},{9,8},{10,11... | collective-permute-start | bytes 12582920 | tf_op jit(solution)/shard_map/ppermute | solution.py:32
  63.7 15.5 %collective-permute-start.12 = (bf16[2048,256]{1,0:T(8,128)(2,1)S(1)}, bf16[2048,256]{1,0:T(8,128)(2,1)S(1)}, u32[]{:S(2)}, u32[]{:S(2)}) collective-permute-start(bf16[2048,256]{1,0:T(8,128)(2,1)S(1)} %add_convert_fusion), channel_id=1, source_target_pairs={{0,2},{1,7},{2,4},{3,1},{4,6},{5,3},{6,0},{7,5},{8,10},{9,15},{10,... | collective-permute-start | bytes 3145736 | tf_op jit(solution)/shard_map/ppermute | solution.py:28
  67.5 9.2 %collective-permute-start.5 = (bf16[1,1024,256]{2,1,0:T(8,128)(2,1)S(1)}, bf16[1,1024,256]{2,1,0:T(8,128)(2,1)S(1)}, u32[]{:S(2)}, u32[]{:S(2)}) collective-permute-start(bf16[1,1024,256]{2,1,0:T(8,128)(2,1)S(1)} %slice.31), channel_id=1, source_target_pairs={{0,32},{1,97},{32,64},{33,1},{64,96},{65,33},{96,0},{97,65},{2,34}... | collective-permute-start | bytes 1572872 | tf_op jit(solution)/shard_map/ppermute | solution.py:28
  79.2 2.6 %copy-start = (bf16[8192,256]{1,0:T(8,128)(2,1)}, bf16[8192,256]{1,0:T(8,128)(2,1)S(1)}, u32[]{:S(2)}) copy-start(bf16[8192,256]{1,0:T(8,128)(2,1)S(1)} %collective-permute-done.11.got_ref.refs_1_) | copy-start | bytes 12582916
  81.8 29.9 %collective-permute-start.16 = (bf16[4096,256]{1,0:T(8,128)(2,1)}, bf16[4096,256]{1,0:T(8,128)(2,1)}, u32[]{:S(2)}, u32[]{:S(2)}) collective-permute-start(bf16[4096,256]{1,0:T(8,128)(2,1)} %near.2.refs_8_), channel_id=1, source_target_pairs={{0,2},{1,7},{2,4},{3,1},{4,6},{5,3},{6,0},{7,5},{8,10},{9,15},{10,... | collective-permute-start | bytes 6291464 | tf_op jit(solution)/shard_map/ppermute | solution.py:28
  84.9 14.7 %collective-permute-start.6 = (bf16[1,1024,256]{2,1,0:T(8,128)(2,1)S(1)}, bf16[1,1024,256]{2,1,0:T(8,128)(2,1)S(1)}, u32[]{:S(2)}, u32[]{:S(2)}) collective-permute-start(bf16[1,1024,256]{2,1,0:T(8,128)(2,1)S(1)} %slice.31), channel_id=1, source_target_pairs={{0,96},{1,33},{32,0},{33,65},{64,32},{65,97},{96,64},{97,1},{2,98}... | collective-permute-start | bytes 1572872 | tf_op jit(solution)/shard_map/ppermute | solution.py:28
  87.2 12.4 %collective-permute-start.7 = (bf16[1,1024,256]{2,1,0:T(8,128)(2,1)S(1)}, bf16[1,1024,256]{2,1,0:T(8,128)(2,1)S(1)}, u32[]{:S(2)}, u32[]{:S(2)}) collective-permute-start(bf16[1,1024,256]{2,1,0:T(8,128)(2,1)S(1)} %collective-permute-done.5.refs_0_.refs_5_), channel_id=1, source_target_pairs={{0,32},{1,97},{32,64},{33,1},{64,96},{65,33},{96,0},{97,65},{2,34}... | collective-permute-start | bytes 1572872 | tf_op jit(solution)/shard_map/ppermute | solution.py:28
  107.9 3.3 %copy-start.6 = (bf16[2048,256]{1,0:T(8,128)(2,1)}, bf16[2048,256]{1,0:T(8,128)(2,1)S(1)}, u32[]{:S(2)}) copy-start(bf16[2048,256]{1,0:T(8,128)(2,1)S(1)} %get-tuple-element.42.keep_ref) | copy-start | bytes 3145732
  108.0 2.4 %collective-permute-start.13 = (bf16[1024,256]{1,0:T(8,128)(2,1)S(1)}, bf16[1024,256]{1,0:T(8,128)(2,1)S(1)}, u32[]{:S(2)}, u32[]{:S(2)}) collective-permute-start(bf16[1024,256]{1,0:T(8,128)(2,1)S(1)} %get-tuple-element.40), channel_id=1, source_target_pairs={{0,1},{1,0},{2,3},{3,2},{4,5},{5,4},{6,7},{7,6},{8,9},{9,8},{10,11... | collective-permute-start | bytes 1572872 | tf_op jit(solution)/shard_map/ppermute | solution.py:32
  111.3 14.4 %collective-permute-start.14 = (bf16[4096,256]{1,0:T(8,128)(2,1)}, bf16[4096,256]{1,0:T(8,128)(2,1)S(1)}, u32[]{:S(2)}, u32[]{:S(2)}) collective-permute-start(bf16[4096,256]{1,0:T(8,128)(2,1)} %get-tuple-element.41.refs_0_), channel_id=1, source_target_pairs={{0,1},{1,0},{2,3},{3,2},{4,5},{5,4},{6,7},{7,6},{8,9},{9,8},{10,11... | collective-permute-start | bytes 6291464 | tf_op jit(solution)/shard_map/ppermute | solution.py:32
  111.7 1.6 copy-start.14
  111.7 14.9 %copy-start.7 = (bf16[2048,256]{1,0:T(8,128)(2,1)S(1)}, bf16[2048,256]{1,0:T(8,128)(2,1)}, u32[]{:S(2)}) copy-start(bf16[2048,256]{1,0:T(8,128)(2,1)} %copy-done.6) | copy-start | bytes 3145732
  113.1 3.9 %collective-permute-start.17 = (bf16[2048,256]{1,0:T(8,128)(2,1)S(1)}, bf16[2048,256]{1,0:T(8,128)(2,1)S(1)}, u32[]{:S(2)}, u32[]{:S(2)}) collective-permute-start(bf16[2048,256]{1,0:T(8,128)(2,1)S(1)} %constant_dynamic-slice_fusion.1), channel_id=1, source_target_pairs={{0,1},{1,0},{2,3},{3,2},{4,5},{5,4},{6,7},{7,6},{8,9},{9,8},{10,11... | collective-permute-start | bytes 3145736 | tf_op jit(solution)/shard_map/ppermute | solution.py:32
  113.3 12.4 %collective-permute-start.15 = (bf16[1024,256]{1,0:T(8,128)(2,1)S(1)}, bf16[1024,256]{1,0:T(8,128)(2,1)S(1)}, u32[]{:S(2)}, u32[]{:S(2)}) collective-permute-start(bf16[1024,256]{1,0:T(8,128)(2,1)S(1)} %copy-done.14), channel_id=1, source_target_pairs={{0,2},{1,7},{2,4},{3,1},{4,6},{5,3},{6,0},{7,5},{8,10},{9,15},{10,... | collective-permute-start | bytes 1572872 | tf_op jit(solution)/shard_map/ppermute | solution.py:28
  117.0 2.2 %copy-start.1 = (bf16[8192,256]{1,0:T(8,128)(2,1)S(1)}, bf16[8192,256]{1,0:T(8,128)(2,1)}, u32[]{:S(2)}) copy-start(bf16[8192,256]{1,0:T(8,128)(2,1)} %copy-done) | copy-start | bytes 12582916
  119.1 2.2 %copy-start.5 = (bf16[8192,256]{1,0:T(8,128)(2,1)S(1)}, bf16[8192,256]{1,0:T(8,128)(2,1)}, u32[]{:S(2)}) copy-start(bf16[8192,256]{1,0:T(8,128)(2,1)} %copy-done.4) | copy-start | bytes 12582916
  123.7 4.8 %copy-start.10 = (bf16[1024,256]{1,0:T(8,128)(2,1)}, bf16[1024,256]{1,0:T(8,128)(2,1)S(1)}, u32[]{:S(2)}) copy-start(bf16[1024,256]{1,0:T(8,128)(2,1)S(1)} %get-tuple-element.48.first_ref) | copy-start | bytes 1572868
  123.7 4.8 %copy-start.12 = (bf16[1024,256]{1,0:T(8,128)(2,1)}, bf16[1024,256]{1,0:T(8,128)(2,1)S(1)}, u32[]{:S(2)}) copy-start(bf16[1024,256]{1,0:T(8,128)(2,1)S(1)} %get-tuple-element.49.second_ref) | copy-start | bytes 1572868
  123.7 2.9 %collective-permute-start.18 = (f32[16,256]{1,0:T(8,128)S(1)}, f32[16,256]{1,0:T(8,128)S(1)}, u32[]{:S(2)}, u32[]{:S(2)}) collective-permute-start(f32[16,256]{1,0:T(8,128)S(1)} %get-tuple-element.43), channel_id=1, source_target_pairs={{1,32},{9,41},{16,49},{24,56},{33,64},{41,73},{48,81},{56,88},{65,... | collective-permute-start | bytes 49160 | tf_op jit(solution)/shard_map/ppermute | solution.py:386
  128.4 14.0 %collective-permute-start.19 = (bf16[2048,256]{1,0:T(8,128)(2,1)}, bf16[2048,256]{1,0:T(8,128)(2,1)S(1)}, u32[]{:S(2)}, u32[]{:S(2)}) collective-permute-start(bf16[2048,256]{1,0:T(8,128)(2,1)} %near.3), channel_id=1, source_target_pairs={{0,2},{1,7},{2,4},{3,1},{4,6},{5,3},{6,0},{7,5},{8,10},{9,15},{10,... | collective-permute-start | bytes 3145736 | tf_op jit(solution)/shard_map/ppermute | solution.py:28
  143.3 18.8 %collective-permute-start.20 = (bf16[1024,256]{1,0:T(8,128)(2,1)}, bf16[1024,256]{1,0:T(8,128)(2,1)}, u32[]{:S(2)}, u32[]{:S(2)}) collective-permute-start(bf16[1024,256]{1,0:T(8,128)(2,1)} %constant_dynamic-slice_fusion), channel_id=1, source_target_pairs={{0,1},{1,0},{2,3},{3,2},{4,5},{5,4},{6,7},{7,6},{8,9},{9,8},{10,11... | collective-permute-start | bytes 1572872 | tf_op jit(solution)/shard_map/ppermute | solution.py:32
  143.7 1.6 collective-permute-start.23
  145.3 1.0 copy-start.11
  146.3 1.0 copy-start.13
  151.7 1.0 copy-start.8
  152.7 1.2 collective-permute-start.24
  154.0 12.8 %copy-start.9 = (f32[2,1024,128]{2,1,0:T(8,128)S(1)}, f32[2,1024,128]{2,1,0:T(8,128)}, u32[]{:S(2)}) copy-start(f32[2,1024,128]{2,1,0:T(8,128)} %copy-done.8) | copy-start | bytes 3145732
  154.0 12.7 %collective-permute-start.25 = (f32[16,256]{1,0:T(8,128)S(1)}, f32[16,256]{1,0:T(8,128)S(1)}, u32[]{:S(2)}, u32[]{:S(2)}) collective-permute-start(f32[16,256]{1,0:T(8,128)S(1)} %fusion.4), channel_id=1, source_target_pairs={{0,32},{32,64},{64,96},{96,0},{1,33},{33,65},{65,97},{97,1},{2,34}... | collective-permute-start | bytes 49160 | tf_op jit(solution)/shard_map/ppermute | solution.py:411
  158.1 8.6 %collective-permute-start.26 = (f32[16,256]{1,0:T(8,128)S(1)}, f32[16,256]{1,0:T(8,128)S(1)}, u32[]{:S(2)}, u32[]{:S(2)}) collective-permute-start(f32[16,256]{1,0:T(8,128)S(1)} %fusion.4), channel_id=1, source_target_pairs={{0,64},{32,96},{64,0},{96,32},{1,65},{33,97},{65,1},{97,33},{2,66}... | collective-permute-start | bytes 49160 | tf_op jit(solution)/shard_map/ppermute | solution.py:411
  160.3 6.5 %collective-permute-start.27 = (f32[16,256]{1,0:T(8,128)S(1)}, f32[16,256]{1,0:T(8,128)S(1)}, u32[]{:S(2)}, u32[]{:S(2)}) collective-permute-start(f32[16,256]{1,0:T(8,128)S(1)} %fusion.4), channel_id=1, source_target_pairs={{0,96},{32,0},{64,32},{96,64},{1,97},{33,1},{65,33},{97,65},{2,98}... | collective-permute-start | bytes 49160 | tf_op jit(solution)/shard_map/ppermute | solution.py:411
  164.2 6.8 %collective-permute-start.21 = (f32[8,256]{1,0:T(8,128)S(1)}, f32[8,256]{1,0:T(8,128)S(1)}, u32[]{:S(2)}, u32[]{:S(2)}) collective-permute-start(f32[8,256]{1,0:T(8,128)S(1)} %get-tuple-element.45), channel_id=1, source_target_pairs={{1,32},{9,41},{16,49},{24,56},{33,64},{41,73},{48,81},{56,88},{65,... | collective-permute-start | bytes 24584 | tf_op jit(solution)/shard_map/ppermute | solution.py:386
  166.6 4.3 %collective-permute-start.22 = (f32[8,256]{1,0:T(8,128)S(1)}, f32[8,256]{1,0:T(8,128)S(1)}, u32[]{:S(2)}, u32[]{:S(2)}) collective-permute-start(f32[8,256]{1,0:T(8,128)S(1)} %get-tuple-element.46), channel_id=1, source_target_pairs={{0,1},{1,0},{2,3},{3,2},{4,5},{5,4},{6,7},{7,6},{8,9},{9,8},{10,11... | collective-permute-start | bytes 24584 | tf_op jit(solution)/shard_map/ppermute | solution.py:32
  172.6 10.0 %collective-permute-start.28 = (bf16[512,256]{1,0:T(8,128)(2,1)S(1)}, bf16[512,256]{1,0:T(8,128)(2,1)S(1)}, u32[]{:S(2)}, u32[]{:S(2)}) collective-permute-start(bf16[512,256]{1,0:T(8,128)(2,1)S(1)} %get-tuple-element.55), channel_id=1, source_target_pairs={{0,0},{1,16},{8,8},{9,24},{16,17},{17,1},{24,25},{25,9},{2,2},{3,1... | collective-permute-start | bytes 786440 | tf_op jit(solution)/shard_map/ppermute | solution.py:436
  174.5 9.5 %collective-permute-start.29 = (bf16[512,256]{1,0:T(8,128)(2,1)S(1)}, bf16[512,256]{1,0:T(8,128)(2,1)S(1)}, u32[]{:S(2)}, u32[]{:S(2)}) collective-permute-start(bf16[512,256]{1,0:T(8,128)(2,1)S(1)} %get-tuple-element.56), channel_id=1, source_target_pairs={{0,8},{1,24},{8,16},{9,0},{16,25},{17,9},{24,1},{25,17},{2,10},{3,... | collective-permute-start | bytes 786440 | tf_op jit(solution)/shard_map/ppermute | solution.py:436

commit v5 on v4

--- a/solution.py
+++ b/solution.py
@@ -142,7 +142,7 @@
         place = pl.multiple_of(stream * TILES * rows + within * rows, rows)
         row = pl.multiple_of(core * (total // 2) + place, rows)
         beyond = pl.multiple_of(total + row, rows)
-        parts = [give.at[pl.ds(beyond, rows)], got.at[pl.ds(beyond, rows)], reached.at[pl.ds(row, rows)], crossed.at[pl.ds(place, rows)]]
+        parts = [give.at[pl.ds(beyond, rows)], got.at[pl.ds(beyond, rows)], reached.at[pl.ds(row, rows)], crossed.at[pl.ds(row, rows)]]
         return [pltpu.make_async_copy(part, buf.at[number, k], sem.at[number, k]) for k, part in enumerate(parts)]
 
     for number in range(count):
@@ -359,10 +359,9 @@
         )
         return summed
 
-    def end(summed, give, got):
+    def end(summed, give, got, *waits):
         reached = split_ring(summed, "z")
-        half = summed.shape[0] // 2
-        return give, got, reached, core_swap(lax.dynamic_slice_in_dim(reached, (1 - c) * half, half, axis=0))
+        return give, got, reached, core_swap(after(reached, *waits) if waits else reached)
 
     def finish(streams, piece):
         tail = jax.ShapeDtypeStruct((streams * HALO, width), F32)
@@ -386,13 +385,12 @@
         return parts, (lax.ppermute(last, ("y", "x", "c"), moves), core_swap(tail1), tail0)
 
     far_ab, near_ab, give_ab, got_ab = begin(pair, [(0, (1, 0, 0, 0)), (0, (2, 1, 1, 1))], (taps, rate, mode_weight, skip))
-    sum_ab = middle(far_ab, near_ab, got_ab, alone[:1])
+    sum_ab = middle(far_ab, near_ab, got_ab, alone[:2])
     far_c, near_c, give_c, got_c = begin(alone, [(0, (0, 0, 0, 0))], (sum_ab,))
     piece_ab = end(sum_ab, give_ab, got_ab)
 
     (first, second), halo12 = finish(2, piece_ab)
     sum_c = middle(far_c, near_c, got_c, (halo12[0],))
-    piece_c = end(sum_c, give_c, got_c)
     state = jax.ShapeDtypeStruct((TILES, modes, width), F32)
     full = jax.ShapeDtypeStruct((width // LANES, length, LANES), F32)
     extended = pltpu.VMEM((TILES, HALO + rows, width), F32)
@@ -418,6 +416,7 @@
         [pltpu.VMEM((TILES, modes, width), F32)],
         "convolve",
     )
+    piece_c = end(sum_c, give_c, got_c, one, two, three)
     (gate,), halo0 = finish(1, piece_c)
     block = jax.ShapeDtypeStruct((rows, width), BF16)
     blocks = local_call(

time: 185 us -> 166 us (0.90)
  local copies, waits for them, and re-layouts: 13.2 us -> 5.88 us
  waiting for transfers between devices: 78.2 us -> 72.3 us
  Pallas kernels: 40.7 us -> 36.4 us
    ppermute x13, waiting for transfers between devices: 61.1 us -> 51.1 us  [split_ring(): return lax.ppermute(value, (axis, 'c'), moves)]
    ppermute x10, starting transfers between devices: 4.81 us -> 10.6 us  [core_swap(): return lax.ppermute(value, 'c', [(0, 1), (1, 0)])]
    unnamed x30 -> x12, local copies, waits for them, and re-layouts: 7.49 us -> 2.6 us
    pallas_call x9, Pallas kernels: 40.7 us -> 36.4 us  [local_call(): pl.pallas_call(kernel, out_shape=shapes, in_specs=[pl.BlockSpec(memory_sp...]
    ppermute x3, starting transfers between devices: 8.1 us -> 4.67 us  [on_device(): lax.ppermute(chip, 'y', [(i, (i + k) % N) for i in range(N)])]
    ppermute x13, starting transfers between devices: 27.2 us -> 23.8 us  [split_ring(): return lax.ppermute(value, (axis, 'c'), moves)]
    ppermute x3, waiting for transfers between devices: 0.01 us -> 2.88 us  [on_device(): lax.ppermute(chip, 'y', [(i, (i + k) % N) for i in range(N)])]
    dynamic_slice x2 -> x0, local copies, waits for them, and re-layouts: 2.24 us -> none  [end(): lax.dynamic_slice_in_dim(reached, (1 - c) * half, half, axis=0)]
  transfers between devices with their start and end apart: 30 -> 30, of which waited for: 16 -> 20; matrix products, arithmetic and copies ran while one was open for 2% -> 3% of each run, Pallas kernels for 12% -> 10%
where the time goes in v5:
time: 166 us
  waiting for transfers between devices  72.3 us (44%)
  starting transfers between devices  48.8 us (29%)
  Pallas kernels  36.4 us (22%)
  local copies, waits for them, and re-layouts  5.88 us (4%)
  other arithmetic  2.18 us (1%)
    ppermute x13, waiting for transfers between devices, split_ring(): return lax.ppermute(value, (axis, 'c'), moves)  51.1 us
    pallas_call x9, Pallas kernels, local_call(): pl.pallas_call(kernel, out_shape=shapes, in_specs=[pl.BlockSpec(memory_sp...  36.4 us
    ppermute x13, starting transfers between devices, split_ring(): return lax.ppermute(value, (axis, 'c'), moves)  23.8 us
    ppermute x10, starting transfers between devices, core_swap(): return lax.ppermute(value, 'c', [(0, 1), (1, 0)])  10.6 us
    ppermute x10, waiting for transfers between devices, core_swap(): return lax.ppermute(value, 'c', [(0, 1), (1, 0)])  9.84 us
    ppermute x2, waiting for transfers between devices, on_device(): placed.append(lax.ppermute(blocks[r], ('x', 'c'), moves))  7.7 us
    ppermute x2, starting transfers between devices, finish(): lax.ppermute(last, ('y', 'x', 'c'), moves)  5.67 us
    ppermute x3, starting transfers between devices, on_device(): lax.ppermute(chip, 'y', [(i, (i + k) % N) for i in range(N)])  4.67 us
  transfers between devices with their start and end apart: 30, of which 20 were waited for; matrix products, arithmetic and copies ran while one was open for 3% of the time, Pallas kernels for 10%

profile of v5, /device:TPU:1, one launch (start us, length us, event | category | flops | bytes accessed | tf_op | source)
XLA Modules:
  0.0 165.9 jit_solution(9184443994082743789)
XLA Ops:
  0.0 3.3 %collective-permute-start = (bf16[512,1024]{1,0:T(8,128)(2,1)}, bf16[512,1024]{1,0:T(8,128)(2,1)}, u32[]{:S(2)}, u32[]{:S(2)}) collective-permute-start(bf16[512,1024]{1,0:T(8,128)(2,1)} %refs_0_.3), channel_id=1, source_target_pairs={{0,8},{1,25},{8,16},{9,1},{16,24},{17,9},{24,0},{25,17},{2,10},{3,... | collective-permute-start | bytes 3145736 | tf_op jit(solution)/shard_map/ppermute | solution.py:28
  3.3 2.3 %slice.40 = bf16[2,1024,256]{2,1,0:T(8,128)(2,1)} slice(bf16[3,1024,256]{2,1,0:T(8,128)(2,1)} %bitcast.34), slice={[1:3], [0:1024], [0:256]} | slice | bytes 2097152 | tf_op jit(solution)/shard_map/slice | solution.py:330
  5.6 2.7 %collective-permute-start.3 = (bf16[2,1024,256]{2,1,0:T(8,128)(2,1)}, bf16[2,1024,256]{2,1,0:T(8,128)(2,1)}, u32[]{:S(2)}, u32[]{:S(2)}) collective-permute-start(bf16[2,1024,256]{2,1,0:T(8,128)(2,1)} %slice.40), channel_id=1, source_target_pairs={{0,32},{1,97},{32,64},{33,1},{64,96},{65,33},{96,0},{97,65},{2,34}... | collective-permute-start | bytes 3145736 | tf_op jit(solution)/shard_map/ppermute | solution.py:28
  8.3 12.7 %collective-permute-done.refs_1_ = bf16[512,1024]{1,0:T(8,128)(2,1)} collective-permute-done((bf16[512,1024]{1,0:T(8,128)(2,1)}, bf16[512,1024]{1,0:T(8,128)(2,1)}, u32[]{:S(2)}, u32[]{:S(2)}) %collective-permute-start) | collective-permute-done | bytes 1048608 | tf_op jit(solution)/shard_map/ppermute | solution.py:28
  21.0 3.4 %collective-permute-start.2 = (bf16[512,1024]{1,0:T(8,128)(2,1)}, bf16[512,1024]{1,0:T(8,128)(2,1)}, u32[]{:S(2)}, u32[]{:S(2)}) collective-permute-start(bf16[512,1024]{1,0:T(8,128)(2,1)} %collective-permute-done.refs_1_), channel_id=1, source_target_pairs={{0,8},{1,25},{8,16},{9,1},{16,24},{17,9},{24,0},{25,17},{2,10},{3,... | collective-permute-start | bytes 3145736 | tf_op jit(solution)/shard_map/ppermute | solution.py:28
  24.4 4.9 %collective-permute-done.3.refs_5_ = bf16[2,1024,256]{2,1,0:T(8,128)(2,1)} collective-permute-done((bf16[2,1024,256]{2,1,0:T(8,128)(2,1)}, bf16[2,1024,256]{2,1,0:T(8,128)(2,1)}, u32[]{:S(2)}, u32[]{:S(2)}) %collective-permute-start.3) | collective-permute-done | bytes 1048608 | tf_op jit(solution)/shard_map/ppermute | solution.py:28
  29.3 3.4 %collective-permute-start.8 = (bf16[2,1024,256]{2,1,0:T(8,128)(2,1)}, bf16[2,1024,256]{2,1,0:T(8,128)(2,1)}, u32[]{:S(2)}, u32[]{:S(2)}) collective-permute-start(bf16[2,1024,256]{2,1,0:T(8,128)(2,1)} %collective-permute-done.3.refs_5_), channel_id=1, source_target_pairs={{0,32},{1,97},{32,64},{33,1},{64,96},{65,33},{96,0},{97,65},{2,34}... | collective-permute-start | bytes 3145736 | tf_op jit(solution)/shard_map/ppermute | solution.py:28
  32.7 0.8 copy.8
  33.6 0.8 fusion.2
  34.4 0.1 collective-permute-start.9
  34.7 0.1 stack.35.where_ref
  34.8 1.0 collective-permute-done.9
  35.9 2.0 %collective-permute-done.2.refs_3_ = bf16[512,1024]{1,0:T(8,128)(2,1)} collective-permute-done((bf16[512,1024]{1,0:T(8,128)(2,1)}, bf16[512,1024]{1,0:T(8,128)(2,1)}, u32[]{:S(2)}, u32[]{:S(2)}) %collective-permute-start.2) | collective-permute-done | bytes 1048608 | tf_op jit(solution)/shard_map/ppermute | solution.py:28
  37.8 7.0 %collective-permute-done.8.refs_7_ = bf16[2,1024,256]{2,1,0:T(8,128)(2,1)} collective-permute-done((bf16[2,1024,256]{2,1,0:T(8,128)(2,1)}, bf16[2,1024,256]{2,1,0:T(8,128)(2,1)}, u32[]{:S(2)}, u32[]{:S(2)}) %collective-permute-start.8) | collective-permute-done | bytes 1048608 | tf_op jit(solution)/shard_map/ppermute | solution.py:28
  44.8 13.3 %project.2 = (bf16[2048,256]{1,0:T(8,128)(2,1)S(1)}, bf16[2048,256]{1,0:T(8,128)(2,1)S(1)}, bf16[4096,256]{1,0:T(8,128)(2,1)S(1)}, bf16[8192,256]{1,0:T(8,128)(2,1)S(1)}) custom-call(s32[8]{0:T(128)S(1)} %stack.35.where_ref, bf16[512,1024]{1,0:T(8,128)(2,1)S(1)} %copy-done.1, bf16[512,1024]{1,0:T(8,128)(2,1)} %collective-permute-done.refs_1_, ...), custom_call_target="tpu_custom_call" | custom-call | flops 1000 | bytes 1000 | tf_op jit(solution)/shard_map/project/pallas_call | solution.py:41
  58.1 2.7 %collective-permute-start.10 = (bf16[2048,256]{1,0:T(8,128)(2,1)S(1)}, bf16[2048,256]{1,0:T(8,128)(2,1)S(1)}, u32[]{:S(2)}, u32[]{:S(2)}) collective-permute-start(bf16[2048,256]{1,0:T(8,128)(2,1)S(1)} %get-tuple-element.37), channel_id=1, source_target_pairs={{0,1},{1,0},{2,3},{3,2},{4,5},{5,4},{6,7},{7,6},{8,9},{9,8},{10,11... | collective-permute-start | bytes 3145736 | tf_op jit(solution)/shard_map/ppermute | solution.py:32
  60.8 2.3 %collective-permute-done.10 = bf16[2048,256]{1,0:T(8,128)(2,1)S(1)} collective-permute-done((bf16[2048,256]{1,0:T(8,128)(2,1)S(1)}, bf16[2048,256]{1,0:T(8,128)(2,1)S(1)}, u32[]{:S(2)}, u32[]{:S(2)}) %collective-permute-start.10) | collective-permute-done | bytes 1048608 | tf_op jit(solution)/shard_map/ppermute | solution.py:32
  63.1 0.3 add_convert_fusion
  63.4 0.5 collective-permute-start.11
  63.9 3.8 %collective-permute-start.12 = (bf16[2048,256]{1,0:T(8,128)(2,1)S(1)}, bf16[2048,256]{1,0:T(8,128)(2,1)S(1)}, u32[]{:S(2)}, u32[]{:S(2)}) collective-permute-start(bf16[2048,256]{1,0:T(8,128)(2,1)S(1)} %add_convert_fusion), channel_id=1, source_target_pairs={{0,2},{1,7},{2,4},{3,1},{4,6},{5,3},{6,0},{7,5},{8,10},{9,15},{10,... | collective-permute-start | bytes 3145736 | tf_op jit(solution)/shard_map/ppermute | solution.py:28
  67.7 1.8 %collective-permute-start.5 = (bf16[1,1024,256]{2,1,0:T(8,128)(2,1)S(1)}, bf16[1,1024,256]{2,1,0:T(8,128)(2,1)S(1)}, u32[]{:S(2)}, u32[]{:S(2)}) collective-permute-start(bf16[1,1024,256]{2,1,0:T(8,128)(2,1)S(1)} %slice.31), channel_id=1, source_target_pairs={{0,32},{1,97},{32,64},{33,1},{64,96},{65,33},{96,0},{97,65},{2,34}... | collective-permute-start | bytes 1572872 | tf_op jit(solution)/shard_map/ppermute | solution.py:28
  69.5 11.7 %collective-permute-done.5.refs_0_.refs_5_ = bf16[1,1024,256]{2,1,0:T(8,128)(2,1)S(1)} collective-permute-done((bf16[1,1024,256]{2,1,0:T(8,128)(2,1)S(1)}, bf16[1,1024,256]{2,1,0:T(8,128)(2,1)S(1)}, u32[]{:S(2)}, u32[]{:S(2)}) %collective-permute-start.5) | collective-permute-done | bytes 524320 | tf_op jit(solution)/shard_map/ppermute | solution.py:28
  81.2 0.1 collective-permute-done.6.refs_1_.refs_6_
  81.3 1.2 near.2.refs_8_
  82.5 1.9 %collective-permute-start.16 = (bf16[4096,256]{1,0:T(8,128)(2,1)S(1)}, bf16[4096,256]{1,0:T(8,128)(2,1)S(1)}, u32[]{:S(2)}, u32[]{:S(2)}) collective-permute-start(bf16[4096,256]{1,0:T(8,128)(2,1)S(1)} %near.2.refs_8_), channel_id=1, source_target_pairs={{0,2},{1,7},{2,4},{3,1},{4,6},{5,3},{6,0},{7,5},{8,10},{9,15},{10,... | collective-permute-start | bytes 6291464 | tf_op jit(solution)/shard_map/ppermute | solution.py:28
  84.4 1.5 collective-permute-start.7
  85.9 6.9 %collective-permute-done.7.refs_7_ = bf16[1,1024,256]{2,1,0:T(8,128)(2,1)S(1)} collective-permute-done((bf16[1,1024,256]{2,1,0:T(8,128)(2,1)S(1)}, bf16[1,1024,256]{2,1,0:T(8,128)(2,1)S(1)}, u32[]{:S(2)}, u32[]{:S(2)}) %collective-permute-start.7) | collective-permute-done | bytes 524320 | tf_op jit(solution)/shard_map/ppermute | solution.py:28
  92.7 7.0 %project.3 = (bf16[1024,256]{1,0:T(8,128)(2,1)S(1)}, bf16[1024,256]{1,0:T(8,128)(2,1)S(1)}, bf16[2048,256]{1,0:T(8,128)(2,1)S(1)}, bf16[4096,256]{1,0:T(8,128)(2,1)S(1)}) custom-call(s32[8]{0:T(128)S(1)} %stack.35.where_ref, bf16[512,1024]{1,0:T(8,128)(2,1)S(1)} %copy-done.1, bf16[512,1024]{1,0:T(8,128)(2,1)} %collective-permute-done.refs_1_, ...), custom_call_target="tpu_custom_call" | custom-call | flops 1000 | bytes 1000 | tf_op jit(solution)/shard_map/project/pallas_call | solution.py:41
  99.8 2.1 %collective-permute-start.13 = (bf16[1024,256]{1,0:T(8,128)(2,1)S(1)}, bf16[1024,256]{1,0:T(8,128)(2,1)S(1)}, u32[]{:S(2)}, u32[]{:S(2)}) collective-permute-start(bf16[1024,256]{1,0:T(8,128)(2,1)S(1)} %get-tuple-element.41), channel_id=1, source_target_pairs={{0,1},{1,0},{2,3},{3,2},{4,5},{5,4},{6,7},{7,6},{8,9},{9,8},{10,11... | collective-permute-start | bytes 1572872 | tf_op jit(solution)/shard_map/ppermute | solution.py:32
  101.9 5.8 %collective-permute-done.16.refs_2_ = bf16[4096,256]{1,0:T(8,128)(2,1)S(1)} collective-permute-done((bf16[4096,256]{1,0:T(8,128)(2,1)S(1)}, bf16[4096,256]{1,0:T(8,128)(2,1)S(1)}, u32[]{:S(2)}, u32[]{:S(2)}) %collective-permute-start.16) | collective-permute-done | bytes 2097184 | tf_op jit(solution)/shard_map/ppermute | solution.py:28
  107.8 2.3 %collective-permute-start.17 = (bf16[4096,256]{1,0:T(8,128)(2,1)S(1)}, bf16[4096,256]{1,0:T(8,128)(2,1)S(1)}, u32[]{:S(2)}, u32[]{:S(2)}) collective-permute-start(bf16[4096,256]{1,0:T(8,128)(2,1)S(1)} %collective-permute-done.16.refs_2_), channel_id=1, source_target_pairs={{0,1},{1,0},{2,3},{3,2},{4,5},{5,4},{6,7},{7,6},{8,9},{9,8},{10,11... | collective-permute-start | bytes 6291464 | tf_op jit(solution)/shard_map/ppermute | solution.py:32
  110.0 0.1 add_convert_fusion.1
  110.2 0.1 collective-permute-start.14
  110.3 1.0 collective-permute-start.15
  111.2 2.6 %collective-permute-done.17.refs_3_ = bf16[4096,256]{1,0:T(8,128)(2,1)S(1)} collective-permute-done((bf16[4096,256]{1,0:T(8,128)(2,1)S(1)}, bf16[4096,256]{1,0:T(8,128)(2,1)S(1)}, u32[]{:S(2)}, u32[]{:S(2)}) %collective-permute-start.17) | collective-permute-done | bytes 2097184 | tf_op jit(solution)/shard_map/ppermute | solution.py:32
  113.8 1.7 %final.2 = (bf16[1024,256]{1,0:T(8,128)(2,1)S(1)}, bf16[1024,256]{1,0:T(8,128)(2,1)S(1)}, f32[16,256]{1,0:T(8,128)S(1)}, f32[16,256]{1,0:T(8,128)S(1)}, f32[16,256]{1,0:T(8,128)S(1)}) custom-call(s32[8]{0:T(128)S(1)} %stack.35.where_ref, bf16[8192,256]{1,0:T(8,128)(2,1)S(1)} %get-tuple-element.38.refs_0_, ...), custom_call_target="tpu_custom_call" | custom-call | flops 1000 | bytes 1000 | tf_op jit(solution)/shard_map/final/pallas_call | solution.py:41
  115.5 3.1 %collective-permute-start.18 = (f32[16,256]{1,0:T(8,128)S(1)}, f32[16,256]{1,0:T(8,128)S(1)}, u32[]{:S(2)}, u32[]{:S(2)}) collective-permute-start(f32[16,256]{1,0:T(8,128)S(1)} %get-tuple-element.44), channel_id=1, source_target_pairs={{1,32},{9,41},{16,49},{24,56},{33,64},{41,73},{48,81},{56,88},{65,... | collective-permute-start | bytes 49160 | tf_op jit(solution)/shard_map/ppermute | solution.py:385
  118.7 0.8 collective-permute-done.18.refs_0_.below_ref
  119.5 1.8 %near.3 = bf16[2048,256]{1,0:T(8,128)(2,1)} custom-call(s32[8]{0:T(128)S(1)} %stack.35.where_ref, bf16[2048,256]{1,0:T(8,128)(2,1)S(1)} %get-tuple-element.43.keep_ref, bf16[4096,256]{1,0:T(8,128)(2,1)S(1)} %collective-permute-done.14.got_ref.refs_1_, bf16[1024,256]{1,0:T(8,128)(2,1)S(1)} %collective-permute-done.15.arrived_ref, ...), custom_call_target="tpu_custom_call" | custom-call | flops 1000 | bytes 1000 | tf_op jit(solution)/shard_map/near/pallas_call | solution.py:41
  121.3 1.0 collective-permute-start.19
  122.3 0.7 collective-permute-start.20
  123.0 0.8 collective-permute-done.20.beside_ref
  123.8 4.4 %states.1 = (f32[2,1024,128]{2,1,0:T(8,128)S(1)}, f32[16,8,256]{2,1,0:T(8,128)S(1)}, f32[2,16,256]{2,1,0:T(8,128)S(1)}) custom-call(s32[8]{0:T(128)S(1)} %stack.35.where_ref, bf16[1024,256]{1,0:T(8,128)(2,1)S(1)} %get-tuple-element.45.first_ref, bf16[1024,256]{1,0:T(8,128)(2,1)S(1)} %get-tuple-element.46.second_ref, ...), custom_call_target="tpu_custom_call" | custom-call | flops 1000 | bytes 1000 | tf_op jit(solution)/shard_map/states/pallas_call | solution.py:41
  128.2 1.0 copy-done.4
  129.2 0.3 collective-permute-start.21
  129.6 0.9 collective-permute-done.21.others_ref
  130.5 1.0 collective-permute-start.22
  131.5 3.6 %collective-permute-start.23 = (f32[16,256]{1,0:T(8,128)S(1)}, f32[16,256]{1,0:T(8,128)S(1)}, u32[]{:S(2)}, u32[]{:S(2)}) collective-permute-start(f32[16,256]{1,0:T(8,128)S(1)} %fusion.4), channel_id=1, source_target_pairs={{0,64},{32,96},{64,0},{96,32},{1,65},{33,97},{65,1},{97,33},{2,66}... | collective-permute-start | bytes 49160 | tf_op jit(solution)/shard_map/ppermute | solution.py:409
  135.1 0.2 collective-permute-done.22.one_ref
  135.4 1.1 collective-permute-done.23.two_ref
  136.4 1.6 collective-permute-done.24.three_ref
  138.0 1.8 %collective-permute-start.25 = (bf16[2048,256]{1,0:T(8,128)(2,1)S(1)}, bf16[2048,256]{1,0:T(8,128)(2,1)S(1)}, u32[]{:S(2)}, u32[]{:S(2)}) collective-permute-start(bf16[2048,256]{1,0:T(8,128)(2,1)S(1)} %collective-permute-done.19.refs_2_), channel_id=1, source_target_pairs={{0,1},{1,0},{2,3},{3,2},{4,5},{5,4},{6,7},{7,6},{8,9},{9,8},{10,11... | collective-permute-start | bytes 3145736 | tf_op jit(solution)/shard_map/ppermute | solution.py:32
  139.8 2.3 %collective-permute-done.25.refs_3_ = bf16[2048,256]{1,0:T(8,128)(2,1)S(1)} collective-permute-done((bf16[2048,256]{1,0:T(8,128)(2,1)S(1)}, bf16[2048,256]{1,0:T(8,128)(2,1)S(1)}, u32[]{:S(2)}, u32[]{:S(2)}) %collective-permute-start.25) | collective-permute-done | bytes 1048608 | tf_op jit(solution)/shard_map/ppermute | solution.py:32
  142.1 1.6 copy-done.3
  143.7 1.2 final.3
  144.8 2.6 %collective-permute-start.26 = (f32[8,256]{1,0:T(8,128)S(1)}, f32[8,256]{1,0:T(8,128)S(1)}, u32[]{:S(2)}, u32[]{:S(2)}) collective-permute-start(f32[8,256]{1,0:T(8,128)S(1)} %get-tuple-element.52), channel_id=1, source_target_pairs={{1,32},{9,41},{16,49},{24,56},{33,64},{41,73},{48,81},{56,88},{65,... | collective-permute-start | bytes 24584 | tf_op jit(solution)/shard_map/ppermute | solution.py:385
  147.4 0.1 collective-permute-start.27
  147.5 4.2 %convolve.1.conv_ref = f32[2,1024,128]{2,1,0:T(8,128)S(1)} custom-call(s32[8]{0:T(128)S(1)} %stack.35.where_ref, f32[2,1024,128]{2,1,0:T(8,128)S(1)} %copy-done.5, f32[16,8,256]{2,1,0:T(8,128)S(1)} %get-tuple-element.56.init_ref, f32[16,256]{1,0:T(8,128)S(1)} %get-tuple-element.62.refs_9_.rate_ref, f32[16,256]{1,0:T(8,128)S(1)} %get-tuple-element.61.refs_10_.weight_ref, ...), custom_call_target="tpu_custom_call" | custom-call | flops 1000 | bytes 1000 | tf_op jit(solution)/shard_map/convolve/pallas_call | solution.py:41
  151.7 1.6 gate.1
  153.3 4.0 %collective-permute-start.28 = (bf16[512,256]{1,0:T(8,128)(2,1)S(1)}, bf16[512,256]{1,0:T(8,128)(2,1)S(1)}, u32[]{:S(2)}, u32[]{:S(2)}) collective-permute-start(bf16[512,256]{1,0:T(8,128)(2,1)S(1)} %get-tuple-element.57), channel_id=1, source_target_pairs={{0,0},{1,16},{8,8},{9,24},{16,17},{17,1},{24,25},{25,9},{2,2},{3,1... | collective-permute-start | bytes 786440 | tf_op jit(solution)/shard_map/ppermute | solution.py:435
  157.3 0.1 collective-permute-start.29
  157.4 5.6 %collective-permute-done.28 = bf16[512,256]{1,0:T(8,128)(2,1)S(1)} collective-permute-done((bf16[512,256]{1,0:T(8,128)(2,1)S(1)}, bf16[512,256]{1,0:T(8,128)(2,1)S(1)}, u32[]{:S(2)}, u32[]{:S(2)}) %collective-permute-start.28) | collective-permute-done | bytes 262176 | tf_op jit(solution)/shard_map/ppermute | solution.py:435
  163.0 2.1 %collective-permute-done.29 = bf16[512,256]{1,0:T(8,128)(2,1)S(1)} collective-permute-done((bf16[512,256]{1,0:T(8,128)(2,1)S(1)}, bf16[512,256]{1,0:T(8,128)(2,1)S(1)}, u32[]{:S(2)}, u32[]{:S(2)}) %collective-permute-start.29) | collective-permute-done | bytes 262176 | tf_op jit(solution)/shard_map/ppermute | solution.py:435
  165.1 0.8 pad_maximum_fusion
  (33 shorter events, 0.3 us)
Async XLA Ops:
  0.0 8.3 %copy-start.1 = (bf16[512,1024]{1,0:T(8,128)(2,1)S(1)}, bf16[512,1024]{1,0:T(8,128)(2,1)}, u32[]{:S(2)}) copy-start(bf16[512,1024]{1,0:T(8,128)(2,1)} %refs_0_.3) | copy-start | bytes 3145732
  0.0 44.8 %copy-start = (bf16[1024,3,256]{2,0,1:T(8,128)(2,1)S(1)}, bf16[1024,3,256]{2,0,1:T(8,128)(2,1)}, u32[]{:S(2)}) copy-start(bf16[1024,3,256]{2,0,1:T(8,128)(2,1)} %param.7) | copy-start | bytes 4718596
  0.0 21.0 %collective-permute-start = (bf16[512,1024]{1,0:T(8,128)(2,1)}, bf16[512,1024]{1,0:T(8,128)(2,1)}, u32[]{:S(2)}, u32[]{:S(2)}) collective-permute-start(bf16[512,1024]{1,0:T(8,128)(2,1)} %refs_0_.3), channel_id=1, source_target_pairs={{0,8},{1,25},{8,16},{9,1},{16,24},{17,9},{24,0},{25,17},{2,10},{3,... | collective-permute-start | bytes 3145736 | tf_op jit(solution)/shard_map/ppermute | solution.py:28
  5.6 23.7 %collective-permute-start.3 = (bf16[2,1024,256]{2,1,0:T(8,128)(2,1)}, bf16[2,1024,256]{2,1,0:T(8,128)(2,1)}, u32[]{:S(2)}, u32[]{:S(2)}) collective-permute-start(bf16[2,1024,256]{2,1,0:T(8,128)(2,1)} %slice.40), channel_id=1, source_target_pairs={{0,32},{1,97},{32,64},{33,1},{64,96},{65,33},{96,0},{97,65},{2,34}... | collective-permute-start | bytes 3145736 | tf_op jit(solution)/shard_map/ppermute | solution.py:28
  8.3 27.5 %collective-permute-start.1 = (bf16[512,1024]{1,0:T(8,128)(2,1)S(1)}, bf16[512,1024]{1,0:T(8,128)(2,1)}, u32[]{:S(2)}, u32[]{:S(2)}) collective-permute-start(bf16[512,1024]{1,0:T(8,128)(2,1)S(1)} %copy-done.1), channel_id=1, source_target_pairs={{0,24},{1,9},{8,0},{9,17},{16,8},{17,25},{24,16},{25,1},{2,26},{3,... | collective-permute-start | bytes 3145736 | tf_op jit(solution)/shard_map/ppermute | solution.py:28
  8.3 27.5 %collective-permute-start.4 = (bf16[2,1024,256]{2,1,0:T(8,128)(2,1)}, bf16[2,1024,256]{2,1,0:T(8,128)(2,1)}, u32[]{:S(2)}, u32[]{:S(2)}) collective-permute-start(bf16[2,1024,256]{2,1,0:T(8,128)(2,1)} %slice.40), channel_id=1, source_target_pairs={{0,96},{1,33},{32,0},{33,65},{64,32},{65,97},{96,64},{97,1},{2,98}... | collective-permute-start | bytes 3145736 | tf_op jit(solution)/shard_map/ppermute | solution.py:28
  21.0 16.8 %collective-permute-start.2 = (bf16[512,1024]{1,0:T(8,128)(2,1)}, bf16[512,1024]{1,0:T(8,128)(2,1)}, u32[]{:S(2)}, u32[]{:S(2)}) collective-permute-start(bf16[512,1024]{1,0:T(8,128)(2,1)} %collective-permute-done.refs_1_), channel_id=1, source_target_pairs={{0,8},{1,25},{8,16},{9,1},{16,24},{17,9},{24,0},{25,17},{2,10},{3,... | collective-permute-start | bytes 3145736 | tf_op jit(solution)/shard_map/ppermute | solution.py:28
  29.3 15.5 %collective-permute-start.8 = (bf16[2,1024,256]{2,1,0:T(8,128)(2,1)}, bf16[2,1024,256]{2,1,0:T(8,128)(2,1)}, u32[]{:S(2)}, u32[]{:S(2)}) collective-permute-start(bf16[2,1024,256]{2,1,0:T(8,128)(2,1)} %collective-permute-done.3.refs_5_), channel_id=1, source_target_pairs={{0,32},{1,97},{32,64},{33,1},{64,96},{65,33},{96,0},{97,65},{2,34}... | collective-permute-start | bytes 3145736 | tf_op jit(solution)/shard_map/ppermute | solution.py:28
  34.4 1.3 collective-permute-start.9
  58.1 5.0 %collective-permute-start.10 = (bf16[2048,256]{1,0:T(8,128)(2,1)S(1)}, bf16[2048,256]{1,0:T(8,128)(2,1)S(1)}, u32[]{:S(2)}, u32[]{:S(2)}) collective-permute-start(bf16[2048,256]{1,0:T(8,128)(2,1)S(1)} %get-tuple-element.37), channel_id=1, source_target_pairs={{0,1},{1,0},{2,3},{3,2},{4,5},{5,4},{6,7},{7,6},{8,9},{9,8},{10,11... | collective-permute-start | bytes 3145736 | tf_op jit(solution)/shard_map/ppermute | solution.py:32
  63.4 17.9 %collective-permute-start.11 = (bf16[8192,256]{1,0:T(8,128)(2,1)S(1)}, bf16[8192,256]{1,0:T(8,128)(2,1)S(1)}, u32[]{:S(2)}, u32[]{:S(2)}) collective-permute-start(bf16[8192,256]{1,0:T(8,128)(2,1)S(1)} %get-tuple-element.38.refs_0_), channel_id=1, source_target_pairs={{0,1},{1,0},{2,3},{3,2},{4,5},{5,4},{6,7},{7,6},{8,9},{9,8},{10,11... | collective-permute-start | bytes 12582920 | tf_op jit(solution)/shard_map/ppermute | solution.py:32
  63.9 17.5 %collective-permute-start.12 = (bf16[2048,256]{1,0:T(8,128)(2,1)S(1)}, bf16[2048,256]{1,0:T(8,128)(2,1)S(1)}, u32[]{:S(2)}, u32[]{:S(2)}) collective-permute-start(bf16[2048,256]{1,0:T(8,128)(2,1)S(1)} %add_convert_fusion), channel_id=1, source_target_pairs={{0,2},{1,7},{2,4},{3,1},{4,6},{5,3},{6,0},{7,5},{8,10},{9,15},{10,... | collective-permute-start | bytes 3145736 | tf_op jit(solution)/shard_map/ppermute | solution.py:28
  67.7 13.6 %collective-permute-start.5 = (bf16[1,1024,256]{2,1,0:T(8,128)(2,1)S(1)}, bf16[1,1024,256]{2,1,0:T(8,128)(2,1)S(1)}, u32[]{:S(2)}, u32[]{:S(2)}) collective-permute-start(bf16[1,1024,256]{2,1,0:T(8,128)(2,1)S(1)} %slice.31), channel_id=1, source_target_pairs={{0,32},{1,97},{32,64},{33,1},{64,96},{65,33},{96,0},{97,65},{2,34}... | collective-permute-start | bytes 1572872 | tf_op jit(solution)/shard_map/ppermute | solution.py:28
  69.5 11.9 %collective-permute-start.6 = (bf16[1,1024,256]{2,1,0:T(8,128)(2,1)S(1)}, bf16[1,1024,256]{2,1,0:T(8,128)(2,1)S(1)}, u32[]{:S(2)}, u32[]{:S(2)}) collective-permute-start(bf16[1,1024,256]{2,1,0:T(8,128)(2,1)S(1)} %slice.31), channel_id=1, source_target_pairs={{0,96},{1,33},{32,0},{33,65},{64,32},{65,97},{96,64},{97,1},{2,98}... | collective-permute-start | bytes 1572872 | tf_op jit(solution)/shard_map/ppermute | solution.py:28
  82.5 25.2 %collective-permute-start.16 = (bf16[4096,256]{1,0:T(8,128)(2,1)S(1)}, bf16[4096,256]{1,0:T(8,128)(2,1)S(1)}, u32[]{:S(2)}, u32[]{:S(2)}) collective-permute-start(bf16[4096,256]{1,0:T(8,128)(2,1)S(1)} %near.2.refs_8_), channel_id=1, source_target_pairs={{0,2},{1,7},{2,4},{3,1},{4,6},{5,3},{6,0},{7,5},{8,10},{9,15},{10,... | collective-permute-start | bytes 6291464 | tf_op jit(solution)/shard_map/ppermute | solution.py:28
  84.4 8.3 %collective-permute-start.7 = (bf16[1,1024,256]{2,1,0:T(8,128)(2,1)S(1)}, bf16[1,1024,256]{2,1,0:T(8,128)(2,1)S(1)}, u32[]{:S(2)}, u32[]{:S(2)}) collective-permute-start(bf16[1,1024,256]{2,1,0:T(8,128)(2,1)S(1)} %collective-permute-done.5.refs_0_.refs_5_), channel_id=1, source_target_pairs={{0,32},{1,97},{32,64},{33,1},{64,96},{65,33},{96,0},{97,65},{2,34}... | collective-permute-start | bytes 1572872 | tf_op jit(solution)/shard_map/ppermute | solution.py:28
  99.8 15.7 %copy-start.2 = (bf16[4096,256]{1,0:T(8,128)(2,1)}, bf16[4096,256]{1,0:T(8,128)(2,1)S(1)}, u32[]{:S(2)}) copy-start(bf16[4096,256]{1,0:T(8,128)(2,1)S(1)} %get-tuple-element.42.refs_0_) | copy-start | bytes 6291460
  99.8 10.2 %collective-permute-start.13 = (bf16[1024,256]{1,0:T(8,128)(2,1)S(1)}, bf16[1024,256]{1,0:T(8,128)(2,1)S(1)}, u32[]{:S(2)}, u32[]{:S(2)}) collective-permute-start(bf16[1024,256]{1,0:T(8,128)(2,1)S(1)} %get-tuple-element.41), channel_id=1, source_target_pairs={{0,1},{1,0},{2,3},{3,2},{4,5},{5,4},{6,7},{7,6},{8,9},{9,8},{10,11... | collective-permute-start | bytes 1572872 | tf_op jit(solution)/shard_map/ppermute | solution.py:32
  107.8 6.1 %collective-permute-start.17 = (bf16[4096,256]{1,0:T(8,128)(2,1)S(1)}, bf16[4096,256]{1,0:T(8,128)(2,1)S(1)}, u32[]{:S(2)}, u32[]{:S(2)}) collective-permute-start(bf16[4096,256]{1,0:T(8,128)(2,1)S(1)} %collective-permute-done.16.refs_2_), channel_id=1, source_target_pairs={{0,1},{1,0},{2,3},{3,2},{4,5},{5,4},{6,7},{7,6},{8,9},{9,8},{10,11... | collective-permute-start | bytes 6291464 | tf_op jit(solution)/shard_map/ppermute | solution.py:32
  110.2 8.5 %collective-permute-start.14 = (bf16[4096,256]{1,0:T(8,128)(2,1)S(1)}, bf16[4096,256]{1,0:T(8,128)(2,1)S(1)}, u32[]{:S(2)}, u32[]{:S(2)}) collective-permute-start(bf16[4096,256]{1,0:T(8,128)(2,1)S(1)} %get-tuple-element.42.refs_0_), channel_id=1, source_target_pairs={{0,1},{1,0},{2,3},{3,2},{4,5},{5,4},{6,7},{7,6},{8,9},{9,8},{10,11... | collective-permute-start | bytes 6291464 | tf_op jit(solution)/shard_map/ppermute | solution.py:32
  110.3 8.4 %collective-permute-start.15 = (bf16[1024,256]{1,0:T(8,128)(2,1)S(1)}, bf16[1024,256]{1,0:T(8,128)(2,1)S(1)}, u32[]{:S(2)}, u32[]{:S(2)}) collective-permute-start(bf16[1024,256]{1,0:T(8,128)(2,1)S(1)} %add_convert_fusion.1), channel_id=1, source_target_pairs={{0,2},{1,7},{2,4},{3,1},{4,6},{5,3},{6,0},{7,5},{8,10},{9,15},{10,... | collective-permute-start | bytes 1572872 | tf_op jit(solution)/shard_map/ppermute | solution.py:28
  115.5 4.0 %collective-permute-start.18 = (f32[16,256]{1,0:T(8,128)S(1)}, f32[16,256]{1,0:T(8,128)S(1)}, u32[]{:S(2)}, u32[]{:S(2)}) collective-permute-start(f32[16,256]{1,0:T(8,128)S(1)} %get-tuple-element.44), channel_id=1, source_target_pairs={{1,32},{9,41},{16,49},{24,56},{33,64},{41,73},{48,81},{56,88},{65,... | collective-permute-start | bytes 49160 | tf_op jit(solution)/shard_map/ppermute | solution.py:385
  121.3 16.7 %collective-permute-start.19 = (bf16[2048,256]{1,0:T(8,128)(2,1)}, bf16[2048,256]{1,0:T(8,128)(2,1)S(1)}, u32[]{:S(2)}, u32[]{:S(2)}) collective-permute-start(bf16[2048,256]{1,0:T(8,128)(2,1)} %near.3), channel_id=1, source_target_pairs={{0,2},{1,7},{2,4},{3,1},{4,6},{5,3},{6,0},{7,5},{8,10},{9,15},{10,... | collective-permute-start | bytes 3145736 | tf_op jit(solution)/shard_map/ppermute | solution.py:28
  122.3 1.5 collective-permute-start.20
  128.2 1.0 copy-start.4
  129.2 1.2 collective-permute-start.21
  130.5 4.9 %collective-permute-start.22 = (f32[16,256]{1,0:T(8,128)S(1)}, f32[16,256]{1,0:T(8,128)S(1)}, u32[]{:S(2)}, u32[]{:S(2)}) collective-permute-start(f32[16,256]{1,0:T(8,128)S(1)} %fusion.4), channel_id=1, source_target_pairs={{0,32},{32,64},{64,96},{96,0},{1,33},{33,65},{65,97},{97,1},{2,34}... | collective-permute-start | bytes 49160 | tf_op jit(solution)/shard_map/ppermute | solution.py:409
  131.5 4.9 %collective-permute-start.23 = (f32[16,256]{1,0:T(8,128)S(1)}, f32[16,256]{1,0:T(8,128)S(1)}, u32[]{:S(2)}, u32[]{:S(2)}) collective-permute-start(f32[16,256]{1,0:T(8,128)S(1)} %fusion.4), channel_id=1, source_target_pairs={{0,64},{32,96},{64,0},{96,32},{1,65},{33,97},{65,1},{97,33},{2,66}... | collective-permute-start | bytes 49160 | tf_op jit(solution)/shard_map/ppermute | solution.py:409
  135.1 2.9 %collective-permute-start.24 = (f32[16,256]{1,0:T(8,128)S(1)}, f32[16,256]{1,0:T(8,128)S(1)}, u32[]{:S(2)}, u32[]{:S(2)}) collective-permute-start(f32[16,256]{1,0:T(8,128)S(1)} %fusion.4), channel_id=1, source_target_pairs={{0,96},{32,0},{64,32},{96,64},{1,97},{33,1},{65,33},{97,65},{2,98}... | collective-permute-start | bytes 49160 | tf_op jit(solution)/shard_map/ppermute | solution.py:409
  138.0 4.0 %collective-permute-start.25 = (bf16[2048,256]{1,0:T(8,128)(2,1)S(1)}, bf16[2048,256]{1,0:T(8,128)(2,1)S(1)}, u32[]{:S(2)}, u32[]{:S(2)}) collective-permute-start(bf16[2048,256]{1,0:T(8,128)(2,1)S(1)} %collective-permute-done.19.refs_2_), channel_id=1, source_target_pairs={{0,1},{1,0},{2,3},{3,2},{4,5},{5,4},{6,7},{7,6},{8,9},{9,8},{10,11... | collective-permute-start | bytes 3145736 | tf_op jit(solution)/shard_map/ppermute | solution.py:32
  142.1 1.6 copy-start.3
  143.7 3.8 %copy-start.5 = (f32[2,1024,128]{2,1,0:T(8,128)S(1)}, f32[2,1024,128]{2,1,0:T(8,128)}, u32[]{:S(2)}) copy-start(f32[2,1024,128]{2,1,0:T(8,128)} %copy-done.4) | copy-start | bytes 3145732
  144.8 6.8 %collective-permute-start.26 = (f32[8,256]{1,0:T(8,128)S(1)}, f32[8,256]{1,0:T(8,128)S(1)}, u32[]{:S(2)}, u32[]{:S(2)}) collective-permute-start(f32[8,256]{1,0:T(8,128)S(1)} %get-tuple-element.52), channel_id=1, source_target_pairs={{1,32},{9,41},{16,49},{24,56},{33,64},{41,73},{48,81},{56,88},{65,... | collective-permute-start | bytes 24584 | tf_op jit(solution)/shard_map/ppermute | solution.py:385
  147.4 4.3 %collective-permute-start.27 = (f32[8,256]{1,0:T(8,128)S(1)}, f32[8,256]{1,0:T(8,128)S(1)}, u32[]{:S(2)}, u32[]{:S(2)}) collective-permute-start(f32[8,256]{1,0:T(8,128)S(1)} %get-tuple-element.53), channel_id=1, source_target_pairs={{0,1},{1,0},{2,3},{3,2},{4,5},{5,4},{6,7},{7,6},{8,9},{9,8},{10,11... | collective-permute-start | bytes 24584 | tf_op jit(solution)/shard_map/ppermute | solution.py:32
  153.3 9.7 %collective-permute-start.28 = (bf16[512,256]{1,0:T(8,128)(2,1)S(1)}, bf16[512,256]{1,0:T(8,128)(2,1)S(1)}, u32[]{:S(2)}, u32[]{:S(2)}) collective-permute-start(bf16[512,256]{1,0:T(8,128)(2,1)S(1)} %get-tuple-element.57), channel_id=1, source_target_pairs={{0,0},{1,16},{8,8},{9,24},{16,17},{17,1},{24,25},{25,9},{2,2},{3,1... | collective-permute-start | bytes 786440 | tf_op jit(solution)/shard_map/ppermute | solution.py:435
  157.3 7.8 %collective-permute-start.29 = (bf16[512,256]{1,0:T(8,128)(2,1)S(1)}, bf16[512,256]{1,0:T(8,128)(2,1)S(1)}, u32[]{:S(2)}, u32[]{:S(2)}) collective-permute-start(bf16[512,256]{1,0:T(8,128)(2,1)S(1)} %get-tuple-element.58), channel_id=1, source_target_pairs={{0,8},{1,24},{8,16},{9,0},{16,25},{17,9},{24,1},{25,17},{2,10},{3,... | collective-permute-start | bytes 786440 | tf_op jit(solution)/shard_map/ppermute | solution.py:435
